TPU v7x, 512 devices: a whole 4x4x16 slice. The times are simulated.
512 devices in a mesh: section: 16 (over z_lo, x), dp: 32 (over z_hi, y, core).
Axes of the slice: x: 4, y: 4, z: 16 (z_hi: 4, z_lo: 4; z = z_hi * 4 + z_lo), core: 2. Of those that a mesh axis runs over, the one named last changes fastest.
Arguments:
- enc_out: bfloat16 [1024, 6144], P('dp'), may hold values from -6 to 6
- kv_weight: bfloat16 [16, 6144, 256], P('section', 'dp'), may hold values from -0.078125 to 0.078125
- queries: bfloat16 [16, 16384, 128], P('section', 'dp'), may hold values from -128 to 128
- out_grad: bfloat16 [16, 16384, 128], P('section', 'dp'), may hold values from -6 to 6
Outputs:
- enc_grad: bfloat16 [16, 1024, 6144], P('section', 'dp')
- weight_grad: float32 [16, 6144, 256], P('section', 'dp')
All inputs are finite; a program needn't handle non-finite values.
Results may differ from a plain program's by a relative error of at most 0.025.
The roundings to bfloat16 on the way count: a program that leaves them out, or rounds other values in their place, can miss the bound.
Values may be sent and summed in bfloat16 or wider, within the bound.
No kernel may reach another device: no remote copies, remote signals or barrier semaphores. Data moves between devices by JAX's collectives and lax.ppermute only.
A program may use at most 64 MiB of HBM per device.

v0:
```python
import jax
import jax.numpy as jnp
from jax import lax
from jax.sharding import PartitionSpec as P


def carried_in(part, axis, combine, identity):
    count = lax.axis_size(axis)
    place = lax.axis_index(axis)
    ahead = count - 1 - place
    gathered = lax.all_gather(part, axis)
    state = jnp.zeros_like(part) + jnp.asarray(identity, part.dtype)

    def one(step, state):
        source = count - 1 - step
        return combine(state, lax.dynamic_index_in_dim(gathered, source, 0, False))

    return lax.fori_loop(0, ahead, one, state)


def contract(left, right, left_dim, right_dim):
    return lax.dot_general(
        left, right, (((left_dim,), (right_dim,)), ((), ())), preferred_element_type=jnp.float32
    )


def add_terms(earlier, later):
    return earlier + later


def shards(enc_out, kv_weight, queries, out_grad):
    head_size = queries.shape[2]
    logit_scale = 1.0 / head_size**0.5
    weights = lax.all_gather(kv_weight[0], "dp", axis=0, tiled=True)
    kv_low = jnp.dot(enc_out, weights, preferred_element_type=jnp.float32).astype(jnp.bfloat16)
    encoder_keys = kv_low[:, :head_size]
    encoder_values = kv_low[:, head_size:]
    decoder_query = queries[0]
    upstream_gradient = out_grad[0]
    attention_scores = contract(decoder_query, encoder_keys, 1, 1) * logit_scale
    peak = jnp.max(attention_scores, axis=-1, keepdims=True)
    expd = jnp.exp(attention_scores - peak)
    probs = expd / jnp.sum(expd, axis=-1, keepdims=True)
    probabilities_reduced = probs.astype(jnp.bfloat16)
    probability_gradient = contract(upstream_gradient, encoder_values, 1, 1)
    delta = jnp.sum(probs * probability_gradient, axis=-1, keepdims=True)
    score_gradient = (probs * (probability_gradient - delta) * logit_scale).astype(jnp.bfloat16)
    key_gradient = contract(score_gradient, decoder_query, 0, 0)
    value_gradient = contract(probabilities_reduced, upstream_gradient, 0, 0)
    dkv = jnp.concatenate([key_gradient, value_gradient], axis=-1).astype(jnp.bfloat16)
    partial_value = contract(dkv, weights, 1, 1)
    higher = carried_in(partial_value, "section", add_terms, jnp.zeros_like(partial_value))
    total = higher + partial_value
    enc_grad = total.astype(jnp.bfloat16)[None]
    grad = lax.psum_scatter(
        contract(enc_out, dkv, 0, 0).astype(jnp.bfloat16), "dp", scatter_dimension=0, tiled=True
    ).astype(jnp.float32)
    return (enc_grad, grad[None])


def solution(mesh):
    in_specs = (
        P("dp", None),
        P("section", "dp", None),
        P("section", "dp", None),
        P("section", "dp", None),
    )
    out_specs = (P("section", "dp", None), P("section", "dp", None))
    return jax.shard_map(shards, mesh=mesh, in_specs=in_specs, out_specs=out_specs, check_vma=False)
```

profile of v0, /device:TPU:1, one launch (start us, length us, event | category | flops | bytes accessed | tf_op | source)
XLA Modules:
  0.0 411.2 jit_solution(9477925088197242283)
XLA Ops:
  7.2 0.0 copy-start
  7.2 0.0 copy-start.3
  7.2 0.0 copy-start.4
  7.2 0.0 all-gather.5.cloned.1.call-start
  7.2 0.7 all-gather.5.cloned.1.call-update
  7.9 0.0 reduce-scatter.4.cloned.1.call-start
  8.0 97.2 %all-gather.5.cloned.1.call-done = bf16[1,6144,256]{2,1,0:T(8,128)(2,1)} async-done(((bf16[1,192,256]{2,1,0:T(8,128)(2,1)}), bf16[1,6144,256]{2,1,0:T(8,128)(2,1)}) %all-gather.5.cloned.1.call-update) | async-done | bytes 3145744 | tf_op jit(solution)/shard_map/all_gather | solution.py:34
  105.2 0.0 copy-done
  105.2 2.5 fusion.5
  107.7 0.0 copy-done.3
  107.7 0.2 fusion.28
  107.9 0.0 copy-done.4
  107.9 0.1 convolution_convert_fusion.1
  108.1 0.2 fusion.13
  108.2 0.2 convolution_convert_fusion.2
  108.4 1.0 fusion
  109.4 2.9 copy.8
  112.3 0.0 copy-start.1
  112.3 0.0 reduce-scatter.4.cloned.1.call-update
  112.3 0.0 all-gather.7.cloned.1.call-start
  112.4 1.8 copy-done.1
  114.2 1.9 fusion.1
  116.1 0.0 all-gather.7.cloned.1.call-update
  116.1 120.4 %reduce-scatter.4.cloned.1.call-done = bf16[192,256]{1,0:T(8,128)(2,1)} async-done(((bf16[6144,256]{1,0:T(8,128)(2,1)}), bf16[192,256]{1,0:T(8,128)(2,1)}) %reduce-scatter.4.cloned.1.call-update) | async-done | bytes 98320
  236.5 1.0 copy.9
  237.5 0.8 copy.7
  238.3 145.6 %all-gather.7.cloned.1.call-done = f32[512,6144]{1,0:T(8,128)} async-done(((f32[32,6144]{1,0:T(8,128)}), f32[512,6144]{1,0:T(8,128)}) %all-gather.7.cloned.1.call-update) | async-done | bytes 12582928 | tf_op jit(solution)/shard_map/all_gather | solution.py:11
  383.9 0.1 broadcast_in_dim.15
  383.9 0.0 copy-start.2
  384.0 19.9 %while.12 = (s32[]{:T(128)}, f32[32,6144]{1,0:T(8,128)S(1)}, s32[]{:T(128)}, f32[16,32,6144]{2,1,0:T(8,128)}, s32[]{:T(128)}, /*index=5*/s32[]{:T(128)}, s32[]{:T(128)}, s32[]{:T(128)}) while((s32[]{:T(128)}, f32[32,6144]{1,0:T(8,128)S(1)}, s32[]{:T(128)}, f32[16,32,6144]{2,1,0:T(8,128)}, s32[]{:T(128)}, /*index=5*/s32[]{:T(128)}, s32[]{:T(128)}, ...), condition=%wide.region_4.5_spmd, body=%wide.region_3.4_spmd.sunk | while | flops 196614 | bytes 2359439 | solution.py:18
  384.0 1.4 bitcast_add_fusion.2
  385.4 1.3 bitcast_add_fusion.2
  386.7 1.3 bitcast_add_fusion.2
  388.0 1.3 bitcast_add_fusion.2
  389.3 1.3 bitcast_add_fusion.2
  390.7 1.3 bitcast_add_fusion.2
  392.0 1.3 bitcast_add_fusion.2
  393.3 1.3 bitcast_add_fusion.2
  394.6 1.3 bitcast_add_fusion.2
  395.9 1.3 bitcast_add_fusion.2
  397.3 1.3 bitcast_add_fusion.2
  398.6 1.3 bitcast_add_fusion.2
  399.9 1.3 bitcast_add_fusion.2
  401.2 1.3 bitcast_add_fusion.2
  402.6 1.3 bitcast_add_fusion.2
  403.9 0.0 copy-done.2
  403.9 0.8 fusion.8
  (2 shorter events, 0.1 us)
Async XLA Ops:
  7.2 98.0 %copy-start = (bf16[32,6144]{1,0:T(8,128)(2,1)S(1)}, bf16[32,6144]{1,0:T(8,128)(2,1)}, u32[]{:S(2)}) copy-start(bf16[32,6144]{1,0:T(8,128)(2,1)} %param.6) | copy-start | bytes 1179652
  7.2 100.5 %copy-start.3 = (bf16[1,512,128]{2,1,0:T(8,128)(2,1)S(1)}, bf16[1,512,128]{2,1,0:T(8,128)(2,1)}, u32[]{:S(2)}) copy-start(bf16[1,512,128]{2,1,0:T(8,128)(2,1)} %param.8) | copy-start | bytes 393220
  7.2 100.7 %copy-start.4 = (bf16[1,512,128]{2,1,0:T(8,128)(2,1)S(1)}, bf16[1,512,128]{2,1,0:T(8,128)(2,1)}, u32[]{:S(2)}) copy-start(bf16[1,512,128]{2,1,0:T(8,128)(2,1)} %param.9) | copy-start | bytes 393220
  7.2 98.0 %all-gather.5.cloned.1.call-start = ((), (), s32[]{:S(2)}) async-start(), calls=%async_computation.1 | async-start | bytes 3244032 | tf_op jit(solution)/shard_map/all_gather | solution.py:34
  7.9 228.6 %reduce-scatter.4.cloned.1.call-start = ((), (), s32[]{:S(2)}) async-start(), calls=%async_computation.3 | async-start | bytes 3244032
  112.3 1.9 copy-start.1
  112.3 271.6 %all-gather.7.cloned.1.call-start = ((), (), s32[]{:S(2)}) async-start(), calls=%async_computation.2 | async-start | bytes 13369344 | tf_op jit(solution)/shard_map/all_gather | solution.py:11
  383.9 19.9 %copy-start.2 = (f32[32,6144]{1,0:T(8,128)S(1)}, f32[32,6144]{1,0:T(8,128)}, u32[]{:S(2)}) copy-start(f32[32,6144]{1,0:T(8,128)} %fusion.1) | copy-start | bytes 2359300
Sparse Core Ops, SparseCore 0:
  11.2 93.9 all-gather.4
  112.4 124.0 reduce-scatter.3
  238.8 145.0 all-gather.6
where the time goes:
time: 412 us; the launch traced here: 411 us
  waiting for transfers between devices  364 us (88%)
  other arithmetic  20.4 us (5%)
  between operations  13.8 us (3%)
  local copies, waits for them, and re-layouts  6.54 us (2%)
  matrix products  6.1 us (1%)
    all_gather x1, waiting for transfers between devices, carried_in(): gathered = lax.all_gather(part, axis)  146 us
    unnamed x4, waiting for transfers between devices  121 us
    all_gather x1, waiting for transfers between devices, shards(): weights = lax.all_gather(kv_weight[0], 'dp', axis=0, tiled=True)  97.2 us
    add x15, other arithmetic, add_terms(): return earlier + later  19.6 us
  transfers between devices with their start and end apart: 3, of which 3 were waited for; matrix products, arithmetic and copies ran while one was open for 1% of the time, Pallas kernels for 0%

commit v1 on v0

v1 whole, which is shorter than its diff:
```python
import functools

import jax
import jax.numpy as jnp
from jax import lax
from jax.experimental import pallas as pl
from jax.experimental.pallas import tpu as pltpu
from jax.sharding import PartitionSpec as P

Z_HI = 4
NEAR = 8


def contract(left, right, left_dim, right_dim):
    return lax.dot_general(
        left, right, (((left_dim,), (right_dim,)), ((), ())), preferred_element_type=jnp.float32
    )


def split_columns(enc_ref, out_ref):
    width = out_ref.shape[2] // Z_HI
    for near in range(NEAR):
        for far in range(Z_HI):
            start = (far * NEAR + near) * width
            out_ref[near, :, far * width : (far + 1) * width] = enc_ref[:, start : start + width]


def join_columns(in_ref, out_ref):
    width = in_ref.shape[2] // Z_HI
    for near in range(NEAR):
        for far in range(Z_HI):
            start = (far * NEAR + near) * width
            out_ref[0, :, start : start + width] = in_ref[near, :, far * width : (far + 1) * width]


def project(place_ref, own_ref, one_ref, two_ref, three_ref, enc_ref, weights_ref, kv_ref):
    place = place_ref[0]
    depth = own_ref.shape[0]
    for step, ref in enumerate((own_ref, one_ref, two_ref, three_ref)):
        far = lax.rem(place + Z_HI - step, Z_HI)
        weights_ref[pl.ds(pl.multiple_of(far * depth, depth), depth), :] = ref[...]
    near, rows, width = enc_ref.shape
    enc = enc_ref[...].reshape(near * rows, width)
    kv = jnp.dot(enc, weights_ref[...], preferred_element_type=jnp.float32)
    kv_ref[...] = kv.reshape(near, rows, kv.shape[1])


def attend(kv_ref, queries_ref, grad_ref, dkv_ref):
    kv = kv_ref[0]
    for near in range(1, kv_ref.shape[0]):
        kv = kv + kv_ref[near]
    kv = kv.astype(jnp.bfloat16)
    head = queries_ref.shape[1]
    scale = 1.0 / head**0.5
    queries = queries_ref[...]
    grad = grad_ref[...]
    scores = contract(kv[:, :head], queries, 1, 1) * scale
    expd = jnp.exp(scores - jnp.max(scores, axis=0, keepdims=True))
    probs = expd / jnp.sum(expd, axis=0, keepdims=True)
    dprobs = contract(kv[:, head:], grad, 1, 1)
    delta = jnp.sum(probs * dprobs, axis=0, keepdims=True)
    dscores = (probs * (dprobs - delta) * scale).astype(jnp.bfloat16)
    dkv_ref[:, :head] = contract(dscores, queries, 1, 0).astype(jnp.bfloat16)
    dkv_ref[:, head:] = contract(probs.astype(jnp.bfloat16), grad, 1, 0).astype(jnp.bfloat16)


def spread(dkv_ref, weights_ref, out_ref):
    near, rows, width = dkv_ref.shape
    dkv = dkv_ref[...].reshape(near * rows, width)
    out = contract(dkv, weights_ref[...], 1, 1)
    out_ref[...] = out.astype(jnp.bfloat16).reshape(out_ref.shape)


def weight_terms(enc_ref, dkv_ref, out_ref):
    near, rows, width = dkv_ref.shape
    dkv = dkv_ref[...].reshape(near * rows, width)
    enc = enc_ref[...].reshape(near * rows, enc_ref.shape[2])
    out_ref[...] = contract(enc, dkv, 0, 0).astype(jnp.bfloat16).reshape(out_ref.shape)


def suffix_sums(in_ref, out_ref):
    sections = in_ref.shape[0]
    total = in_ref[sections - 1].astype(jnp.float32)
    out_ref[sections - 1] = in_ref[sections - 1]
    for section in range(sections - 2, -1, -1):
        total = total + in_ref[section].astype(jnp.float32)
        out_ref[section] = total.astype(jnp.bfloat16)


def add_terms(in_ref, out_ref):
    total = in_ref[0].astype(jnp.float32)
    for far in range(1, in_ref.shape[0]):
        total = total + in_ref[far].astype(jnp.float32)
    out_ref[0] = total


def call(kernel, shape, dtype, args, flops=0, scalars=0):
    many = isinstance(dtype, tuple)
    outs = [jax.ShapeDtypeStruct(s, d) for s, d in zip(shape, dtype)] if many else jax.ShapeDtypeStruct(shape, dtype)
    vmem = pl.BlockSpec(memory_space=pltpu.VMEM)
    smem = pl.BlockSpec(memory_space=pltpu.SMEM)
    moved = sum(a.size * a.dtype.itemsize for a in args) + sum(o.size * o.dtype.itemsize for o in (outs if many else [outs]))
    return pl.pallas_call(
        kernel,
        out_shape=outs,
        in_specs=[smem] * scalars + [vmem] * (len(args) - scalars),
        out_specs=[vmem] * len(outs) if many else vmem,
        cost_estimate=pl.CostEstimate(flops=flops, bytes_accessed=moved, transcendentals=0),
        compiler_params=pltpu.CompilerParams(vmem_limit_bytes=24 << 20),
    )(*args)


def shards(enc_out, kv_weight, queries, out_grad):
    rows, model = enc_out.shape
    depth, both = kv_weight.shape[1:]
    sections = lax.axis_size("section")
    width = Z_HI * depth
    near_groups = [[far * NEAR + near for near in range(NEAR)] for far in range(Z_HI)]
    far_groups = [[far * NEAR + near for far in range(Z_HI)] for near in range(NEAR)]
    place = (lax.axis_index("dp") // NEAR).astype(jnp.int32).reshape(1)
    own = kv_weight[0]

    def shifted(step):
        pairs = [
            (far * NEAR + near, (far + step) % Z_HI * NEAR + near) for far in range(Z_HI) for near in range(NEAR)
        ]
        return lax.ppermute(own, "dp", pairs)

    def exchange(array, axis, groups=None):
        return lax.all_to_all(array, axis, 0, 0, axis_index_groups=groups)

    others = [shifted(step) for step in (1, 2, 3)]
    enc = call(split_columns, (NEAR, rows, width), jnp.bfloat16, [enc_out])
    enc = exchange(enc, "dp", near_groups)
    weights, kv = call(
        project,
        ((width, both), (NEAR, rows, both)),
        (jnp.bfloat16, jnp.float32),
        [place, own, *others, enc],
        flops=2 * NEAR * rows * width * both,
        scalars=1,
    )
    kv = exchange(kv, "dp", near_groups)
    dkv = call(attend, (rows, both), jnp.bfloat16, [kv, queries[0], out_grad[0]], flops=8 * rows * queries.size)
    dkv = exchange(jnp.broadcast_to(dkv[None], (NEAR, rows, both)), "dp", near_groups)
    piece = NEAR * rows // sections
    part = call(
        spread, (sections, piece, width), jnp.bfloat16, [dkv, weights], flops=2 * NEAR * rows * width * both
    )
    part = exchange(part, "section")
    terms = call(
        weight_terms, (Z_HI, depth, both), jnp.bfloat16, [enc, dkv], flops=2 * NEAR * rows * width * both
    )
    terms = exchange(terms, "dp", far_groups)
    sums = call(suffix_sums, (sections, piece, width), jnp.bfloat16, [part])
    sums = exchange(sums, "section")
    sums = exchange(sums.reshape(NEAR, rows, width), "dp", near_groups)
    enc_grad = call(join_columns, (1, rows, model), jnp.bfloat16, [sums])
    weight_grad = call(add_terms, (1, depth, both), jnp.float32, [terms])
    return enc_grad, weight_grad


def solution(mesh):
    in_specs = (
        P("dp", None),
        P("section", "dp", None),
        P("section", "dp", None),
        P("section", "dp", None),
    )
    out_specs = (P("section", "dp", None), P("section", "dp", None))
    return jax.shard_map(shards, mesh=mesh, in_specs=in_specs, out_specs=out_specs, check_vma=False)
```

time: 412 us -> 151 us (0.37)
  waiting for transfers between devices: 364 us -> 39.7 us
  starting transfers between devices: 0.12 us -> 56.9 us
  blocking collectives: 0 us -> 47.1 us
  other arithmetic: 20.4 us -> 0 us
  between operations: 13.8 us -> 0.74 us
  matrix products: 6.1 us -> 0 us
  local copies, waits for them, and re-layouts: 6.54 us -> 1.02 us
  Pallas kernels: 0 us -> 5.32 us
    all_gather x2 -> x0, waiting for transfers between devices: 243 us -> none  [the longest x1 146 us: carried_in(): gathered = lax.all_gather(part, axis)]
    unnamed x4 -> x0, waiting for transfers between devices: 121 us -> none
    all_to_all x0 -> x3, blocking collectives: none -> 47.1 us  [exchange(): return lax.all_to_all(array, axis, 0, 0, axis_index_groups=groups)]
    all_to_all x0 -> x4, starting transfers between devices: none -> 36.5 us  [exchange(): return lax.all_to_all(array, axis, 0, 0, axis_index_groups=groups)]
    all_to_all x0 -> x4, waiting for transfers between devices: none -> 32.4 us  [exchange(): return lax.all_to_all(array, axis, 0, 0, axis_index_groups=groups)]
    ppermute x0 -> x3, starting transfers between devices: none -> 20.4 us  [shifted(): return lax.ppermute(own, 'dp', pairs)]
    add x15 -> x0, other arithmetic: 19.6 us -> none  [add_terms(): return earlier + later]
    ppermute x0 -> x3, waiting for transfers between devices: none -> 7.23 us  [shifted(): return lax.ppermute(own, 'dp', pairs)]
  transfers between devices with their start and end apart: 3 -> 7, of which waited for: 3 -> 5; matrix products, arithmetic and copies ran while one was open for 1% -> 0% of each run, Pallas kernels for 0% -> 1%
where the time goes in v1:
time: 151 us
  starting transfers between devices  56.9 us (38%)
  blocking collectives  47.1 us (31%)
  waiting for transfers between devices  39.7 us (26%)
  Pallas kernels  5.32 us (4%)
    all_to_all x3, blocking collectives, exchange(): return lax.all_to_all(array, axis, 0, 0, axis_index_groups=groups)  47.1 us
    all_to_all x4, starting transfers between devices, exchange(): return lax.all_to_all(array, axis, 0, 0, axis_index_groups=groups)  36.5 us
    all_to_all x4, waiting for transfers between devices, exchange(): return lax.all_to_all(array, axis, 0, 0, axis_index_groups=groups)  32.4 us
    ppermute x3, starting transfers between devices, shifted(): return lax.ppermute(own, 'dp', pairs)  20.4 us
    ppermute x3, waiting for transfers between devices, shifted(): return lax.ppermute(own, 'dp', pairs)  7.23 us
    pallas_call x8, Pallas kernels, call(): pl.pallas_call(kernel, out_shape=outs, in_specs=[smem] * scalars + [vmem]...  5.32 us
  transfers between devices with their start and end apart: 7, of which 5 were waited for; matrix products, arithmetic and copies ran while one was open for 0% of the time, Pallas kernels for 1%

profile of v1, /device:TPU:1, one launch (start us, length us, event | category | flops | bytes accessed | tf_op | source)
XLA Modules:
  0.0 150.7 jit_solution(16687964995795870508)
XLA Ops:
  0.6 0.0 copy-start
  0.6 1.0 copy-done
  1.6 0.9 shard_map.59
  2.5 0.0 copy-start.3
  2.5 10.4 %all-to-all-start = ((bf16[8,32,768]{2,1,0:T(8,128)(2,1)}), bf16[8,32,768]{2,1,0:T(8,128)(2,1)S(1)}, u32[]{:S(2)}, u32[]{:S(2)}) async-start(bf16[8,32,768]{2,1,0:T(8,128)(2,1)} %shard_map.59), calls=%async_computation | async-start | bytes 786432 | tf_op jit(solution)/shard_map/all_to_all | solution.py:130
  12.9 0.0 copy-done.3
  12.9 8.2 %collective-permute-start.2 = (bf16[192,256]{1,0:T(8,128)(2,1)S(1)}, bf16[192,256]{1,0:T(8,128)(2,1)S(1)}, u32[]{:S(2)}, u32[]{:S(2)}) collective-permute-start(bf16[192,256]{1,0:T(8,128)(2,1)S(1)} %bitcast.7), channel_id=1, source_target_pairs={{0,24},{1,25},{2,26},{3,27},{4,28},{5,29},{6,30},{7,31},{8,0},{9,1... | collective-permute-start | bytes 294920 | tf_op jit(solution)/shard_map/ppermute | solution.py:127
  21.1 4.9 %collective-permute-start.1 = (bf16[192,256]{1,0:T(8,128)(2,1)S(1)}, bf16[192,256]{1,0:T(8,128)(2,1)S(1)}, u32[]{:S(2)}, u32[]{:S(2)}) collective-permute-start(bf16[192,256]{1,0:T(8,128)(2,1)S(1)} %bitcast.8), channel_id=1, source_target_pairs={{0,16},{1,17},{2,18},{3,19},{4,20},{5,21},{6,22},{7,23},{8,24},{9,... | collective-permute-start | bytes 294920 | tf_op jit(solution)/shard_map/ppermute | solution.py:127
  26.0 7.3 %collective-permute-start = (bf16[192,256]{1,0:T(8,128)(2,1)S(1)}, bf16[192,256]{1,0:T(8,128)(2,1)S(1)}, u32[]{:S(2)}, u32[]{:S(2)}) collective-permute-start(bf16[192,256]{1,0:T(8,128)(2,1)S(1)} %bitcast.9), channel_id=1, source_target_pairs={{0,8},{1,9},{2,10},{3,11},{4,12},{5,13},{6,14},{7,15},{8,16},{9,17... | collective-permute-start | bytes 294920 | tf_op jit(solution)/shard_map/ppermute | solution.py:127
  33.3 0.0 collective-permute-done.2.three_ref
  33.3 2.7 %collective-permute-done.1.two_ref = bf16[192,256]{1,0:T(8,128)(2,1)S(1)} collective-permute-done((bf16[192,256]{1,0:T(8,128)(2,1)S(1)}, bf16[192,256]{1,0:T(8,128)(2,1)S(1)}, u32[]{:S(2)}, u32[]{:S(2)}) %collective-permute-start.1) | collective-permute-done | bytes 98336 | tf_op jit(solution)/shard_map/ppermute | solution.py:127
  36.0 4.5 %collective-permute-done.one_ref = bf16[192,256]{1,0:T(8,128)(2,1)S(1)} collective-permute-done((bf16[192,256]{1,0:T(8,128)(2,1)S(1)}, bf16[192,256]{1,0:T(8,128)(2,1)S(1)}, u32[]{:S(2)}, u32[]{:S(2)}) %collective-permute-start) | collective-permute-done | bytes 98336 | tf_op jit(solution)/shard_map/ppermute | solution.py:127
  40.5 0.0 all-to-all-done.enc_ref
  40.5 0.3 shard_map.60
  40.8 0.0 copy-start.1
  40.8 0.0 copy-start.2
  40.8 11.8 %all_to_all.35.kv_ref = f32[8,32,256]{2,1,0:T(8,128)S(1)} all-to-all(f32[8,32,256]{2,1,0:T(8,128)S(1)} %get-tuple-element.4), channel_id=1, replica_groups={{0,1,2,3,4,5,6,7},{8,9,10,11,12,13,14,15},{16,17,18,19,20,21,22,23},{24..., dimensions={0} | all-to-all | bytes 524288 | tf_op jit(solution)/shard_map/all_to_all | solution.py:130
  52.6 0.0 copy-done.1
  52.6 0.0 copy-done.2
  52.6 0.4 shard_map.61
  53.0 8.7 %all_to_all.36.dkv_ref = bf16[8,32,256]{2,1,0:T(8,128)(2,1)S(1)} all-to-all(bf16[8,32,256]{2,1,0:T(8,128)(2,1)S(1)} %broadcast_in_dim.2), channel_id=1, replica_groups={{0,1,2,3,4,5,6,7},{8,9,10,11,12,13,14,15},{16,17,18,19,20,21,22,23},{24..., dimensions={0} | all-to-all | bytes 262144 | tf_op jit(solution)/shard_map/all_to_all | solution.py:130
  61.7 1.0 shard_map.62
  62.8 12.0 %all-to-all-start.3 = ((bf16[16,16,768]{2,1,0:T(8,128)(2,1)}), bf16[16,16,768]{2,1,0:T(8,128)(2,1)S(1)}, u32[]{:S(2)}, u32[]{:S(2)}) async-start(bf16[16,16,768]{2,1,0:T(8,128)(2,1)} %shard_map.62), calls=%async_computation.3 | async-start | bytes 786432 | tf_op jit(solution)/shard_map/all_to_all | solution.py:130
  74.8 1.1 shard_map.65
  75.8 10.4 %all-to-all-done.3.in_ref = bf16[16,16,768]{2,1,0:T(8,128)(2,1)S(1)} async-done(((bf16[16,16,768]{2,1,0:T(8,128)(2,1)}), bf16[16,16,768]{2,1,0:T(8,128)(2,1)S(1)}, u32[]{:S(2)}, u32[]{:S(2)}) %all-to-all-start.3) | async-done | bytes 393248 | tf_op jit(solution)/shard_map/all_to_all | solution.py:130
  86.2 8.5 %all-to-all-start.6 = ((bf16[4,192,256]{2,1,0:T(8,128)(2,1)}), bf16[4,192,256]{2,1,0:T(8,128)(2,1)S(1)}, u32[]{:S(2)}, u32[]{:S(2)}) async-start(bf16[4,192,256]{2,1,0:T(8,128)(2,1)} %shard_map.65), calls=%async_computation.6 | async-start | bytes 786432 | tf_op jit(solution)/shard_map/all_to_all | solution.py:130
  94.8 0.1 shard_map.63
  94.8 14.6 %all-to-all-done.6.in_ref = bf16[4,192,256]{2,1,0:T(8,128)(2,1)S(1)} async-done(((bf16[4,192,256]{2,1,0:T(8,128)(2,1)}), bf16[4,192,256]{2,1,0:T(8,128)(2,1)S(1)}, u32[]{:S(2)}, u32[]{:S(2)}) %all-to-all-start.6) | async-done | bytes 393248 | tf_op jit(solution)/shard_map/all_to_all | solution.py:130
  109.5 26.6 %all_to_all.37 = bf16[16,16,768]{2,1,0:T(8,128)(2,1)} all-to-all(bf16[16,16,768]{2,1,0:T(8,128)(2,1)S(1)} %shard_map.63), channel_id=1, replica_groups=mesh['section'=16,'dp'=32] {'section'}, dimensions={0} | all-to-all | bytes 786432 | tf_op jit(solution)/shard_map/all_to_all | solution.py:130
  136.1 5.7 %all-to-all-start.5 = ((bf16[8,32,768]{2,1,0:T(8,128)(2,1)}), bf16[8,32,768]{2,1,0:T(8,128)(2,1)S(1)}, u32[]{:S(2)}, u32[]{:S(2)}) async-start(bf16[8,32,768]{2,1,0:T(8,128)(2,1)} %bitcast.4), calls=%async_computation.5 | async-start | bytes 786432 | tf_op jit(solution)/shard_map/all_to_all | solution.py:130
  141.7 0.7 shard_map.66
  142.5 7.4 %all-to-all-done.5.in_ref = bf16[8,32,768]{2,1,0:T(8,128)(2,1)S(1)} async-done(((bf16[8,32,768]{2,1,0:T(8,128)(2,1)}), bf16[8,32,768]{2,1,0:T(8,128)(2,1)S(1)}, u32[]{:S(2)}, u32[]{:S(2)}) %all-to-all-start.5) | async-done | bytes 393248 | tf_op jit(solution)/shard_map/all_to_all | solution.py:130
  149.8 0.9 shard_map.64
  (1 shorter events, 0.0 us)
Async XLA Ops:
  0.6 1.0 copy-start
  2.5 10.4 %copy-start.3 = (bf16[1,192,256]{2,1,0:T(8,128)(2,1)S(1)}, bf16[1,192,256]{2,1,0:T(8,128)(2,1)}, u32[]{:S(2)}) copy-start(bf16[1,192,256]{2,1,0:T(8,128)(2,1)} %param.5) | copy-start | bytes 294916
  2.5 38.0 %all-to-all-start = ((bf16[8,32,768]{2,1,0:T(8,128)(2,1)}), bf16[8,32,768]{2,1,0:T(8,128)(2,1)S(1)}, u32[]{:S(2)}, u32[]{:S(2)}) async-start(bf16[8,32,768]{2,1,0:T(8,128)(2,1)} %shard_map.59), calls=%async_computation | async-start | bytes 786432 | tf_op jit(solution)/shard_map/all_to_all | solution.py:130
  12.9 20.4 %collective-permute-start.2 = (bf16[192,256]{1,0:T(8,128)(2,1)S(1)}, bf16[192,256]{1,0:T(8,128)(2,1)S(1)}, u32[]{:S(2)}, u32[]{:S(2)}) collective-permute-start(bf16[192,256]{1,0:T(8,128)(2,1)S(1)} %bitcast.7), channel_id=1, source_target_pairs={{0,24},{1,25},{2,26},{3,27},{4,28},{5,29},{6,30},{7,31},{8,0},{9,1... | collective-permute-start | bytes 294920 | tf_op jit(solution)/shard_map/ppermute | solution.py:127
  21.1 14.9 %collective-permute-start.1 = (bf16[192,256]{1,0:T(8,128)(2,1)S(1)}, bf16[192,256]{1,0:T(8,128)(2,1)S(1)}, u32[]{:S(2)}, u32[]{:S(2)}) collective-permute-start(bf16[192,256]{1,0:T(8,128)(2,1)S(1)} %bitcast.8), channel_id=1, source_target_pairs={{0,16},{1,17},{2,18},{3,19},{4,20},{5,21},{6,22},{7,23},{8,24},{9,... | collective-permute-start | bytes 294920 | tf_op jit(solution)/shard_map/ppermute | solution.py:127
  26.0 14.5 %collective-permute-start = (bf16[192,256]{1,0:T(8,128)(2,1)S(1)}, bf16[192,256]{1,0:T(8,128)(2,1)S(1)}, u32[]{:S(2)}, u32[]{:S(2)}) collective-permute-start(bf16[192,256]{1,0:T(8,128)(2,1)S(1)} %bitcast.9), channel_id=1, source_target_pairs={{0,8},{1,9},{2,10},{3,11},{4,12},{5,13},{6,14},{7,15},{8,16},{9,17... | collective-permute-start | bytes 294920 | tf_op jit(solution)/shard_map/ppermute | solution.py:127
  40.8 11.8 %copy-start.1 = (bf16[1,512,128]{2,1,0:T(8,128)(2,1)S(1)}, bf16[1,512,128]{2,1,0:T(8,128)(2,1)}, u32[]{:S(2)}) copy-start(bf16[1,512,128]{2,1,0:T(8,128)(2,1)} %param.6) | copy-start | bytes 393220
  40.8 11.8 %copy-start.2 = (bf16[1,512,128]{2,1,0:T(8,128)(2,1)S(1)}, bf16[1,512,128]{2,1,0:T(8,128)(2,1)}, u32[]{:S(2)}) copy-start(bf16[1,512,128]{2,1,0:T(8,128)(2,1)} %param.7) | copy-start | bytes 393220
  62.8 23.5 %all-to-all-start.3 = ((bf16[16,16,768]{2,1,0:T(8,128)(2,1)}), bf16[16,16,768]{2,1,0:T(8,128)(2,1)S(1)}, u32[]{:S(2)}, u32[]{:S(2)}) async-start(bf16[16,16,768]{2,1,0:T(8,128)(2,1)} %shard_map.62), calls=%async_computation.3 | async-start | bytes 786432 | tf_op jit(solution)/shard_map/all_to_all | solution.py:130
  86.2 23.2 %all-to-all-start.6 = ((bf16[4,192,256]{2,1,0:T(8,128)(2,1)}), bf16[4,192,256]{2,1,0:T(8,128)(2,1)S(1)}, u32[]{:S(2)}, u32[]{:S(2)}) async-start(bf16[4,192,256]{2,1,0:T(8,128)(2,1)} %shard_map.65), calls=%async_computation.6 | async-start | bytes 786432 | tf_op jit(solution)/shard_map/all_to_all | solution.py:130
  136.1 13.8 %all-to-all-start.5 = ((bf16[8,32,768]{2,1,0:T(8,128)(2,1)}), bf16[8,32,768]{2,1,0:T(8,128)(2,1)S(1)}, u32[]{:S(2)}, u32[]{:S(2)}) async-start(bf16[8,32,768]{2,1,0:T(8,128)(2,1)} %bitcast.4), calls=%async_computation.5 | async-start | bytes 786432 | tf_op jit(solution)/shard_map/all_to_all | solution.py:130

commit v2 on v1

v2 whole, which is shorter than its diff:
```python
import jax
import jax.numpy as jnp
from jax import lax
from jax.experimental import pallas as pl
from jax.experimental.pallas import tpu as pltpu
from jax.sharding import PartitionSpec as P

Z_HI = 4
Z_LO = 4
NEAR = 8


def contract(left, right, left_dim, right_dim):
    return lax.dot_general(
        left, right, (((left_dim,), (right_dim,)), ((), ())), preferred_element_type=jnp.float32
    )


def split_columns(enc_ref, out_ref):
    width = out_ref.shape[2] // Z_HI
    for near in range(NEAR):
        for far in range(Z_HI):
            start = (far * NEAR + near) * width
            out_ref[near, :, far * width : (far + 1) * width] = enc_ref[:, start : start + width]


def join_columns(in_ref, out_ref):
    width = in_ref.shape[2] // Z_HI
    for near in range(NEAR):
        for far in range(Z_HI):
            start = (far * NEAR + near) * width
            out_ref[0, :, start : start + width] = in_ref[near, :, far * width : (far + 1) * width]


def project(enc_ref, weights_ref, kv_ref):
    near, rows, width = enc_ref.shape
    enc = enc_ref[...].reshape(near * rows, width)
    kv = jnp.dot(enc, weights_ref[...], preferred_element_type=jnp.float32)
    kv_ref[...] = kv.reshape(near, rows, kv.shape[1])


def attend(kv_ref, queries_ref, grad_ref, dkv_ref):
    kv = kv_ref[0]
    for near in range(1, kv_ref.shape[0]):
        kv = kv + kv_ref[near]
    kv = kv.astype(jnp.bfloat16)
    head = queries_ref.shape[1]
    scale = 1.0 / head**0.5
    queries = queries_ref[...]
    grad = grad_ref[...]
    scores = contract(kv[:, :head], queries, 1, 1) * scale
    expd = jnp.exp(scores - jnp.max(scores, axis=0, keepdims=True))
    probs = expd / jnp.sum(expd, axis=0, keepdims=True)
    dprobs = contract(kv[:, head:], grad, 1, 1)
    delta = jnp.sum(probs * dprobs, axis=0, keepdims=True)
    dscores = (probs * (dprobs - delta) * scale).astype(jnp.bfloat16)
    dkv_ref[:, :head] = contract(dscores, queries, 1, 0).astype(jnp.bfloat16)
    dkv_ref[:, head:] = contract(probs.astype(jnp.bfloat16), grad, 1, 0).astype(jnp.bfloat16)


def spread(dkv_ref, weights_ref, out_ref):
    near, rows, width = dkv_ref.shape
    dkv = dkv_ref[...].reshape(near * rows, width)
    out = contract(dkv, weights_ref[...], 1, 1)
    out_ref[...] = out.astype(jnp.bfloat16).reshape(out_ref.shape)


def weight_terms(place_ref, enc_ref, dkv_ref, own_ref, next_ref, far_ref, last_ref, terms_ref):
    near, rows, width = dkv_ref.shape
    dkv = dkv_ref[...].reshape(near * rows, width)
    enc = enc_ref[...].reshape(near * rows, enc_ref.shape[2])
    terms = contract(enc, dkv, 0, 0)
    depth = own_ref.shape[0]
    for far in range(Z_HI):
        terms_ref[far] = terms[far * depth : (far + 1) * depth]
    for step, ref in enumerate((own_ref, next_ref, far_ref, last_ref)):
        ref[...] = terms_ref[lax.rem(place_ref[0] + step, Z_HI)].astype(ref.dtype)


def row_total(in_ref, out_ref):
    total = in_ref[0].astype(jnp.float32)
    for step in range(1, in_ref.shape[0]):
        total = total + in_ref[step].astype(jnp.float32)
    out_ref[...] = total.astype(jnp.bfloat16)


def suffix_sums(in_ref, one_ref, two_ref, three_ref, out_ref):
    total = one_ref[...].astype(jnp.float32) + two_ref[...].astype(jnp.float32) + three_ref[...].astype(jnp.float32)
    for step in range(in_ref.shape[0] - 1, -1, -1):
        total = total + in_ref[step].astype(jnp.float32)
        out_ref[step] = total.astype(jnp.bfloat16)


def add_terms(own_ref, *refs):
    total = own_ref[...]
    for ref in refs[:-1]:
        total = total + ref[...].astype(jnp.float32)
    refs[-1][...] = total.astype(refs[-1].dtype)


def call(kernel, outs, args, flops=0, scalars=0, scratch=()):
    outs = [jax.ShapeDtypeStruct(shape, dtype) for shape, dtype in outs]
    vmem = pl.BlockSpec(memory_space=pltpu.VMEM)
    smem = pl.BlockSpec(memory_space=pltpu.SMEM)
    moved = sum(a.size * a.dtype.itemsize for a in [*args, *outs])
    results = pl.pallas_call(
        kernel,
        out_shape=outs,
        in_specs=[smem] * scalars + [vmem] * (len(args) - scalars),
        out_specs=[vmem] * len(outs),
        scratch_shapes=scratch,
        cost_estimate=pl.CostEstimate(flops=flops, bytes_accessed=moved, transcendentals=0),
        compiler_params=pltpu.CompilerParams(vmem_limit_bytes=24 << 20),
    )(*args)
    return results[0] if len(outs) == 1 else results


def shards(enc_out, kv_weight, queries, out_grad):
    rows, model = enc_out.shape
    depth, both = kv_weight.shape[1:]
    sections = lax.axis_size("section")
    width = Z_HI * depth
    low, high = jnp.bfloat16, jnp.float32
    near_groups = [[far * NEAR + near for near in range(NEAR)] for far in range(Z_HI)]
    far_groups = [[far * NEAR + near for far in range(Z_HI)] for near in range(NEAR)]
    place = lax.div(lax.axis_index("dp"), NEAR).astype(jnp.int32).reshape(1)
    work = 2 * NEAR * rows * width * both

    def shifted(array, step):
        pairs = [
            (far * NEAR + near, (far + step) % Z_HI * NEAR + near) for far in range(Z_HI) for near in range(NEAR)
        ]
        return lax.ppermute(array, "dp", pairs)

    def exchange(array, axis, groups=None):
        return lax.all_to_all(array, axis, 0, 0, axis_index_groups=groups)

    enc = call(split_columns, [((NEAR, rows, width), low)], [enc_out])
    own, enc = lax.optimization_barrier((kv_weight[0], enc))
    enc = exchange(enc, "dp", near_groups)
    weights = lax.all_gather(own, "dp", axis=0, tiled=True, axis_index_groups=far_groups)
    kv = call(project, [((NEAR, rows, both), high)], [enc, weights], flops=work)
    kv = exchange(kv, "dp", near_groups)
    dkv = call(attend, [((rows, both), low)], [kv, queries[0], out_grad[0]], flops=8 * rows * queries.size)
    dkv = exchange(jnp.broadcast_to(dkv[None], (NEAR, rows, both)), "dp", near_groups)
    line = sections // Z_LO
    line_groups = [[up * line + step for step in range(line)] for up in range(Z_LO)]
    piece = NEAR * rows // line

    def lowered(array, step):
        pairs = [(up * line + at, (up - step) * line + at) for up in range(step, Z_LO) for at in range(line)]
        return lax.ppermute(array, "section", pairs)

    part = call(spread, [((line, piece, width), low)], [dkv, weights], flops=work)
    part, dkv = lax.optimization_barrier((part, dkv))
    part = exchange(part, "section", line_groups)
    mine, after, beyond, before = call(
        weight_terms,
        [((depth, both), high)] * 2 + [((depth, both), low)] * 2,
        [place, enc, dkv],
        flops=work,
        scalars=1,
        scratch=[pltpu.VMEM((Z_HI, depth, both), high)],
    )
    beyond = shifted(beyond, 1)
    before = shifted(before, 3)
    total = call(row_total, [((piece, width), low)], [part])
    above = [lowered(total, step) for step in range(1, Z_LO)]
    above, beyond = lax.optimization_barrier((above, beyond))
    sums = call(suffix_sums, [((line, piece, width), low)], [part, *above])
    sums = exchange(sums, "section", line_groups)
    sums = exchange(sums.reshape(NEAR, rows, width), "dp", near_groups)
    after = call(add_terms, [((depth, both), low)], [after, beyond])
    after = shifted(after, 1)
    mine = call(add_terms, [((depth, both), high)], [mine, before], flops=30_000_000_000)
    sums, mine = lax.optimization_barrier((sums, mine))
    enc_grad = call(join_columns, [((1, rows, model), low)], [sums])
    enc_grad, mine, after = lax.optimization_barrier((enc_grad, mine, after))
    weight_grad = call(add_terms, [((depth, both), high)], [mine, after])[None]
    return enc_grad, weight_grad


def solution(mesh):
    in_specs = (
        P("dp", None),
        P("section", "dp", None),
        P("section", "dp", None),
        P("section", "dp", None),
    )
    out_specs = (P("section", "dp", None), P("section", "dp", None))
    return jax.shard_map(shards, mesh=mesh, in_specs=in_specs, out_specs=out_specs, check_vma=False)
```

time: 151 us -> 115 us (0.76)
  waiting for transfers between devices: 39.7 us -> 17.3 us
  starting transfers between devices: 56.9 us -> 44.8 us
  blocking collectives: 47.1 us -> 44.5 us
    all_to_all x3 -> x2, blocking collectives: 47.1 us -> 21.8 us  [exchange(): return lax.all_to_all(array, axis, 0, 0, axis_index_groups=groups)]
    all_to_all x4, waiting for transfers between devices: 32.4 us -> 8.59 us  [exchange(): return lax.all_to_all(array, axis, 0, 0, axis_index_groups=groups)]
    all_gather x0 -> x1, blocking collectives: none -> 22.7 us  [shards(): lax.all_gather(own, 'dp', axis=0, tiled=True, axis_index_groups=far_groups)]
    all_to_all x4, starting transfers between devices: 36.5 us -> 26 us  [exchange(): return lax.all_to_all(array, axis, 0, 0, axis_index_groups=groups)]
    ppermute x3 -> x6, starting transfers between devices: 20.4 us -> 18.8 us  [the longest x3 14.9 us: shifted(): return lax.ppermute(array, 'dp', pairs)]
    ppermute x3 -> x6, waiting for transfers between devices: 7.23 us -> 8.71 us  [the longest x3 8.71 us: lowered(): return lax.ppermute(array, 'section', pairs)]
    pallas_call x8 -> x11, Pallas kernels: 5.32 us -> 5.48 us  [call(): pl.pallas_call(kernel, out_shape=outs, in_specs=[smem] * scalars + [vmem]...]
  transfers between devices with their start and end apart: 7 -> 10, of which waited for: 5 -> 5; matrix products, arithmetic and copies ran while one was open for 0% -> 0% of each run, Pallas kernels for 1% -> 1%
where the time goes in v2:
time: 115 us; the launch traced here: 114 us
  starting transfers between devices  44.8 us (39%)
  blocking collectives  44.5 us (39%)
  waiting for transfers between devices  17.3 us (15%)
  Pallas kernels  5.48 us (5%)
    all_to_all x4, starting transfers between devices, exchange(): return lax.all_to_all(array, axis, 0, 0, axis_index_groups=groups)  26 us
    all_gather x1, blocking collectives, shards(): lax.all_gather(own, 'dp', axis=0, tiled=True, axis_index_groups=far_groups)  22.7 us
    all_to_all x2, blocking collectives, exchange(): return lax.all_to_all(array, axis, 0, 0, axis_index_groups=groups)  21.8 us
    ppermute x3, starting transfers between devices, shifted(): return lax.ppermute(array, 'dp', pairs)  14.9 us
    ppermute x3, waiting for transfers between devices, lowered(): return lax.ppermute(array, 'section', pairs)  8.71 us
    all_to_all x4, waiting for transfers between devices, exchange(): return lax.all_to_all(array, axis, 0, 0, axis_index_groups=groups)  8.59 us
    pallas_call x11, Pallas kernels, call(): pl.pallas_call(kernel, out_shape=outs, in_specs=[smem] * scalars + [vmem]...  5.48 us
    ppermute x3, starting transfers between devices, lowered(): return lax.ppermute(array, 'section', pairs)  3.88 us
  transfers between devices with their start and end apart: 10, of which 5 were waited for; matrix products, arithmetic and copies ran while one was open for 0% of the time, Pallas kernels for 1%

profile of v2, /device:TPU:1, one launch (start us, length us, event | category | flops | bytes accessed | tf_op | source)
XLA Modules:
  0.0 113.9 jit_solution(13734773012413907027)
XLA Ops:
  0.6 0.0 copy-start
  0.6 1.0 copy-done
  1.6 0.9 shard_map.59
  2.5 0.0 copy-start.3
  2.5 10.4 %all-to-all-start = ((bf16[8,32,768]{2,1,0:T(8,128)(2,1)}), bf16[8,32,768]{2,1,0:T(8,128)(2,1)S(1)}, u32[]{:S(2)}, u32[]{:S(2)}) async-start(bf16[8,32,768]{2,1,0:T(8,128)(2,1)} %shard_map.59), calls=%async_computation | async-start | bytes 786432 | tf_op jit(solution)/shard_map/all_to_all | solution.py:136
  12.9 0.0 copy-done.3
  12.9 22.7 %all_gather.3.weights_ref = bf16[768,256]{1,0:T(8,128)(2,1)S(1)} all-gather(bf16[192,256]{1,0:T(8,128)(2,1)S(1)} %bitcast.9), channel_id=1, replica_groups={{0,8,16,24},{1,9,17,25},{2,10,18,26},{3,11,19,27},{4,12,20,28},{5,13,21..., dimensions={0}, use_global_device_ids=true | all-gather | bytes 491520 | tf_op jit(solution)/shard_map/all_gather | solution.py:141
  35.6 0.0 all-to-all-done.enc_ref
  35.6 0.3 shard_map.60
  35.8 0.0 copy-start.1
  35.9 0.0 copy-start.2
  35.9 13.1 %all_to_all.30.kv_ref = f32[8,32,256]{2,1,0:T(8,128)S(1)} all-to-all(f32[8,32,256]{2,1,0:T(8,128)S(1)} %shard_map.60), channel_id=1, replica_groups={{0,1,2,3,4,5,6,7},{8,9,10,11,12,13,14,15},{16,17,18,19,20,21,22,23},{24..., dimensions={0} | all-to-all | bytes 524288 | tf_op jit(solution)/shard_map/all_to_all | solution.py:136
  49.0 0.0 copy-done.1
  49.0 0.0 copy-done.2
  49.0 0.4 shard_map.61
  49.4 8.7 %all_to_all.31.dkv_ref = bf16[8,32,256]{2,1,0:T(8,128)(2,1)S(1)} all-to-all(bf16[8,32,256]{2,1,0:T(8,128)(2,1)S(1)} %broadcast_in_dim.4), channel_id=1, replica_groups={{0,1,2,3,4,5,6,7},{8,9,10,11,12,13,14,15},{16,17,18,19,20,21,22,23},{24..., dimensions={0} | all-to-all | bytes 262144 | tf_op jit(solution)/shard_map/all_to_all | solution.py:136
  58.1 1.0 shard_map.62
  59.1 4.0 %all-to-all-start.3 = ((bf16[4,64,768]{2,1,0:T(8,128)(2,1)}), bf16[4,64,768]{2,1,0:T(8,128)(2,1)S(1)}, u32[]{:S(2)}, u32[]{:S(2)}) async-start(bf16[4,64,768]{2,1,0:T(8,128)(2,1)} %shard_map.62), calls=%async_computation.3 | async-start | bytes 786432 | tf_op jit(solution)/shard_map/all_to_all | solution.py:136
  63.1 0.4 shard_map.64
  63.5 5.7 %collective-permute-start.3 = (bf16[192,256]{1,0:T(8,128)(2,1)S(1)}, bf16[192,256]{1,0:T(8,128)(2,1)S(1)}, u32[]{:S(2)}, u32[]{:S(2)}) collective-permute-start(bf16[192,256]{1,0:T(8,128)(2,1)S(1)} %get-tuple-element.23), channel_id=1, source_target_pairs={{0,8},{1,9},{2,10},{3,11},{4,12},{5,13},{6,14},{7,15},{8,16},{9,17... | collective-permute-start | bytes 294920 | tf_op jit(solution)/shard_map/ppermute | solution.py:133
  69.3 0.5 all-to-all-done.3.in_ref
  69.8 0.1 shard_map.63
  69.9 1.3 %collective-permute-start = (bf16[64,768]{1,0:T(8,128)(2,1)S(1)}, bf16[64,768]{1,0:T(8,128)(2,1)S(1)}, u32[]{:S(2)}, u32[]{:S(2)}) collective-permute-start(bf16[64,768]{1,0:T(8,128)(2,1)S(1)} %shard_map.63), channel_id=1, source_target_pairs={{128,0},{160,32},{192,64},{224,96},{256,128},{288,160},{320,192},{... | collective-permute-start | bytes 294920 | tf_op jit(solution)/shard_map/ppermute | solution.py:152
  71.2 1.3 %collective-permute-start.1 = (bf16[64,768]{1,0:T(8,128)(2,1)S(1)}, bf16[64,768]{1,0:T(8,128)(2,1)S(1)}, u32[]{:S(2)}, u32[]{:S(2)}) collective-permute-start(bf16[64,768]{1,0:T(8,128)(2,1)S(1)} %shard_map.63), channel_id=1, source_target_pairs={{256,0},{288,32},{320,64},{352,96},{384,128},{416,160},{448,192},{... | collective-permute-start | bytes 294920 | tf_op jit(solution)/shard_map/ppermute | solution.py:152
  72.5 1.3 %collective-permute-start.2 = (bf16[64,768]{1,0:T(8,128)(2,1)S(1)}, bf16[64,768]{1,0:T(8,128)(2,1)S(1)}, u32[]{:S(2)}, u32[]{:S(2)}) collective-permute-start(bf16[64,768]{1,0:T(8,128)(2,1)S(1)} %shard_map.63), channel_id=1, source_target_pairs={{384,0},{416,32},{448,64},{480,96},{385,1},{417,33},{449,65},{481,... | collective-permute-start | bytes 294920 | tf_op jit(solution)/shard_map/ppermute | solution.py:152
  73.8 0.0 collective-permute-done.3.refs_0_
  73.8 2.6 %collective-permute-done.one_ref = bf16[64,768]{1,0:T(8,128)(2,1)S(1)} collective-permute-done((bf16[64,768]{1,0:T(8,128)(2,1)S(1)}, bf16[64,768]{1,0:T(8,128)(2,1)S(1)}, u32[]{:S(2)}, u32[]{:S(2)}) %collective-permute-start) | collective-permute-done | bytes 98336 | tf_op jit(solution)/shard_map/ppermute | solution.py:152
  76.4 2.3 %collective-permute-done.1.two_ref = bf16[64,768]{1,0:T(8,128)(2,1)S(1)} collective-permute-done((bf16[64,768]{1,0:T(8,128)(2,1)S(1)}, bf16[64,768]{1,0:T(8,128)(2,1)S(1)}, u32[]{:S(2)}, u32[]{:S(2)}) %collective-permute-start.1) | collective-permute-done | bytes 98336 | tf_op jit(solution)/shard_map/ppermute | solution.py:152
  78.7 3.8 %collective-permute-done.2.three_ref = bf16[64,768]{1,0:T(8,128)(2,1)S(1)} collective-permute-done((bf16[64,768]{1,0:T(8,128)(2,1)S(1)}, bf16[64,768]{1,0:T(8,128)(2,1)S(1)}, u32[]{:S(2)}, u32[]{:S(2)}) %collective-permute-start.2) | collective-permute-done | bytes 98336 | tf_op jit(solution)/shard_map/ppermute | solution.py:152
  82.5 0.8 shard_map.65
  83.3 4.1 %all-to-all-start.4 = ((bf16[4,64,768]{2,1,0:T(8,128)(2,1)}), bf16[4,64,768]{2,1,0:T(8,128)(2,1)}, u32[]{:S(2)}, u32[]{:S(2)}) async-start(bf16[4,64,768]{2,1,0:T(8,128)(2,1)} %shard_map.65), calls=%async_computation.4 | async-start | bytes 786432 | tf_op jit(solution)/shard_map/all_to_all | solution.py:136
  87.4 4.6 %collective-permute-start.4 = (bf16[192,256]{1,0:T(8,128)(2,1)S(1)}, bf16[192,256]{1,0:T(8,128)(2,1)S(1)}, u32[]{:S(2)}, u32[]{:S(2)}) collective-permute-start(bf16[192,256]{1,0:T(8,128)(2,1)S(1)} %get-tuple-element.28), channel_id=1, source_target_pairs={{0,24},{1,25},{2,26},{3,27},{4,28},{5,29},{6,30},{7,31},{8,0},{9,1... | collective-permute-start | bytes 294920 | tf_op jit(solution)/shard_map/ppermute | solution.py:133
  92.1 4.6 %collective-permute-start.5 = (bf16[192,256]{1,0:T(8,128)(2,1)S(1)}, bf16[192,256]{1,0:T(8,128)(2,1)S(1)}, u32[]{:S(2)}, u32[]{:S(2)}) collective-permute-start(bf16[192,256]{1,0:T(8,128)(2,1)S(1)} %shard_map.68), channel_id=1, source_target_pairs={{0,8},{1,9},{2,10},{3,11},{4,12},{5,13},{6,14},{7,15},{8,16},{9,17... | collective-permute-start | bytes 294920 | tf_op jit(solution)/shard_map/ppermute | solution.py:133
  96.7 0.0 all-to-all-done.4
  96.7 7.5 %all-to-all-start.5 = ((bf16[8,32,768]{2,1,0:T(8,128)(2,1)}), bf16[8,32,768]{2,1,0:T(8,128)(2,1)S(1)}, u32[]{:S(2)}, u32[]{:S(2)}) async-start(bf16[8,32,768]{2,1,0:T(8,128)(2,1)} %bitcast.4), calls=%async_computation.5 | async-start | bytes 786432 | tf_op jit(solution)/shard_map/all_to_all | solution.py:136
  104.2 0.0 collective-permute-done.4.refs_0_
  104.2 8.1 %all-to-all-done.5.in_ref = bf16[8,32,768]{2,1,0:T(8,128)(2,1)S(1)} async-done(((bf16[8,32,768]{2,1,0:T(8,128)(2,1)}), bf16[8,32,768]{2,1,0:T(8,128)(2,1)S(1)}, u32[]{:S(2)}, u32[]{:S(2)}) %all-to-all-start.5) | async-done | bytes 393248 | tf_op jit(solution)/shard_map/all_to_all | solution.py:136
  112.3 0.9 shard_map.67
  113.2 0.0 collective-permute-done.5.refs_0_
  113.2 0.7 shard_map.69
  (3 shorter events, 0.1 us)
Async XLA Ops:
  0.6 1.0 copy-start
  2.5 10.4 %copy-start.3 = (bf16[1,192,256]{2,1,0:T(8,128)(2,1)S(1)}, bf16[1,192,256]{2,1,0:T(8,128)(2,1)}, u32[]{:S(2)}) copy-start(bf16[1,192,256]{2,1,0:T(8,128)(2,1)} %param.5) | copy-start | bytes 294916
  2.5 33.1 %all-to-all-start = ((bf16[8,32,768]{2,1,0:T(8,128)(2,1)}), bf16[8,32,768]{2,1,0:T(8,128)(2,1)S(1)}, u32[]{:S(2)}, u32[]{:S(2)}) async-start(bf16[8,32,768]{2,1,0:T(8,128)(2,1)} %shard_map.59), calls=%async_computation | async-start | bytes 786432 | tf_op jit(solution)/shard_map/all_to_all | solution.py:136
  35.8 13.1 %copy-start.1 = (bf16[1,512,128]{2,1,0:T(8,128)(2,1)S(1)}, bf16[1,512,128]{2,1,0:T(8,128)(2,1)}, u32[]{:S(2)}) copy-start(bf16[1,512,128]{2,1,0:T(8,128)(2,1)} %param.6) | copy-start | bytes 393220
  35.9 13.1 %copy-start.2 = (bf16[1,512,128]{2,1,0:T(8,128)(2,1)S(1)}, bf16[1,512,128]{2,1,0:T(8,128)(2,1)}, u32[]{:S(2)}) copy-start(bf16[1,512,128]{2,1,0:T(8,128)(2,1)} %param.7) | copy-start | bytes 393220
  59.1 10.7 %all-to-all-start.3 = ((bf16[4,64,768]{2,1,0:T(8,128)(2,1)}), bf16[4,64,768]{2,1,0:T(8,128)(2,1)S(1)}, u32[]{:S(2)}, u32[]{:S(2)}) async-start(bf16[4,64,768]{2,1,0:T(8,128)(2,1)} %shard_map.62), calls=%async_computation.3 | async-start | bytes 786432 | tf_op jit(solution)/shard_map/all_to_all | solution.py:136
  63.5 10.2 %collective-permute-start.3 = (bf16[192,256]{1,0:T(8,128)(2,1)S(1)}, bf16[192,256]{1,0:T(8,128)(2,1)S(1)}, u32[]{:S(2)}, u32[]{:S(2)}) collective-permute-start(bf16[192,256]{1,0:T(8,128)(2,1)S(1)} %get-tuple-element.23), channel_id=1, source_target_pairs={{0,8},{1,9},{2,10},{3,11},{4,12},{5,13},{6,14},{7,15},{8,16},{9,17... | collective-permute-start | bytes 294920 | tf_op jit(solution)/shard_map/ppermute | solution.py:133
  69.9 6.5 %collective-permute-start = (bf16[64,768]{1,0:T(8,128)(2,1)S(1)}, bf16[64,768]{1,0:T(8,128)(2,1)S(1)}, u32[]{:S(2)}, u32[]{:S(2)}) collective-permute-start(bf16[64,768]{1,0:T(8,128)(2,1)S(1)} %shard_map.63), channel_id=1, source_target_pairs={{128,0},{160,32},{192,64},{224,96},{256,128},{288,160},{320,192},{... | collective-permute-start | bytes 294920 | tf_op jit(solution)/shard_map/ppermute | solution.py:152
  71.2 7.5 %collective-permute-start.1 = (bf16[64,768]{1,0:T(8,128)(2,1)S(1)}, bf16[64,768]{1,0:T(8,128)(2,1)S(1)}, u32[]{:S(2)}, u32[]{:S(2)}) collective-permute-start(bf16[64,768]{1,0:T(8,128)(2,1)S(1)} %shard_map.63), channel_id=1, source_target_pairs={{256,0},{288,32},{320,64},{352,96},{384,128},{416,160},{448,192},{... | collective-permute-start | bytes 294920 | tf_op jit(solution)/shard_map/ppermute | solution.py:152
  72.5 10.0 %collective-permute-start.2 = (bf16[64,768]{1,0:T(8,128)(2,1)S(1)}, bf16[64,768]{1,0:T(8,128)(2,1)S(1)}, u32[]{:S(2)}, u32[]{:S(2)}) collective-permute-start(bf16[64,768]{1,0:T(8,128)(2,1)S(1)} %shard_map.63), channel_id=1, source_target_pairs={{384,0},{416,32},{448,64},{480,96},{385,1},{417,33},{449,65},{481,... | collective-permute-start | bytes 294920 | tf_op jit(solution)/shard_map/ppermute | solution.py:152
  83.3 13.4 %all-to-all-start.4 = ((bf16[4,64,768]{2,1,0:T(8,128)(2,1)}), bf16[4,64,768]{2,1,0:T(8,128)(2,1)}, u32[]{:S(2)}, u32[]{:S(2)}) async-start(bf16[4,64,768]{2,1,0:T(8,128)(2,1)} %shard_map.65), calls=%async_computation.4 | async-start | bytes 786432 | tf_op jit(solution)/shard_map/all_to_all | solution.py:136
  87.4 16.8 %collective-permute-start.4 = (bf16[192,256]{1,0:T(8,128)(2,1)S(1)}, bf16[192,256]{1,0:T(8,128)(2,1)S(1)}, u32[]{:S(2)}, u32[]{:S(2)}) collective-permute-start(bf16[192,256]{1,0:T(8,128)(2,1)S(1)} %get-tuple-element.28), channel_id=1, source_target_pairs={{0,24},{1,25},{2,26},{3,27},{4,28},{5,29},{6,30},{7,31},{8,0},{9,1... | collective-permute-start | bytes 294920 | tf_op jit(solution)/shard_map/ppermute | solution.py:133
  92.1 21.1 %collective-permute-start.5 = (bf16[192,256]{1,0:T(8,128)(2,1)S(1)}, bf16[192,256]{1,0:T(8,128)(2,1)S(1)}, u32[]{:S(2)}, u32[]{:S(2)}) collective-permute-start(bf16[192,256]{1,0:T(8,128)(2,1)S(1)} %shard_map.68), channel_id=1, source_target_pairs={{0,8},{1,9},{2,10},{3,11},{4,12},{5,13},{6,14},{7,15},{8,16},{9,17... | collective-permute-start | bytes 294920 | tf_op jit(solution)/shard_map/ppermute | solution.py:133
  96.7 15.6 %all-to-all-start.5 = ((bf16[8,32,768]{2,1,0:T(8,128)(2,1)}), bf16[8,32,768]{2,1,0:T(8,128)(2,1)S(1)}, u32[]{:S(2)}, u32[]{:S(2)}) async-start(bf16[8,32,768]{2,1,0:T(8,128)(2,1)} %bitcast.4), calls=%async_computation.5 | async-start | bytes 786432 | tf_op jit(solution)/shard_map/all_to_all | solution.py:136

commit v3 on v2

--- a/solution.py
+++ b/solution.py
@@ -25,11 +25,16 @@
 
 
 def join_columns(in_ref, out_ref):
-    width = in_ref.shape[2] // Z_HI
+    line = in_ref.shape[0] // NEAR
+    part = in_ref.shape[1] // 2
+    width = 2 * in_ref.shape[2] // Z_HI
     for near in range(NEAR):
+        blocks = [in_ref[at * NEAR + near].astype(jnp.float32) for at in range(line)]
+        blocks = [jnp.concatenate([block[:part], block[part:]], axis=1) for block in blocks]
+        block = jnp.concatenate(blocks, axis=0).astype(jnp.bfloat16)
         for far in range(Z_HI):
             start = (far * NEAR + near) * width
-            out_ref[0, :, start : start + width] = in_ref[near, :, far * width : (far + 1) * width]
+            out_ref[0, :, start : start + width] = block[:, far * width : (far + 1) * width]
 
 
 def project(enc_ref, weights_ref, kv_ref):
@@ -59,8 +64,12 @@
 
 
 def spread(dkv_ref, weights_ref, out_ref):
-    near, rows, width = dkv_ref.shape
-    dkv = dkv_ref[...].reshape(near * rows, width)
+    line, piece, width = out_ref.shape
+    near, rows, both = dkv_ref.shape
+    part = rows // line
+    dkv = dkv_ref[...].astype(jnp.float32)
+    dkv = [dkv[:, at * part : (at + 1) * part].reshape(piece, both) for at in range(line)]
+    dkv = jnp.concatenate(dkv, axis=0).astype(jnp.bfloat16)
     out = contract(dkv, weights_ref[...], 1, 1)
     out_ref[...] = out.astype(jnp.bfloat16).reshape(out_ref.shape)
 
@@ -85,10 +94,15 @@
 
 
 def suffix_sums(in_ref, one_ref, two_ref, three_ref, out_ref):
+    line, piece, width = in_ref.shape
+    part = piece // NEAR
+    half = width // 2
     total = one_ref[...].astype(jnp.float32) + two_ref[...].astype(jnp.float32) + three_ref[...].astype(jnp.float32)
-    for step in range(in_ref.shape[0] - 1, -1, -1):
-        total = total + in_ref[step].astype(jnp.float32)
-        out_ref[step] = total.astype(jnp.bfloat16)
+    for at in range(line - 1, -1, -1):
+        total = total + in_ref[at].astype(jnp.float32)
+        left = total[:, :half].reshape(NEAR, part, half)
+        right = total[:, half:].reshape(NEAR, part, half)
+        out_ref[at * NEAR : (at + 1) * NEAR] = jnp.concatenate([left, right], axis=1).astype(jnp.bfloat16)
 
 
 def add_terms(own_ref, *refs):
@@ -146,6 +160,11 @@
     line = sections // Z_LO
     line_groups = [[up * line + step for step in range(line)] for up in range(Z_LO)]
     piece = NEAR * rows // line
+    plane_groups = [
+        [((up * line + at) * Z_HI + far) * NEAR + near for at in range(line) for near in range(NEAR)]
+        for up in range(Z_LO)
+        for far in range(Z_HI)
+    ]
 
     def lowered(array, step):
         pairs = [(up * line + at, (up - step) * line + at) for up in range(step, Z_LO) for at in range(line)]
@@ -167,16 +186,13 @@
     total = call(row_total, [((piece, width), low)], [part])
     above = [lowered(total, step) for step in range(1, Z_LO)]
     above, beyond = lax.optimization_barrier((above, beyond))
-    sums = call(suffix_sums, [((line, piece, width), low)], [part, *above])
-    sums = exchange(sums, "section", line_groups)
-    sums = exchange(sums.reshape(NEAR, rows, width), "dp", near_groups)
+    sums = call(suffix_sums, [((line * NEAR, 2 * piece // NEAR, width // 2), low)], [part, *above])
+    sums = exchange(sums, ("section", "dp"), plane_groups)
     after = call(add_terms, [((depth, both), low)], [after, beyond])
     after = shifted(after, 1)
-    mine = call(add_terms, [((depth, both), high)], [mine, before], flops=30_000_000_000)
-    sums, mine = lax.optimization_barrier((sums, mine))
     enc_grad = call(join_columns, [((1, rows, model), low)], [sums])
-    enc_grad, mine, after = lax.optimization_barrier((enc_grad, mine, after))
-    weight_grad = call(add_terms, [((depth, both), high)], [mine, after])[None]
+    enc_grad, mine, after, before = lax.optimization_barrier((enc_grad, mine, after, before))
+    weight_grad = call(add_terms, [((depth, both), high)], [mine, after, before])[None]
     return enc_grad, weight_grad
 
 

time: 115 us -> 112 us (0.974)
  starting transfers between devices: 44.8 us -> 40.3 us
  waiting for transfers between devices: 17.3 us -> 19.6 us
    ppermute x3, waiting for transfers between devices: 0.01 us -> 9.17 us  [shifted(): return lax.ppermute(array, 'dp', pairs)]
    all_to_all x4 -> x3, waiting for transfers between devices: 8.59 us -> 1.7 us  [exchange(): return lax.all_to_all(array, axis, 0, 0, axis_index_groups=groups)]
    all_to_all x4 -> x3, starting transfers between devices: 26 us -> 21.5 us  [exchange(): return lax.all_to_all(array, axis, 0, 0, axis_index_groups=groups)]
    pallas_call x11 -> x10, Pallas kernels: 5.48 us -> 5.47 us  [call(): pl.pallas_call(kernel, out_shape=outs, in_specs=[smem] * scalars + [vmem]...]
  transfers between devices with their start and end apart: 10 -> 9, of which waited for: 5 -> 7; matrix products, arithmetic and copies ran while one was open for 0% -> 0% of each run, Pallas kernels for 1% -> 1%
where the time goes in v3:
time: 112 us
  blocking collectives  44.5 us (40%)
  starting transfers between devices  40.3 us (36%)
  waiting for transfers between devices  19.6 us (18%)
  Pallas kernels  5.47 us (5%)
    all_gather x1, blocking collectives, shards(): lax.all_gather(own, 'dp', axis=0, tiled=True, axis_index_groups=far_groups)  22.7 us
    all_to_all x2, blocking collectives, exchange(): return lax.all_to_all(array, axis, 0, 0, axis_index_groups=groups)  21.8 us
    all_to_all x3, starting transfers between devices, exchange(): return lax.all_to_all(array, axis, 0, 0, axis_index_groups=groups)  21.5 us
    ppermute x3, starting transfers between devices, shifted(): return lax.ppermute(array, 'dp', pairs)  14.9 us
    ppermute x3, waiting for transfers between devices, shifted(): return lax.ppermute(array, 'dp', pairs)  9.17 us
    ppermute x3, waiting for transfers between devices, lowered(): return lax.ppermute(array, 'section', pairs)  8.71 us
    pallas_call x10, Pallas kernels, call(): pl.pallas_call(kernel, out_shape=outs, in_specs=[smem] * scalars + [vmem]...  5.47 us
    ppermute x3, starting transfers between devices, lowered(): return lax.ppermute(array, 'section', pairs)  3.88 us
  transfers between devices with their start and end apart: 9, of which 7 were waited for; matrix products, arithmetic and copies ran while one was open for 0% of the time, Pallas kernels for 1%

profile of v3, /device:TPU:1, one launch (start us, length us, event | category | flops | bytes accessed | tf_op | source)
XLA Modules:
  0.0 111.6 jit_solution(570734980037449631)
XLA Ops:
  0.6 0.0 copy-start
  0.6 1.0 copy-done
  1.6 0.9 shard_map.59
  2.5 0.0 copy-start.3
  2.5 10.4 %all-to-all-start = ((bf16[8,32,768]{2,1,0:T(8,128)(2,1)}), bf16[8,32,768]{2,1,0:T(8,128)(2,1)S(1)}, u32[]{:S(2)}, u32[]{:S(2)}) async-start(bf16[8,32,768]{2,1,0:T(8,128)(2,1)} %shard_map.59), calls=%async_computation | async-start | bytes 786432 | tf_op jit(solution)/shard_map/all_to_all | solution.py:150
  12.9 0.0 copy-done.3
  12.9 22.7 %all_gather.3.weights_ref = bf16[768,256]{1,0:T(8,128)(2,1)S(1)} all-gather(bf16[192,256]{1,0:T(8,128)(2,1)S(1)} %bitcast.8), channel_id=1, replica_groups={{0,8,16,24},{1,9,17,25},{2,10,18,26},{3,11,19,27},{4,12,20,28},{5,13,21..., dimensions={0}, use_global_device_ids=true | all-gather | bytes 491520 | tf_op jit(solution)/shard_map/all_gather | solution.py:155
  35.6 0.0 all-to-all-done.enc_ref
  35.6 0.3 shard_map.60
  35.8 0.0 copy-start.1
  35.9 0.0 copy-start.2
  35.9 13.1 %all_to_all.25.kv_ref = f32[8,32,256]{2,1,0:T(8,128)S(1)} all-to-all(f32[8,32,256]{2,1,0:T(8,128)S(1)} %shard_map.60), channel_id=1, replica_groups={{0,1,2,3,4,5,6,7},{8,9,10,11,12,13,14,15},{16,17,18,19,20,21,22,23},{24..., dimensions={0} | all-to-all | bytes 524288 | tf_op jit(solution)/shard_map/all_to_all | solution.py:150
  49.0 0.0 copy-done.1
  49.0 0.0 copy-done.2
  49.0 0.4 shard_map.61
  49.4 8.7 %all_to_all.26.dkv_ref = bf16[8,32,256]{2,1,0:T(8,128)(2,1)S(1)} all-to-all(bf16[8,32,256]{2,1,0:T(8,128)(2,1)S(1)} %broadcast_in_dim.4), channel_id=1, replica_groups={{0,1,2,3,4,5,6,7},{8,9,10,11,12,13,14,15},{16,17,18,19,20,21,22,23},{24..., dimensions={0} | all-to-all | bytes 262144 | tf_op jit(solution)/shard_map/all_to_all | solution.py:150
  58.1 1.0 shard_map.62
  59.1 4.0 %all-to-all-start.3 = ((bf16[4,64,768]{2,1,0:T(8,128)(2,1)}), bf16[4,64,768]{2,1,0:T(8,128)(2,1)S(1)}, u32[]{:S(2)}, u32[]{:S(2)}) async-start(bf16[4,64,768]{2,1,0:T(8,128)(2,1)} %shard_map.62), calls=%async_computation.3 | async-start | bytes 786432 | tf_op jit(solution)/shard_map/all_to_all | solution.py:150
  63.1 0.4 shard_map.64
  63.5 5.7 %collective-permute-start.3 = (bf16[192,256]{1,0:T(8,128)(2,1)S(1)}, bf16[192,256]{1,0:T(8,128)(2,1)S(1)}, u32[]{:S(2)}, u32[]{:S(2)}) collective-permute-start(bf16[192,256]{1,0:T(8,128)(2,1)S(1)} %get-tuple-element.22), channel_id=1, source_target_pairs={{0,8},{1,9},{2,10},{3,11},{4,12},{5,13},{6,14},{7,15},{8,16},{9,17... | collective-permute-start | bytes 294920 | tf_op jit(solution)/shard_map/ppermute | solution.py:147
  69.3 0.5 all-to-all-done.3.in_ref
  69.8 0.1 shard_map.63
  69.9 1.3 %collective-permute-start = (bf16[64,768]{1,0:T(8,128)(2,1)S(1)}, bf16[64,768]{1,0:T(8,128)(2,1)S(1)}, u32[]{:S(2)}, u32[]{:S(2)}) collective-permute-start(bf16[64,768]{1,0:T(8,128)(2,1)S(1)} %shard_map.63), channel_id=1, source_target_pairs={{128,0},{160,32},{192,64},{224,96},{256,128},{288,160},{320,192},{... | collective-permute-start | bytes 294920 | tf_op jit(solution)/shard_map/ppermute | solution.py:171
  71.2 1.3 %collective-permute-start.1 = (bf16[64,768]{1,0:T(8,128)(2,1)S(1)}, bf16[64,768]{1,0:T(8,128)(2,1)S(1)}, u32[]{:S(2)}, u32[]{:S(2)}) collective-permute-start(bf16[64,768]{1,0:T(8,128)(2,1)S(1)} %shard_map.63), channel_id=1, source_target_pairs={{256,0},{288,32},{320,64},{352,96},{384,128},{416,160},{448,192},{... | collective-permute-start | bytes 294920 | tf_op jit(solution)/shard_map/ppermute | solution.py:171
  72.5 1.3 %collective-permute-start.2 = (bf16[64,768]{1,0:T(8,128)(2,1)S(1)}, bf16[64,768]{1,0:T(8,128)(2,1)S(1)}, u32[]{:S(2)}, u32[]{:S(2)}) collective-permute-start(bf16[64,768]{1,0:T(8,128)(2,1)S(1)} %shard_map.63), channel_id=1, source_target_pairs={{384,0},{416,32},{448,64},{480,96},{385,1},{417,33},{449,65},{481,... | collective-permute-start | bytes 294920 | tf_op jit(solution)/shard_map/ppermute | solution.py:171
  73.8 0.0 collective-permute-done.3.refs_0_
  73.8 2.6 %collective-permute-done.one_ref = bf16[64,768]{1,0:T(8,128)(2,1)S(1)} collective-permute-done((bf16[64,768]{1,0:T(8,128)(2,1)S(1)}, bf16[64,768]{1,0:T(8,128)(2,1)S(1)}, u32[]{:S(2)}, u32[]{:S(2)}) %collective-permute-start) | collective-permute-done | bytes 98336 | tf_op jit(solution)/shard_map/ppermute | solution.py:171
  76.4 2.3 %collective-permute-done.1.two_ref = bf16[64,768]{1,0:T(8,128)(2,1)S(1)} collective-permute-done((bf16[64,768]{1,0:T(8,128)(2,1)S(1)}, bf16[64,768]{1,0:T(8,128)(2,1)S(1)}, u32[]{:S(2)}, u32[]{:S(2)}) %collective-permute-start.1) | collective-permute-done | bytes 98336 | tf_op jit(solution)/shard_map/ppermute | solution.py:171
  78.7 3.8 %collective-permute-done.2.three_ref = bf16[64,768]{1,0:T(8,128)(2,1)S(1)} collective-permute-done((bf16[64,768]{1,0:T(8,128)(2,1)S(1)}, bf16[64,768]{1,0:T(8,128)(2,1)S(1)}, u32[]{:S(2)}, u32[]{:S(2)}) %collective-permute-start.2) | collective-permute-done | bytes 98336 | tf_op jit(solution)/shard_map/ppermute | solution.py:171
  82.5 0.8 shard_map.65
  83.3 7.1 %all-to-all-start.4 = ((bf16[32,16,384]{2,1,0:T(8,128)(2,1)}), bf16[32,16,384]{2,1,0:T(8,128)(2,1)S(1)}, u32[]{:S(2)}, u32[]{:S(2)}) async-start(bf16[32,16,384]{2,1,0:T(8,128)(2,1)} %shard_map.65), calls=%async_computation.4 | async-start | bytes 786432 | tf_op jit(solution)/shard_map/all_to_all | solution.py:150
  90.5 4.3 %collective-permute-start.5 = (bf16[192,256]{1,0:T(8,128)(2,1)S(1)}, bf16[192,256]{1,0:T(8,128)(2,1)S(1)}, u32[]{:S(2)}, u32[]{:S(2)}) collective-permute-start(bf16[192,256]{1,0:T(8,128)(2,1)S(1)} %get-tuple-element.29), channel_id=1, source_target_pairs={{0,24},{1,25},{2,26},{3,27},{4,28},{5,29},{6,30},{7,31},{8,0},{9,1... | collective-permute-start | bytes 294920 | tf_op jit(solution)/shard_map/ppermute | solution.py:147
  94.7 4.9 %collective-permute-start.4 = (bf16[192,256]{1,0:T(8,128)(2,1)S(1)}, bf16[192,256]{1,0:T(8,128)(2,1)S(1)}, u32[]{:S(2)}, u32[]{:S(2)}) collective-permute-start(bf16[192,256]{1,0:T(8,128)(2,1)S(1)} %shard_map.67), channel_id=1, source_target_pairs={{0,8},{1,9},{2,10},{3,11},{4,12},{5,13},{6,14},{7,15},{8,16},{9,17... | collective-permute-start | bytes 294920 | tf_op jit(solution)/shard_map/ppermute | solution.py:147
  99.7 1.2 %all-to-all-done.4.in_ref = bf16[32,16,384]{2,1,0:T(8,128)(2,1)S(1)} async-done(((bf16[32,16,384]{2,1,0:T(8,128)(2,1)}), bf16[32,16,384]{2,1,0:T(8,128)(2,1)S(1)}, u32[]{:S(2)}, u32[]{:S(2)}) %all-to-all-start.4) | async-done | bytes 393248 | tf_op jit(solution)/shard_map/all_to_all | solution.py:150
  100.9 0.9 shard_map.66
  101.8 3.6 %collective-permute-done.5.refs_1_ = bf16[192,256]{1,0:T(8,128)(2,1)S(1)} collective-permute-done((bf16[192,256]{1,0:T(8,128)(2,1)S(1)}, bf16[192,256]{1,0:T(8,128)(2,1)S(1)}, u32[]{:S(2)}, u32[]{:S(2)}) %collective-permute-start.5) | collective-permute-done | bytes 98336 | tf_op jit(solution)/shard_map/ppermute | solution.py:147
  105.4 5.5 %collective-permute-done.4.refs_0_ = bf16[192,256]{1,0:T(8,128)(2,1)S(1)} collective-permute-done((bf16[192,256]{1,0:T(8,128)(2,1)S(1)}, bf16[192,256]{1,0:T(8,128)(2,1)S(1)}, u32[]{:S(2)}, u32[]{:S(2)}) %collective-permute-start.4) | collective-permute-done | bytes 98336 | tf_op jit(solution)/shard_map/ppermute | solution.py:147
  110.9 0.7 shard_map.68
  (2 shorter events, 0.0 us)
Async XLA Ops:
  0.6 1.0 copy-start
  2.5 10.4 %copy-start.3 = (bf16[1,192,256]{2,1,0:T(8,128)(2,1)S(1)}, bf16[1,192,256]{2,1,0:T(8,128)(2,1)}, u32[]{:S(2)}) copy-start(bf16[1,192,256]{2,1,0:T(8,128)(2,1)} %param.5) | copy-start | bytes 294916
  2.5 33.1 %all-to-all-start = ((bf16[8,32,768]{2,1,0:T(8,128)(2,1)}), bf16[8,32,768]{2,1,0:T(8,128)(2,1)S(1)}, u32[]{:S(2)}, u32[]{:S(2)}) async-start(bf16[8,32,768]{2,1,0:T(8,128)(2,1)} %shard_map.59), calls=%async_computation | async-start | bytes 786432 | tf_op jit(solution)/shard_map/all_to_all | solution.py:150
  35.8 13.1 %copy-start.1 = (bf16[1,512,128]{2,1,0:T(8,128)(2,1)S(1)}, bf16[1,512,128]{2,1,0:T(8,128)(2,1)}, u32[]{:S(2)}) copy-start(bf16[1,512,128]{2,1,0:T(8,128)(2,1)} %param.6) | copy-start | bytes 393220
  35.9 13.1 %copy-start.2 = (bf16[1,512,128]{2,1,0:T(8,128)(2,1)S(1)}, bf16[1,512,128]{2,1,0:T(8,128)(2,1)}, u32[]{:S(2)}) copy-start(bf16[1,512,128]{2,1,0:T(8,128)(2,1)} %param.7) | copy-start | bytes 393220
  59.1 10.7 %all-to-all-start.3 = ((bf16[4,64,768]{2,1,0:T(8,128)(2,1)}), bf16[4,64,768]{2,1,0:T(8,128)(2,1)S(1)}, u32[]{:S(2)}, u32[]{:S(2)}) async-start(bf16[4,64,768]{2,1,0:T(8,128)(2,1)} %shard_map.62), calls=%async_computation.3 | async-start | bytes 786432 | tf_op jit(solution)/shard_map/all_to_all | solution.py:150
  63.5 10.2 %collective-permute-start.3 = (bf16[192,256]{1,0:T(8,128)(2,1)S(1)}, bf16[192,256]{1,0:T(8,128)(2,1)S(1)}, u32[]{:S(2)}, u32[]{:S(2)}) collective-permute-start(bf16[192,256]{1,0:T(8,128)(2,1)S(1)} %get-tuple-element.22), channel_id=1, source_target_pairs={{0,8},{1,9},{2,10},{3,11},{4,12},{5,13},{6,14},{7,15},{8,16},{9,17... | collective-permute-start | bytes 294920 | tf_op jit(solution)/shard_map/ppermute | solution.py:147
  69.9 6.5 %collective-permute-start = (bf16[64,768]{1,0:T(8,128)(2,1)S(1)}, bf16[64,768]{1,0:T(8,128)(2,1)S(1)}, u32[]{:S(2)}, u32[]{:S(2)}) collective-permute-start(bf16[64,768]{1,0:T(8,128)(2,1)S(1)} %shard_map.63), channel_id=1, source_target_pairs={{128,0},{160,32},{192,64},{224,96},{256,128},{288,160},{320,192},{... | collective-permute-start | bytes 294920 | tf_op jit(solution)/shard_map/ppermute | solution.py:171
  71.2 7.5 %collective-permute-start.1 = (bf16[64,768]{1,0:T(8,128)(2,1)S(1)}, bf16[64,768]{1,0:T(8,128)(2,1)S(1)}, u32[]{:S(2)}, u32[]{:S(2)}) collective-permute-start(bf16[64,768]{1,0:T(8,128)(2,1)S(1)} %shard_map.63), channel_id=1, source_target_pairs={{256,0},{288,32},{320,64},{352,96},{384,128},{416,160},{448,192},{... | collective-permute-start | bytes 294920 | tf_op jit(solution)/shard_map/ppermute | solution.py:171
  72.5 10.0 %collective-permute-start.2 = (bf16[64,768]{1,0:T(8,128)(2,1)S(1)}, bf16[64,768]{1,0:T(8,128)(2,1)S(1)}, u32[]{:S(2)}, u32[]{:S(2)}) collective-permute-start(bf16[64,768]{1,0:T(8,128)(2,1)S(1)} %shard_map.63), channel_id=1, source_target_pairs={{384,0},{416,32},{448,64},{480,96},{385,1},{417,33},{449,65},{481,... | collective-permute-start | bytes 294920 | tf_op jit(solution)/shard_map/ppermute | solution.py:171
  83.3 17.6 %all-to-all-start.4 = ((bf16[32,16,384]{2,1,0:T(8,128)(2,1)}), bf16[32,16,384]{2,1,0:T(8,128)(2,1)S(1)}, u32[]{:S(2)}, u32[]{:S(2)}) async-start(bf16[32,16,384]{2,1,0:T(8,128)(2,1)} %shard_map.65), calls=%async_computation.4 | async-start | bytes 786432 | tf_op jit(solution)/shard_map/all_to_all | solution.py:150
  90.5 14.9 %collective-permute-start.5 = (bf16[192,256]{1,0:T(8,128)(2,1)S(1)}, bf16[192,256]{1,0:T(8,128)(2,1)S(1)}, u32[]{:S(2)}, u32[]{:S(2)}) collective-permute-start(bf16[192,256]{1,0:T(8,128)(2,1)S(1)} %get-tuple-element.29), channel_id=1, source_target_pairs={{0,24},{1,25},{2,26},{3,27},{4,28},{5,29},{6,30},{7,31},{8,0},{9,1... | collective-permute-start | bytes 294920 | tf_op jit(solution)/shard_map/ppermute | solution.py:147
  94.7 16.2 %collective-permute-start.4 = (bf16[192,256]{1,0:T(8,128)(2,1)S(1)}, bf16[192,256]{1,0:T(8,128)(2,1)S(1)}, u32[]{:S(2)}, u32[]{:S(2)}) collective-permute-start(bf16[192,256]{1,0:T(8,128)(2,1)S(1)} %shard_map.67), channel_id=1, source_target_pairs={{0,8},{1,9},{2,10},{3,11},{4,12},{5,13},{6,14},{7,15},{8,16},{9,17... | collective-permute-start | bytes 294920 | tf_op jit(solution)/shard_map/ppermute | solution.py:147

commit v4 on v3

--- a/solution.py
+++ b/solution.py
@@ -182,17 +182,18 @@
         scratch=[pltpu.VMEM((Z_HI, depth, both), high)],
     )
     beyond = shifted(beyond, 1)
+    after = shifted(call(add_terms, [((depth, both), low)], [after, beyond]), 1)
     before = shifted(before, 3)
     total = call(row_total, [((piece, width), low)], [part])
     above = [lowered(total, step) for step in range(1, Z_LO)]
     above, beyond = lax.optimization_barrier((above, beyond))
     sums = call(suffix_sums, [((line * NEAR, 2 * piece // NEAR, width // 2), low)], [part, *above])
     sums = exchange(sums, ("section", "dp"), plane_groups)
-    after = call(add_terms, [((depth, both), low)], [after, beyond])
-    after = shifted(after, 1)
+    mine = call(add_terms, [((depth, both), high)], [mine, after], flops=int(8e9))
+    mine = call(add_terms, [((depth, both), high)], [mine, before], flops=int(1e9))
+    sums, mine = lax.optimization_barrier((sums, mine))
     enc_grad = call(join_columns, [((1, rows, model), low)], [sums])
-    enc_grad, mine, after, before = lax.optimization_barrier((enc_grad, mine, after, before))
-    weight_grad = call(add_terms, [((depth, both), high)], [mine, after, before])[None]
+    weight_grad = mine[None]
     return enc_grad, weight_grad
 
 

time: 112 us -> 106 us (0.946)
  the two profiles are of different devices: /device:TPU:1 before, /device:TPU:97 now
where the time goes in v4:
time: 106 us
  blocking collectives  47.7 us (45%)
  starting transfers between devices  35.3 us (33%)
  waiting for transfers between devices  15.5 us (15%)
  Pallas kernels  5.48 us (5%)
    all_gather x1, blocking collectives, shards(): lax.all_gather(own, 'dp', axis=0, tiled=True, axis_index_groups=far_groups)  24 us
    all_to_all x2, blocking collectives, exchange(): return lax.all_to_all(array, axis, 0, 0, axis_index_groups=groups)  23.7 us
    all_to_all x3, starting transfers between devices, exchange(): return lax.all_to_all(array, axis, 0, 0, axis_index_groups=groups)  15.6 us
    ppermute x3, starting transfers between devices, shifted(): return lax.ppermute(array, 'dp', pairs)  13.4 us
    all_to_all x3, waiting for transfers between devices, exchange(): return lax.all_to_all(array, axis, 0, 0, axis_index_groups=groups)  11.6 us
    ppermute x3, starting transfers between devices, lowered(): return lax.ppermute(array, 'section', pairs)  6.29 us
    pallas_call x11, Pallas kernels, call(): pl.pallas_call(kernel, out_shape=outs, in_specs=[smem] * scalars + [vmem]...  5.48 us
    ppermute x3, waiting for transfers between devices, shifted(): return lax.ppermute(array, 'dp', pairs)  3.91 us
  transfers between devices with their start and end apart: 9, of which 3 were waited for; matrix products, arithmetic and copies ran while one was open for 0% of the time, Pallas kernels for 2%

profile of v4, /device:TPU:97, one launch (start us, length us, event | category | flops | bytes accessed | tf_op | source)
XLA Modules:
  0.0 105.8 jit_solution(5333320025155902068)
XLA Ops:
  0.6 0.0 copy-start
  0.6 1.0 copy-done
  1.6 0.9 shard_map.59
  2.5 0.0 copy-start.3
  2.5 5.3 %all-to-all-start = ((bf16[8,32,768]{2,1,0:T(8,128)(2,1)}), bf16[8,32,768]{2,1,0:T(8,128)(2,1)S(1)}, u32[]{:S(2)}, u32[]{:S(2)}) async-start(bf16[8,32,768]{2,1,0:T(8,128)(2,1)} %shard_map.59), calls=%async_computation | async-start | bytes 786432 | tf_op jit(solution)/shard_map/all_to_all | solution.py:150
  7.8 0.0 copy-done.3
  7.8 24.0 %all_gather.3.weights_ref = bf16[768,256]{1,0:T(8,128)(2,1)S(1)} all-gather(bf16[192,256]{1,0:T(8,128)(2,1)S(1)} %bitcast.7), channel_id=1, replica_groups={{0,8,16,24},{1,9,17,25},{2,10,18,26},{3,11,19,27},{4,12,20,28},{5,13,21..., dimensions={0}, use_global_device_ids=true | all-gather | bytes 491520 | tf_op jit(solution)/shard_map/all_gather | solution.py:155
  31.8 0.0 all-to-all-done.enc_ref
  31.8 0.3 shard_map.60
  32.1 0.0 copy-start.1
  32.1 0.0 copy-start.2
  32.1 15.0 %all_to_all.25.kv_ref = f32[8,32,256]{2,1,0:T(8,128)S(1)} all-to-all(f32[8,32,256]{2,1,0:T(8,128)S(1)} %shard_map.60), channel_id=1, replica_groups={{0,1,2,3,4,5,6,7},{8,9,10,11,12,13,14,15},{16,17,18,19,20,21,22,23},{24..., dimensions={0} | all-to-all | bytes 524288 | tf_op jit(solution)/shard_map/all_to_all | solution.py:150
  47.1 0.0 copy-done.1
  47.1 0.0 copy-done.2
  47.1 0.4 shard_map.61
  47.5 8.7 %all_to_all.26.dkv_ref = bf16[8,32,256]{2,1,0:T(8,128)(2,1)S(1)} all-to-all(bf16[8,32,256]{2,1,0:T(8,128)(2,1)S(1)} %broadcast_in_dim.4), channel_id=1, replica_groups={{0,1,2,3,4,5,6,7},{8,9,10,11,12,13,14,15},{16,17,18,19,20,21,22,23},{24..., dimensions={0} | all-to-all | bytes 262144 | tf_op jit(solution)/shard_map/all_to_all | solution.py:150
  56.2 1.0 shard_map.62
  57.2 4.0 %all-to-all-start.3 = ((bf16[4,64,768]{2,1,0:T(8,128)(2,1)}), bf16[4,64,768]{2,1,0:T(8,128)(2,1)S(1)}, u32[]{:S(2)}, u32[]{:S(2)}) async-start(bf16[4,64,768]{2,1,0:T(8,128)(2,1)} %shard_map.62), calls=%async_computation.3 | async-start | bytes 786432 | tf_op jit(solution)/shard_map/all_to_all | solution.py:150
  61.2 0.4 shard_map.64
  61.6 4.2 %collective-permute-start.3 = (bf16[192,256]{1,0:T(8,128)(2,1)S(1)}, bf16[192,256]{1,0:T(8,128)(2,1)S(1)}, u32[]{:S(2)}, u32[]{:S(2)}) collective-permute-start(bf16[192,256]{1,0:T(8,128)(2,1)S(1)} %get-tuple-element.19), channel_id=1, source_target_pairs={{0,8},{1,9},{2,10},{3,11},{4,12},{5,13},{6,14},{7,15},{8,16},{9,17... | collective-permute-start | bytes 294920 | tf_op jit(solution)/shard_map/ppermute | solution.py:147
  65.8 2.0 %all-to-all-done.3.in_ref = bf16[4,64,768]{2,1,0:T(8,128)(2,1)S(1)} async-done(((bf16[4,64,768]{2,1,0:T(8,128)(2,1)}), bf16[4,64,768]{2,1,0:T(8,128)(2,1)S(1)}, u32[]{:S(2)}, u32[]{:S(2)}) %all-to-all-start.3) | async-done | bytes 393248 | tf_op jit(solution)/shard_map/all_to_all | solution.py:150
  67.9 0.1 shard_map.63
  68.0 3.2 %collective-permute-start = (bf16[64,768]{1,0:T(8,128)(2,1)S(1)}, bf16[64,768]{1,0:T(8,128)(2,1)S(1)}, u32[]{:S(2)}, u32[]{:S(2)}) collective-permute-start(bf16[64,768]{1,0:T(8,128)(2,1)S(1)} %shard_map.63), channel_id=1, source_target_pairs={{128,0},{160,32},{192,64},{224,96},{256,128},{288,160},{320,192},{... | collective-permute-start | bytes 294920 | tf_op jit(solution)/shard_map/ppermute | solution.py:171
  71.1 1.8 %collective-permute-start.1 = (bf16[64,768]{1,0:T(8,128)(2,1)S(1)}, bf16[64,768]{1,0:T(8,128)(2,1)S(1)}, u32[]{:S(2)}, u32[]{:S(2)}) collective-permute-start(bf16[64,768]{1,0:T(8,128)(2,1)S(1)} %shard_map.63), channel_id=1, source_target_pairs={{256,0},{288,32},{320,64},{352,96},{384,128},{416,160},{448,192},{... | collective-permute-start | bytes 294920 | tf_op jit(solution)/shard_map/ppermute | solution.py:171
  73.0 1.3 %collective-permute-start.2 = (bf16[64,768]{1,0:T(8,128)(2,1)S(1)}, bf16[64,768]{1,0:T(8,128)(2,1)S(1)}, u32[]{:S(2)}, u32[]{:S(2)}) collective-permute-start(bf16[64,768]{1,0:T(8,128)(2,1)S(1)} %shard_map.63), channel_id=1, source_target_pairs={{384,0},{416,32},{448,64},{480,96},{385,1},{417,33},{449,65},{481,... | collective-permute-start | bytes 294920 | tf_op jit(solution)/shard_map/ppermute | solution.py:171
  74.3 3.9 %collective-permute-done.3.refs_0_ = bf16[192,256]{1,0:T(8,128)(2,1)S(1)} collective-permute-done((bf16[192,256]{1,0:T(8,128)(2,1)S(1)}, bf16[192,256]{1,0:T(8,128)(2,1)S(1)}, u32[]{:S(2)}, u32[]{:S(2)}) %collective-permute-start.3) | collective-permute-done | bytes 98336 | tf_op jit(solution)/shard_map/ppermute | solution.py:147
  78.2 1.9 %collective-permute-start.4 = (bf16[192,256]{1,0:T(8,128)(2,1)S(1)}, bf16[192,256]{1,0:T(8,128)(2,1)S(1)}, u32[]{:S(2)}, u32[]{:S(2)}) collective-permute-start(bf16[192,256]{1,0:T(8,128)(2,1)S(1)} %shard_map.66), channel_id=1, source_target_pairs={{0,8},{1,9},{2,10},{3,11},{4,12},{5,13},{6,14},{7,15},{8,16},{9,17... | collective-permute-start | bytes 294920 | tf_op jit(solution)/shard_map/ppermute | solution.py:147
  80.1 7.3 %collective-permute-start.5 = (bf16[192,256]{1,0:T(8,128)(2,1)S(1)}, bf16[192,256]{1,0:T(8,128)(2,1)S(1)}, u32[]{:S(2)}, u32[]{:S(2)}) collective-permute-start(bf16[192,256]{1,0:T(8,128)(2,1)S(1)} %get-tuple-element.25), channel_id=1, source_target_pairs={{0,24},{1,25},{2,26},{3,27},{4,28},{5,29},{6,30},{7,31},{8,0},{9,1... | collective-permute-start | bytes 294920 | tf_op jit(solution)/shard_map/ppermute | solution.py:147
  87.4 0.0 collective-permute-done.one_ref
  87.4 0.0 collective-permute-done.1.two_ref
  87.4 0.0 collective-permute-done.2.three_ref
  87.4 0.8 shard_map.65
  88.3 6.4 %all-to-all-start.4 = ((bf16[32,16,384]{2,1,0:T(8,128)(2,1)}), bf16[32,16,384]{2,1,0:T(8,128)(2,1)S(1)}, u32[]{:S(2)}, u32[]{:S(2)}) async-start(bf16[32,16,384]{2,1,0:T(8,128)(2,1)} %shard_map.65), calls=%async_computation.4 | async-start | bytes 786432 | tf_op jit(solution)/shard_map/all_to_all | solution.py:150
  94.6 0.0 collective-permute-done.4.refs_0_
  94.7 0.0 collective-permute-done.5.refs_0_
  94.7 0.7 shard_map.68
  95.4 9.6 %all-to-all-done.4.in_ref = bf16[32,16,384]{2,1,0:T(8,128)(2,1)S(1)} async-done(((bf16[32,16,384]{2,1,0:T(8,128)(2,1)}), bf16[32,16,384]{2,1,0:T(8,128)(2,1)S(1)}, u32[]{:S(2)}, u32[]{:S(2)}) %all-to-all-start.4) | async-done | bytes 393248 | tf_op jit(solution)/shard_map/all_to_all | solution.py:150
  104.9 0.9 shard_map.69
  (3 shorter events, 0.1 us)
Async XLA Ops:
  0.6 1.0 copy-start
  2.5 5.3 %copy-start.3 = (bf16[1,192,256]{2,1,0:T(8,128)(2,1)S(1)}, bf16[1,192,256]{2,1,0:T(8,128)(2,1)}, u32[]{:S(2)}) copy-start(bf16[1,192,256]{2,1,0:T(8,128)(2,1)} %param.5) | copy-start | bytes 294916
  2.5 29.3 %all-to-all-start = ((bf16[8,32,768]{2,1,0:T(8,128)(2,1)}), bf16[8,32,768]{2,1,0:T(8,128)(2,1)S(1)}, u32[]{:S(2)}, u32[]{:S(2)}) async-start(bf16[8,32,768]{2,1,0:T(8,128)(2,1)} %shard_map.59), calls=%async_computation | async-start | bytes 786432 | tf_op jit(solution)/shard_map/all_to_all | solution.py:150
  32.1 15.0 %copy-start.1 = (bf16[1,512,128]{2,1,0:T(8,128)(2,1)S(1)}, bf16[1,512,128]{2,1,0:T(8,128)(2,1)}, u32[]{:S(2)}) copy-start(bf16[1,512,128]{2,1,0:T(8,128)(2,1)} %param.6) | copy-start | bytes 393220
  32.1 15.0 %copy-start.2 = (bf16[1,512,128]{2,1,0:T(8,128)(2,1)S(1)}, bf16[1,512,128]{2,1,0:T(8,128)(2,1)}, u32[]{:S(2)}) copy-start(bf16[1,512,128]{2,1,0:T(8,128)(2,1)} %param.7) | copy-start | bytes 393220
  57.2 10.7 %all-to-all-start.3 = ((bf16[4,64,768]{2,1,0:T(8,128)(2,1)}), bf16[4,64,768]{2,1,0:T(8,128)(2,1)S(1)}, u32[]{:S(2)}, u32[]{:S(2)}) async-start(bf16[4,64,768]{2,1,0:T(8,128)(2,1)} %shard_map.62), calls=%async_computation.3 | async-start | bytes 786432 | tf_op jit(solution)/shard_map/all_to_all | solution.py:150
  61.6 16.5 %collective-permute-start.3 = (bf16[192,256]{1,0:T(8,128)(2,1)S(1)}, bf16[192,256]{1,0:T(8,128)(2,1)S(1)}, u32[]{:S(2)}, u32[]{:S(2)}) collective-permute-start(bf16[192,256]{1,0:T(8,128)(2,1)S(1)} %get-tuple-element.19), channel_id=1, source_target_pairs={{0,8},{1,9},{2,10},{3,11},{4,12},{5,13},{6,14},{7,15},{8,16},{9,17... | collective-permute-start | bytes 294920 | tf_op jit(solution)/shard_map/ppermute | solution.py:147
  68.0 19.4 %collective-permute-start = (bf16[64,768]{1,0:T(8,128)(2,1)S(1)}, bf16[64,768]{1,0:T(8,128)(2,1)S(1)}, u32[]{:S(2)}, u32[]{:S(2)}) collective-permute-start(bf16[64,768]{1,0:T(8,128)(2,1)S(1)} %shard_map.63), channel_id=1, source_target_pairs={{128,0},{160,32},{192,64},{224,96},{256,128},{288,160},{320,192},{... | collective-permute-start | bytes 294920 | tf_op jit(solution)/shard_map/ppermute | solution.py:171
  71.1 16.3 %collective-permute-start.1 = (bf16[64,768]{1,0:T(8,128)(2,1)S(1)}, bf16[64,768]{1,0:T(8,128)(2,1)S(1)}, u32[]{:S(2)}, u32[]{:S(2)}) collective-permute-start(bf16[64,768]{1,0:T(8,128)(2,1)S(1)} %shard_map.63), channel_id=1, source_target_pairs={{256,0},{288,32},{320,64},{352,96},{384,128},{416,160},{448,192},{... | collective-permute-start | bytes 294920 | tf_op jit(solution)/shard_map/ppermute | solution.py:171
  73.0 14.5 %collective-permute-start.2 = (bf16[64,768]{1,0:T(8,128)(2,1)S(1)}, bf16[64,768]{1,0:T(8,128)(2,1)S(1)}, u32[]{:S(2)}, u32[]{:S(2)}) collective-permute-start(bf16[64,768]{1,0:T(8,128)(2,1)S(1)} %shard_map.63), channel_id=1, source_target_pairs={{384,0},{416,32},{448,64},{480,96},{385,1},{417,33},{449,65},{481,... | collective-permute-start | bytes 294920 | tf_op jit(solution)/shard_map/ppermute | solution.py:171
  78.2 16.5 %collective-permute-start.4 = (bf16[192,256]{1,0:T(8,128)(2,1)S(1)}, bf16[192,256]{1,0:T(8,128)(2,1)S(1)}, u32[]{:S(2)}, u32[]{:S(2)}) collective-permute-start(bf16[192,256]{1,0:T(8,128)(2,1)S(1)} %shard_map.66), channel_id=1, source_target_pairs={{0,8},{1,9},{2,10},{3,11},{4,12},{5,13},{6,14},{7,15},{8,16},{9,17... | collective-permute-start | bytes 294920 | tf_op jit(solution)/shard_map/ppermute | solution.py:147
  80.1 14.6 %collective-permute-start.5 = (bf16[192,256]{1,0:T(8,128)(2,1)S(1)}, bf16[192,256]{1,0:T(8,128)(2,1)S(1)}, u32[]{:S(2)}, u32[]{:S(2)}) collective-permute-start(bf16[192,256]{1,0:T(8,128)(2,1)S(1)} %get-tuple-element.25), channel_id=1, source_target_pairs={{0,24},{1,25},{2,26},{3,27},{4,28},{5,29},{6,30},{7,31},{8,0},{9,1... | collective-permute-start | bytes 294920 | tf_op jit(solution)/shard_map/ppermute | solution.py:147
  88.3 16.7 %all-to-all-start.4 = ((bf16[32,16,384]{2,1,0:T(8,128)(2,1)}), bf16[32,16,384]{2,1,0:T(8,128)(2,1)S(1)}, u32[]{:S(2)}, u32[]{:S(2)}) async-start(bf16[32,16,384]{2,1,0:T(8,128)(2,1)} %shard_map.65), calls=%async_computation.4 | async-start | bytes 786432 | tf_op jit(solution)/shard_map/all_to_all | solution.py:150

commit v5 on v4

--- a/solution.py
+++ b/solution.py
@@ -133,6 +133,7 @@
     rows, model = enc_out.shape
     depth, both = kv_weight.shape[1:]
     sections = lax.axis_size("section")
+    line = sections // Z_LO
     width = Z_HI * depth
     low, high = jnp.bfloat16, jnp.float32
     near_groups = [[far * NEAR + near for near in range(NEAR)] for far in range(Z_HI)]
@@ -145,6 +146,16 @@
             (far * NEAR + near, (far + step) % Z_HI * NEAR + near) for far in range(Z_HI) for near in range(NEAR)
         ]
         return lax.ppermute(array, "dp", pairs)
+
+    def returned(array, ups):
+        pairs = [
+            ((up * line + at) * Z_HI * NEAR + far * NEAR + near, (up * line + at) * Z_HI * NEAR + (far - 1) % Z_HI * NEAR + near)
+            for up in ups
+            for at in range(line)
+            for far in range(Z_HI)
+            for near in range(NEAR)
+        ]
+        return lax.ppermute(array, ("section", "dp"), pairs)
 
     def exchange(array, axis, groups=None):
         return lax.all_to_all(array, axis, 0, 0, axis_index_groups=groups)
@@ -157,7 +168,6 @@
     kv = exchange(kv, "dp", near_groups)
     dkv = call(attend, [((rows, both), low)], [kv, queries[0], out_grad[0]], flops=8 * rows * queries.size)
     dkv = exchange(jnp.broadcast_to(dkv[None], (NEAR, rows, both)), "dp", near_groups)
-    line = sections // Z_LO
     line_groups = [[up * line + step for step in range(line)] for up in range(Z_LO)]
     piece = NEAR * rows // line
     plane_groups = [
@@ -183,17 +193,17 @@
     )
     beyond = shifted(beyond, 1)
     after = shifted(call(add_terms, [((depth, both), low)], [after, beyond]), 1)
-    before = shifted(before, 3)
+    lower, upper = returned(before, range(Z_LO // 2)), returned(before, range(Z_LO // 2, Z_LO))
     total = call(row_total, [((piece, width), low)], [part])
-    above = [lowered(total, step) for step in range(1, Z_LO)]
+    above = [lowered(total, step) for step in range(Z_LO - 1, 0, -1)]
     above, beyond = lax.optimization_barrier((above, beyond))
     sums = call(suffix_sums, [((line * NEAR, 2 * piece // NEAR, width // 2), low)], [part, *above])
     sums = exchange(sums, ("section", "dp"), plane_groups)
-    mine = call(add_terms, [((depth, both), high)], [mine, after], flops=int(8e9))
-    mine = call(add_terms, [((depth, both), high)], [mine, before], flops=int(1e9))
+    mine = call(add_terms, [((depth, both), high)], [mine, after, upper], flops=int(4e9))
     sums, mine = lax.optimization_barrier((sums, mine))
     enc_grad = call(join_columns, [((1, rows, model), low)], [sums])
-    weight_grad = mine[None]
+    enc_grad, mine, lower = lax.optimization_barrier((enc_grad, mine, lower))
+    weight_grad = call(add_terms, [((depth, both), high)], [mine, lower])[None]
     return enc_grad, weight_grad
 
 

time: 106 us -> 104 us (0.981)
  the two profiles are of different devices: /device:TPU:97 before, /device:TPU:1 now
where the time goes in v5:
time: 104 us; the launch traced here: 102 us
  blocking collectives  44.5 us (43%)
  starting transfers between devices  43.5 us (42%)
  waiting for transfers between devices  6.62 us (6%)
  Pallas kernels  5.49 us (5%)
    all_to_all x3, starting transfers between devices, exchange(): return lax.all_to_all(array, axis, 0, 0, axis_index_groups=groups)  23.2 us
    all_gather x1, blocking collectives, shards(): lax.all_gather(own, 'dp', axis=0, tiled=True, axis_index_groups=far_groups)  22.7 us
    all_to_all x2, blocking collectives, exchange(): return lax.all_to_all(array, axis, 0, 0, axis_index_groups=groups)  21.8 us
    ppermute x2, starting transfers between devices, shifted(): return lax.ppermute(array, 'dp', pairs)  11.5 us
    all_to_all x3, waiting for transfers between devices, exchange(): return lax.all_to_all(array, axis, 0, 0, axis_index_groups=groups)  6.5 us
    pallas_call x11, Pallas kernels, call(): pl.pallas_call(kernel, out_shape=outs, in_specs=[smem] * scalars + [vmem]...  5.49 us
    ppermute x2, starting transfers between devices, returned(): return lax.ppermute(array, ('section', 'dp'), pairs)  4.91 us
    ppermute x3, starting transfers between devices, lowered(): return lax.ppermute(array, 'section', pairs)  3.88 us
  transfers between devices with their start and end apart: 10, of which 3 were waited for; matrix products, arithmetic and copies ran while one was open for 0% of the time, Pallas kernels for 2%

profile of v5, /device:TPU:1, one launch (start us, length us, event | category | flops | bytes accessed | tf_op | source)
XLA Modules:
  0.0 101.9 jit_solution(9357586934479521130)
XLA Ops:
  0.6 0.0 copy-start
  0.6 1.0 copy-done
  1.6 0.9 shard_map.59
  2.5 0.0 copy-start.3
  2.5 10.4 %all-to-all-start = ((bf16[8,32,768]{2,1,0:T(8,128)(2,1)}), bf16[8,32,768]{2,1,0:T(8,128)(2,1)S(1)}, u32[]{:S(2)}, u32[]{:S(2)}) async-start(bf16[8,32,768]{2,1,0:T(8,128)(2,1)} %shard_map.59), calls=%async_computation | async-start | bytes 786432 | tf_op jit(solution)/shard_map/all_to_all | solution.py:161
  12.9 0.0 copy-done.3
  12.9 22.7 %all_gather.3.weights_ref = bf16[768,256]{1,0:T(8,128)(2,1)S(1)} all-gather(bf16[192,256]{1,0:T(8,128)(2,1)S(1)} %bitcast.8), channel_id=1, replica_groups={{0,8,16,24},{1,9,17,25},{2,10,18,26},{3,11,19,27},{4,12,20,28},{5,13,21..., dimensions={0}, use_global_device_ids=true | all-gather | bytes 491520 | tf_op jit(solution)/shard_map/all_gather | solution.py:166
  35.6 0.0 all-to-all-done.enc_ref
  35.6 0.3 shard_map.60
  35.8 0.0 copy-start.1
  35.9 0.0 copy-start.2
  35.9 13.1 %all_to_all.25.kv_ref = f32[8,32,256]{2,1,0:T(8,128)S(1)} all-to-all(f32[8,32,256]{2,1,0:T(8,128)S(1)} %shard_map.60), channel_id=1, replica_groups={{0,1,2,3,4,5,6,7},{8,9,10,11,12,13,14,15},{16,17,18,19,20,21,22,23},{24..., dimensions={0} | all-to-all | bytes 524288 | tf_op jit(solution)/shard_map/all_to_all | solution.py:161
  49.0 0.0 copy-done.1
  49.0 0.0 copy-done.2
  49.0 0.4 shard_map.61
  49.4 8.7 %all_to_all.26.dkv_ref = bf16[8,32,256]{2,1,0:T(8,128)(2,1)S(1)} all-to-all(bf16[8,32,256]{2,1,0:T(8,128)(2,1)S(1)} %broadcast_in_dim.4), channel_id=1, replica_groups={{0,1,2,3,4,5,6,7},{8,9,10,11,12,13,14,15},{16,17,18,19,20,21,22,23},{24..., dimensions={0} | all-to-all | bytes 262144 | tf_op jit(solution)/shard_map/all_to_all | solution.py:161
  58.1 1.0 %shard_map.62 = bf16[4,64,768]{2,1,0:T(8,128)(2,1)} custom-call(bf16[8,32,256]{2,1,0:T(8,128)(2,1)S(1)} %all_to_all.26.dkv_ref, bf16[768,256]{1,0:T(8,128)(2,1)S(1)} %all_gather.3.weights_ref), custom_call_target="tpu_custom_call" | custom-call | flops 100663296 | bytes 917504 | tf_op jit(solution)/shard_map/pallas_call | solution.py:120
  59.1 4.0 %all-to-all-start.3 = ((bf16[4,64,768]{2,1,0:T(8,128)(2,1)}), bf16[4,64,768]{2,1,0:T(8,128)(2,1)S(1)}, u32[]{:S(2)}, u32[]{:S(2)}) async-start(bf16[4,64,768]{2,1,0:T(8,128)(2,1)} %shard_map.62), calls=%async_computation.3 | async-start | bytes 786432 | tf_op jit(solution)/shard_map/all_to_all | solution.py:161
  63.1 0.4 shard_map.64
  63.5 5.7 %collective-permute-start.3 = (bf16[192,256]{1,0:T(8,128)(2,1)S(1)}, bf16[192,256]{1,0:T(8,128)(2,1)S(1)}, u32[]{:S(2)}, u32[]{:S(2)}) collective-permute-start(bf16[192,256]{1,0:T(8,128)(2,1)S(1)} %get-tuple-element.22), channel_id=1, source_target_pairs={{0,8},{1,9},{2,10},{3,11},{4,12},{5,13},{6,14},{7,15},{8,16},{9,17... | collective-permute-start | bytes 294920 | tf_op jit(solution)/shard_map/ppermute | solution.py:148
  69.3 0.5 all-to-all-done.3.in_ref
  69.8 0.1 shard_map.63
  69.9 1.3 %collective-permute-start = (bf16[64,768]{1,0:T(8,128)(2,1)S(1)}, bf16[64,768]{1,0:T(8,128)(2,1)S(1)}, u32[]{:S(2)}, u32[]{:S(2)}) collective-permute-start(bf16[64,768]{1,0:T(8,128)(2,1)S(1)} %shard_map.63), channel_id=1, source_target_pairs={{384,0},{416,32},{448,64},{480,96},{385,1},{417,33},{449,65},{481,... | collective-permute-start | bytes 294920 | tf_op jit(solution)/shard_map/ppermute | solution.py:181
  71.2 1.3 %collective-permute-start.1 = (bf16[64,768]{1,0:T(8,128)(2,1)S(1)}, bf16[64,768]{1,0:T(8,128)(2,1)S(1)}, u32[]{:S(2)}, u32[]{:S(2)}) collective-permute-start(bf16[64,768]{1,0:T(8,128)(2,1)S(1)} %shard_map.63), channel_id=1, source_target_pairs={{256,0},{288,32},{320,64},{352,96},{384,128},{416,160},{448,192},{... | collective-permute-start | bytes 294920 | tf_op jit(solution)/shard_map/ppermute | solution.py:181
  72.5 1.3 %collective-permute-start.2 = (bf16[64,768]{1,0:T(8,128)(2,1)S(1)}, bf16[64,768]{1,0:T(8,128)(2,1)S(1)}, u32[]{:S(2)}, u32[]{:S(2)}) collective-permute-start(bf16[64,768]{1,0:T(8,128)(2,1)S(1)} %shard_map.63), channel_id=1, source_target_pairs={{128,0},{160,32},{192,64},{224,96},{256,128},{288,160},{320,192},{... | collective-permute-start | bytes 294920 | tf_op jit(solution)/shard_map/ppermute | solution.py:181
  73.8 0.7 collective-permute-start.5
  74.4 0.0 collective-permute-done.3.refs_0_
  74.5 5.7 %collective-permute-start.4 = (bf16[192,256]{1,0:T(8,128)(2,1)S(1)}, bf16[192,256]{1,0:T(8,128)(2,1)S(1)}, u32[]{:S(2)}, u32[]{:S(2)}) collective-permute-start(bf16[192,256]{1,0:T(8,128)(2,1)S(1)} %shard_map.66), channel_id=1, source_target_pairs={{0,8},{1,9},{2,10},{3,11},{4,12},{5,13},{6,14},{7,15},{8,16},{9,17... | collective-permute-start | bytes 294920 | tf_op jit(solution)/shard_map/ppermute | solution.py:148
  80.2 0.0 collective-permute-done.one_ref
  80.2 0.1 collective-permute-done.1.two_ref
  80.3 0.0 collective-permute-done.2.three_ref
  80.3 0.8 shard_map.65
  81.2 8.9 %all-to-all-start.4 = ((bf16[32,16,384]{2,1,0:T(8,128)(2,1)}), bf16[32,16,384]{2,1,0:T(8,128)(2,1)S(1)}, u32[]{:S(2)}, u32[]{:S(2)}) async-start(bf16[32,16,384]{2,1,0:T(8,128)(2,1)} %shard_map.65), calls=%async_computation.4 | async-start | bytes 786432 | tf_op jit(solution)/shard_map/all_to_all | solution.py:161
  90.0 4.2 %collective-permute-start.6 = (bf16[192,256]{1,0:T(8,128)(2,1)S(1)}, bf16[192,256]{1,0:T(8,128)(2,1)S(1)}, u32[]{:S(2)}, u32[]{:S(2)}) collective-permute-start(bf16[192,256]{1,0:T(8,128)(2,1)S(1)} %get-tuple-element.28), channel_id=1, source_target_pairs={{0,24},{1,25},{2,26},{3,27},{4,28},{5,29},{6,30},{7,31},{8,0},{9,1... | collective-permute-start | bytes 294920 | tf_op jit(solution)/shard_map/ppermute | solution.py:158
  94.3 0.0 collective-permute-done.5.refs_1_
  94.3 0.0 collective-permute-done.4.refs_0_
  94.4 6.0 %all-to-all-done.4.in_ref = bf16[32,16,384]{2,1,0:T(8,128)(2,1)S(1)} async-done(((bf16[32,16,384]{2,1,0:T(8,128)(2,1)}), bf16[32,16,384]{2,1,0:T(8,128)(2,1)S(1)}, u32[]{:S(2)}, u32[]{:S(2)}) %all-to-all-start.4) | async-done | bytes 393248 | tf_op jit(solution)/shard_map/all_to_all | solution.py:161
  100.4 0.9 shard_map.68
  101.2 0.0 collective-permute-done.6.refs_0_
  101.2 0.7 shard_map.69
  (3 shorter events, 0.1 us)
Async XLA Ops:
  0.6 1.0 copy-start
  2.5 10.4 %copy-start.3 = (bf16[1,192,256]{2,1,0:T(8,128)(2,1)S(1)}, bf16[1,192,256]{2,1,0:T(8,128)(2,1)}, u32[]{:S(2)}) copy-start(bf16[1,192,256]{2,1,0:T(8,128)(2,1)} %param.5) | copy-start | bytes 294916
  2.5 33.1 %all-to-all-start = ((bf16[8,32,768]{2,1,0:T(8,128)(2,1)}), bf16[8,32,768]{2,1,0:T(8,128)(2,1)S(1)}, u32[]{:S(2)}, u32[]{:S(2)}) async-start(bf16[8,32,768]{2,1,0:T(8,128)(2,1)} %shard_map.59), calls=%async_computation | async-start | bytes 786432 | tf_op jit(solution)/shard_map/all_to_all | solution.py:161
  35.8 13.1 %copy-start.1 = (bf16[1,512,128]{2,1,0:T(8,128)(2,1)S(1)}, bf16[1,512,128]{2,1,0:T(8,128)(2,1)}, u32[]{:S(2)}) copy-start(bf16[1,512,128]{2,1,0:T(8,128)(2,1)} %param.6) | copy-start | bytes 393220
  35.9 13.1 %copy-start.2 = (bf16[1,512,128]{2,1,0:T(8,128)(2,1)S(1)}, bf16[1,512,128]{2,1,0:T(8,128)(2,1)}, u32[]{:S(2)}) copy-start(bf16[1,512,128]{2,1,0:T(8,128)(2,1)} %param.7) | copy-start | bytes 393220
  59.1 10.7 %all-to-all-start.3 = ((bf16[4,64,768]{2,1,0:T(8,128)(2,1)}), bf16[4,64,768]{2,1,0:T(8,128)(2,1)S(1)}, u32[]{:S(2)}, u32[]{:S(2)}) async-start(bf16[4,64,768]{2,1,0:T(8,128)(2,1)} %shard_map.62), calls=%async_computation.3 | async-start | bytes 786432 | tf_op jit(solution)/shard_map/all_to_all | solution.py:161
  63.5 10.9 %collective-permute-start.3 = (bf16[192,256]{1,0:T(8,128)(2,1)S(1)}, bf16[192,256]{1,0:T(8,128)(2,1)S(1)}, u32[]{:S(2)}, u32[]{:S(2)}) collective-permute-start(bf16[192,256]{1,0:T(8,128)(2,1)S(1)} %get-tuple-element.22), channel_id=1, source_target_pairs={{0,8},{1,9},{2,10},{3,11},{4,12},{5,13},{6,14},{7,15},{8,16},{9,17... | collective-permute-start | bytes 294920 | tf_op jit(solution)/shard_map/ppermute | solution.py:148
  69.9 10.4 %collective-permute-start = (bf16[64,768]{1,0:T(8,128)(2,1)S(1)}, bf16[64,768]{1,0:T(8,128)(2,1)S(1)}, u32[]{:S(2)}, u32[]{:S(2)}) collective-permute-start(bf16[64,768]{1,0:T(8,128)(2,1)S(1)} %shard_map.63), channel_id=1, source_target_pairs={{384,0},{416,32},{448,64},{480,96},{385,1},{417,33},{449,65},{481,... | collective-permute-start | bytes 294920 | tf_op jit(solution)/shard_map/ppermute | solution.py:181
  71.2 9.2 %collective-permute-start.1 = (bf16[64,768]{1,0:T(8,128)(2,1)S(1)}, bf16[64,768]{1,0:T(8,128)(2,1)S(1)}, u32[]{:S(2)}, u32[]{:S(2)}) collective-permute-start(bf16[64,768]{1,0:T(8,128)(2,1)S(1)} %shard_map.63), channel_id=1, source_target_pairs={{256,0},{288,32},{320,64},{352,96},{384,128},{416,160},{448,192},{... | collective-permute-start | bytes 294920 | tf_op jit(solution)/shard_map/ppermute | solution.py:181
  72.5 7.9 %collective-permute-start.2 = (bf16[64,768]{1,0:T(8,128)(2,1)S(1)}, bf16[64,768]{1,0:T(8,128)(2,1)S(1)}, u32[]{:S(2)}, u32[]{:S(2)}) collective-permute-start(bf16[64,768]{1,0:T(8,128)(2,1)S(1)} %shard_map.63), channel_id=1, source_target_pairs={{128,0},{160,32},{192,64},{224,96},{256,128},{288,160},{320,192},{... | collective-permute-start | bytes 294920 | tf_op jit(solution)/shard_map/ppermute | solution.py:181
  73.8 20.6 %collective-permute-start.5 = (bf16[192,256]{1,0:T(8,128)(2,1)S(1)}, bf16[192,256]{1,0:T(8,128)(2,1)S(1)}, u32[]{:S(2)}, u32[]{:S(2)}) collective-permute-start(bf16[192,256]{1,0:T(8,128)(2,1)S(1)} %get-tuple-element.28), channel_id=1, source_target_pairs={{256,280},{257,281},{258,282},{259,283},{260,284},{261,285},{262,2... | collective-permute-start | bytes 294920 | tf_op jit(solution)/shard_map/ppermute | solution.py:158
  74.5 19.9 %collective-permute-start.4 = (bf16[192,256]{1,0:T(8,128)(2,1)S(1)}, bf16[192,256]{1,0:T(8,128)(2,1)S(1)}, u32[]{:S(2)}, u32[]{:S(2)}) collective-permute-start(bf16[192,256]{1,0:T(8,128)(2,1)S(1)} %shard_map.66), channel_id=1, source_target_pairs={{0,8},{1,9},{2,10},{3,11},{4,12},{5,13},{6,14},{7,15},{8,16},{9,17... | collective-permute-start | bytes 294920 | tf_op jit(solution)/shard_map/ppermute | solution.py:148
  81.2 19.2 %all-to-all-start.4 = ((bf16[32,16,384]{2,1,0:T(8,128)(2,1)}), bf16[32,16,384]{2,1,0:T(8,128)(2,1)S(1)}, u32[]{:S(2)}, u32[]{:S(2)}) async-start(bf16[32,16,384]{2,1,0:T(8,128)(2,1)} %shard_map.65), calls=%async_computation.4 | async-start | bytes 786432 | tf_op jit(solution)/shard_map/all_to_all | solution.py:161
  90.0 11.2 %collective-permute-start.6 = (bf16[192,256]{1,0:T(8,128)(2,1)S(1)}, bf16[192,256]{1,0:T(8,128)(2,1)S(1)}, u32[]{:S(2)}, u32[]{:S(2)}) collective-permute-start(bf16[192,256]{1,0:T(8,128)(2,1)S(1)} %get-tuple-element.28), channel_id=1, source_target_pairs={{0,24},{1,25},{2,26},{3,27},{4,28},{5,29},{6,30},{7,31},{8,0},{9,1... | collective-permute-start | bytes 294920 | tf_op jit(solution)/shard_map/ppermute | solution.py:158

commit v6 on v5

--- a/solution.py
+++ b/solution.py
@@ -195,7 +195,7 @@
     after = shifted(call(add_terms, [((depth, both), low)], [after, beyond]), 1)
     lower, upper = returned(before, range(Z_LO // 2)), returned(before, range(Z_LO // 2, Z_LO))
     total = call(row_total, [((piece, width), low)], [part])
-    above = [lowered(total, step) for step in range(Z_LO - 1, 0, -1)]
+    above = [lowered(total, step) for step in (2,3,1)]
     above, beyond = lax.optimization_barrier((above, beyond))
     sums = call(suffix_sums, [((line * NEAR, 2 * piece // NEAR, width // 2), low)], [part, *above])
     sums = exchange(sums, ("section", "dp"), plane_groups)

time: 104 us -> 103 us (level)
  transfers between devices with their start and end apart: 10 -> 10, of which waited for: 3 -> 2; matrix products, arithmetic and copies ran while one was open for 0% -> 0% of each run, Pallas kernels for 2% -> 2%
where the time goes in v6:
time: 103 us; the launch traced here: 102 us
  blocking collectives  44.5 us (43%)
  starting transfers between devices  42.7 us (41%)
  waiting for transfers between devices  7.41 us (7%)
  Pallas kernels  5.5 us (5%)
    all_to_all x3, starting transfers between devices, exchange(): return lax.all_to_all(array, axis, 0, 0, axis_index_groups=groups)  23.3 us
    all_gather x1, blocking collectives, shards(): lax.all_gather(own, 'dp', axis=0, tiled=True, axis_index_groups=far_groups)  22.7 us
    all_to_all x2, blocking collectives, exchange(): return lax.all_to_all(array, axis, 0, 0, axis_index_groups=groups)  21.8 us
    ppermute x2, starting transfers between devices, shifted(): return lax.ppermute(array, 'dp', pairs)  11.5 us
    all_to_all x3, waiting for transfers between devices, exchange(): return lax.all_to_all(array, axis, 0, 0, axis_index_groups=groups)  7.39 us
    pallas_call x11, Pallas kernels, call(): pl.pallas_call(kernel, out_shape=outs, in_specs=[smem] * scalars + [vmem]...  5.5 us
    ppermute x2, starting transfers between devices, returned(): return lax.ppermute(array, ('section', 'dp'), pairs)  4.03 us
    ppermute x3, starting transfers between devices, lowered(): return lax.ppermute(array, 'section', pairs)  3.88 us
  transfers between devices with their start and end apart: 10, of which 2 were waited for; matrix products, arithmetic and copies ran while one was open for 0% of the time, Pallas kernels for 2%

profile of v6, /device:TPU:1, one launch (start us, length us, event | category | flops | bytes accessed | tf_op | source)
XLA Modules:
  0.0 101.9 jit_solution(6118125414804694185)
XLA Ops:
  0.6 0.0 copy-start
  0.6 1.0 copy-done
  1.6 0.9 shard_map.59
  2.5 0.0 copy-start.3
  2.5 10.4 %all-to-all-start = ((bf16[8,32,768]{2,1,0:T(8,128)(2,1)}), bf16[8,32,768]{2,1,0:T(8,128)(2,1)S(1)}, u32[]{:S(2)}, u32[]{:S(2)}) async-start(bf16[8,32,768]{2,1,0:T(8,128)(2,1)} %shard_map.59), calls=%async_computation | async-start | bytes 786432 | tf_op jit(solution)/shard_map/all_to_all | solution.py:161
  12.9 0.0 copy-done.3
  12.9 22.7 %all_gather.3.weights_ref = bf16[768,256]{1,0:T(8,128)(2,1)S(1)} all-gather(bf16[192,256]{1,0:T(8,128)(2,1)S(1)} %bitcast.8), channel_id=1, replica_groups={{0,8,16,24},{1,9,17,25},{2,10,18,26},{3,11,19,27},{4,12,20,28},{5,13,21..., dimensions={0}, use_global_device_ids=true | all-gather | bytes 491520 | tf_op jit(solution)/shard_map/all_gather | solution.py:166
  35.6 0.0 all-to-all-done.enc_ref
  35.6 0.3 shard_map.60
  35.8 0.0 copy-start.1
  35.9 0.0 copy-start.2
  35.9 13.1 %all_to_all.25.kv_ref = f32[8,32,256]{2,1,0:T(8,128)S(1)} all-to-all(f32[8,32,256]{2,1,0:T(8,128)S(1)} %shard_map.60), channel_id=1, replica_groups={{0,1,2,3,4,5,6,7},{8,9,10,11,12,13,14,15},{16,17,18,19,20,21,22,23},{24..., dimensions={0} | all-to-all | bytes 524288 | tf_op jit(solution)/shard_map/all_to_all | solution.py:161
  49.0 0.0 copy-done.1
  49.0 0.0 copy-done.2
  49.0 0.4 shard_map.61
  49.4 8.7 %all_to_all.26.dkv_ref = bf16[8,32,256]{2,1,0:T(8,128)(2,1)S(1)} all-to-all(bf16[8,32,256]{2,1,0:T(8,128)(2,1)S(1)} %broadcast_in_dim.4), channel_id=1, replica_groups={{0,1,2,3,4,5,6,7},{8,9,10,11,12,13,14,15},{16,17,18,19,20,21,22,23},{24..., dimensions={0} | all-to-all | bytes 262144 | tf_op jit(solution)/shard_map/all_to_all | solution.py:161
  58.1 1.0 %shard_map.62 = bf16[4,64,768]{2,1,0:T(8,128)(2,1)} custom-call(bf16[8,32,256]{2,1,0:T(8,128)(2,1)S(1)} %all_to_all.26.dkv_ref, bf16[768,256]{1,0:T(8,128)(2,1)S(1)} %all_gather.3.weights_ref), custom_call_target="tpu_custom_call" | custom-call | flops 100663296 | bytes 917504 | tf_op jit(solution)/shard_map/pallas_call | solution.py:120
  59.1 4.0 %all-to-all-start.3 = ((bf16[4,64,768]{2,1,0:T(8,128)(2,1)}), bf16[4,64,768]{2,1,0:T(8,128)(2,1)S(1)}, u32[]{:S(2)}, u32[]{:S(2)}) async-start(bf16[4,64,768]{2,1,0:T(8,128)(2,1)} %shard_map.62), calls=%async_computation.3 | async-start | bytes 786432 | tf_op jit(solution)/shard_map/all_to_all | solution.py:161
  63.1 0.4 shard_map.64
  63.5 5.7 %collective-permute-start.3 = (bf16[192,256]{1,0:T(8,128)(2,1)S(1)}, bf16[192,256]{1,0:T(8,128)(2,1)S(1)}, u32[]{:S(2)}, u32[]{:S(2)}) collective-permute-start(bf16[192,256]{1,0:T(8,128)(2,1)S(1)} %get-tuple-element.22), channel_id=1, source_target_pairs={{0,8},{1,9},{2,10},{3,11},{4,12},{5,13},{6,14},{7,15},{8,16},{9,17... | collective-permute-start | bytes 294920 | tf_op jit(solution)/shard_map/ppermute | solution.py:148
  69.3 0.5 all-to-all-done.3.in_ref
  69.8 0.1 shard_map.63
  69.9 1.3 %collective-permute-start = (bf16[64,768]{1,0:T(8,128)(2,1)S(1)}, bf16[64,768]{1,0:T(8,128)(2,1)S(1)}, u32[]{:S(2)}, u32[]{:S(2)}) collective-permute-start(bf16[64,768]{1,0:T(8,128)(2,1)S(1)} %shard_map.63), channel_id=1, source_target_pairs={{256,0},{288,32},{320,64},{352,96},{384,128},{416,160},{448,192},{... | collective-permute-start | bytes 294920 | tf_op jit(solution)/shard_map/ppermute | solution.py:181
  71.2 1.3 %collective-permute-start.1 = (bf16[64,768]{1,0:T(8,128)(2,1)S(1)}, bf16[64,768]{1,0:T(8,128)(2,1)S(1)}, u32[]{:S(2)}, u32[]{:S(2)}) collective-permute-start(bf16[64,768]{1,0:T(8,128)(2,1)S(1)} %shard_map.63), channel_id=1, source_target_pairs={{384,0},{416,32},{448,64},{480,96},{385,1},{417,33},{449,65},{481,... | collective-permute-start | bytes 294920 | tf_op jit(solution)/shard_map/ppermute | solution.py:181
  72.5 1.3 %collective-permute-start.2 = (bf16[64,768]{1,0:T(8,128)(2,1)S(1)}, bf16[64,768]{1,0:T(8,128)(2,1)S(1)}, u32[]{:S(2)}, u32[]{:S(2)}) collective-permute-start(bf16[64,768]{1,0:T(8,128)(2,1)S(1)} %shard_map.63), channel_id=1, source_target_pairs={{128,0},{160,32},{192,64},{224,96},{256,128},{288,160},{320,192},{... | collective-permute-start | bytes 294920 | tf_op jit(solution)/shard_map/ppermute | solution.py:181
  73.8 0.7 collective-permute-start.5
  74.4 0.0 collective-permute-done.3.refs_0_
  74.5 5.7 %collective-permute-start.4 = (bf16[192,256]{1,0:T(8,128)(2,1)S(1)}, bf16[192,256]{1,0:T(8,128)(2,1)S(1)}, u32[]{:S(2)}, u32[]{:S(2)}) collective-permute-start(bf16[192,256]{1,0:T(8,128)(2,1)S(1)} %shard_map.66), channel_id=1, source_target_pairs={{0,8},{1,9},{2,10},{3,11},{4,12},{5,13},{6,14},{7,15},{8,16},{9,17... | collective-permute-start | bytes 294920 | tf_op jit(solution)/shard_map/ppermute | solution.py:148
  80.2 0.0 collective-permute-done.one_ref
  80.2 0.0 collective-permute-done.1.two_ref
  80.2 0.0 collective-permute-done.2.three_ref
  80.2 0.8 shard_map.65
  81.1 8.9 %all-to-all-start.4 = ((bf16[32,16,384]{2,1,0:T(8,128)(2,1)}), bf16[32,16,384]{2,1,0:T(8,128)(2,1)S(1)}, u32[]{:S(2)}, u32[]{:S(2)}) async-start(bf16[32,16,384]{2,1,0:T(8,128)(2,1)} %shard_map.65), calls=%async_computation.4 | async-start | bytes 786432 | tf_op jit(solution)/shard_map/all_to_all | solution.py:161
  90.0 3.4 %collective-permute-start.6 = (bf16[192,256]{1,0:T(8,128)(2,1)S(1)}, bf16[192,256]{1,0:T(8,128)(2,1)S(1)}, u32[]{:S(2)}, u32[]{:S(2)}) collective-permute-start(bf16[192,256]{1,0:T(8,128)(2,1)S(1)} %get-tuple-element.28), channel_id=1, source_target_pairs={{0,24},{1,25},{2,26},{3,27},{4,28},{5,29},{6,30},{7,31},{8,0},{9,1... | collective-permute-start | bytes 294920 | tf_op jit(solution)/shard_map/ppermute | solution.py:158
  93.4 0.0 collective-permute-done.5.refs_1_
  93.4 0.0 collective-permute-done.4.refs_0_
  93.5 6.9 %all-to-all-done.4.in_ref = bf16[32,16,384]{2,1,0:T(8,128)(2,1)S(1)} async-done(((bf16[32,16,384]{2,1,0:T(8,128)(2,1)}), bf16[32,16,384]{2,1,0:T(8,128)(2,1)S(1)}, u32[]{:S(2)}, u32[]{:S(2)}) %all-to-all-start.4) | async-done | bytes 393248 | tf_op jit(solution)/shard_map/all_to_all | solution.py:161
  100.4 0.9 shard_map.68
  101.2 0.0 collective-permute-done.6.refs_0_
  101.2 0.7 shard_map.69
  (3 shorter events, 0.1 us)
Async XLA Ops:
  0.6 1.0 copy-start
  2.5 10.4 %copy-start.3 = (bf16[1,192,256]{2,1,0:T(8,128)(2,1)S(1)}, bf16[1,192,256]{2,1,0:T(8,128)(2,1)}, u32[]{:S(2)}) copy-start(bf16[1,192,256]{2,1,0:T(8,128)(2,1)} %param.5) | copy-start | bytes 294916
  2.5 33.1 %all-to-all-start = ((bf16[8,32,768]{2,1,0:T(8,128)(2,1)}), bf16[8,32,768]{2,1,0:T(8,128)(2,1)S(1)}, u32[]{:S(2)}, u32[]{:S(2)}) async-start(bf16[8,32,768]{2,1,0:T(8,128)(2,1)} %shard_map.59), calls=%async_computation | async-start | bytes 786432 | tf_op jit(solution)/shard_map/all_to_all | solution.py:161
  35.8 13.1 %copy-start.1 = (bf16[1,512,128]{2,1,0:T(8,128)(2,1)S(1)}, bf16[1,512,128]{2,1,0:T(8,128)(2,1)}, u32[]{:S(2)}) copy-start(bf16[1,512,128]{2,1,0:T(8,128)(2,1)} %param.6) | copy-start | bytes 393220
  35.9 13.1 %copy-start.2 = (bf16[1,512,128]{2,1,0:T(8,128)(2,1)S(1)}, bf16[1,512,128]{2,1,0:T(8,128)(2,1)}, u32[]{:S(2)}) copy-start(bf16[1,512,128]{2,1,0:T(8,128)(2,1)} %param.7) | copy-start | bytes 393220
  59.1 10.7 %all-to-all-start.3 = ((bf16[4,64,768]{2,1,0:T(8,128)(2,1)}), bf16[4,64,768]{2,1,0:T(8,128)(2,1)S(1)}, u32[]{:S(2)}, u32[]{:S(2)}) async-start(bf16[4,64,768]{2,1,0:T(8,128)(2,1)} %shard_map.62), calls=%async_computation.3 | async-start | bytes 786432 | tf_op jit(solution)/shard_map/all_to_all | solution.py:161
  63.5 10.9 %collective-permute-start.3 = (bf16[192,256]{1,0:T(8,128)(2,1)S(1)}, bf16[192,256]{1,0:T(8,128)(2,1)S(1)}, u32[]{:S(2)}, u32[]{:S(2)}) collective-permute-start(bf16[192,256]{1,0:T(8,128)(2,1)S(1)} %get-tuple-element.22), channel_id=1, source_target_pairs={{0,8},{1,9},{2,10},{3,11},{4,12},{5,13},{6,14},{7,15},{8,16},{9,17... | collective-permute-start | bytes 294920 | tf_op jit(solution)/shard_map/ppermute | solution.py:148
  69.9 10.4 %collective-permute-start = (bf16[64,768]{1,0:T(8,128)(2,1)S(1)}, bf16[64,768]{1,0:T(8,128)(2,1)S(1)}, u32[]{:S(2)}, u32[]{:S(2)}) collective-permute-start(bf16[64,768]{1,0:T(8,128)(2,1)S(1)} %shard_map.63), channel_id=1, source_target_pairs={{256,0},{288,32},{320,64},{352,96},{384,128},{416,160},{448,192},{... | collective-permute-start | bytes 294920 | tf_op jit(solution)/shard_map/ppermute | solution.py:181
  71.2 9.1 %collective-permute-start.1 = (bf16[64,768]{1,0:T(8,128)(2,1)S(1)}, bf16[64,768]{1,0:T(8,128)(2,1)S(1)}, u32[]{:S(2)}, u32[]{:S(2)}) collective-permute-start(bf16[64,768]{1,0:T(8,128)(2,1)S(1)} %shard_map.63), channel_id=1, source_target_pairs={{384,0},{416,32},{448,64},{480,96},{385,1},{417,33},{449,65},{481,... | collective-permute-start | bytes 294920 | tf_op jit(solution)/shard_map/ppermute | solution.py:181
  72.5 7.8 %collective-permute-start.2 = (bf16[64,768]{1,0:T(8,128)(2,1)S(1)}, bf16[64,768]{1,0:T(8,128)(2,1)S(1)}, u32[]{:S(2)}, u32[]{:S(2)}) collective-permute-start(bf16[64,768]{1,0:T(8,128)(2,1)S(1)} %shard_map.63), channel_id=1, source_target_pairs={{128,0},{160,32},{192,64},{224,96},{256,128},{288,160},{320,192},{... | collective-permute-start | bytes 294920 | tf_op jit(solution)/shard_map/ppermute | solution.py:181
  73.8 19.7 %collective-permute-start.5 = (bf16[192,256]{1,0:T(8,128)(2,1)S(1)}, bf16[192,256]{1,0:T(8,128)(2,1)S(1)}, u32[]{:S(2)}, u32[]{:S(2)}) collective-permute-start(bf16[192,256]{1,0:T(8,128)(2,1)S(1)} %get-tuple-element.28), channel_id=1, source_target_pairs={{256,280},{257,281},{258,282},{259,283},{260,284},{261,285},{262,2... | collective-permute-start | bytes 294920 | tf_op jit(solution)/shard_map/ppermute | solution.py:158
  74.5 19.0 %collective-permute-start.4 = (bf16[192,256]{1,0:T(8,128)(2,1)S(1)}, bf16[192,256]{1,0:T(8,128)(2,1)S(1)}, u32[]{:S(2)}, u32[]{:S(2)}) collective-permute-start(bf16[192,256]{1,0:T(8,128)(2,1)S(1)} %shard_map.66), channel_id=1, source_target_pairs={{0,8},{1,9},{2,10},{3,11},{4,12},{5,13},{6,14},{7,15},{8,16},{9,17... | collective-permute-start | bytes 294920 | tf_op jit(solution)/shard_map/ppermute | solution.py:148
  81.1 19.3 %all-to-all-start.4 = ((bf16[32,16,384]{2,1,0:T(8,128)(2,1)}), bf16[32,16,384]{2,1,0:T(8,128)(2,1)S(1)}, u32[]{:S(2)}, u32[]{:S(2)}) async-start(bf16[32,16,384]{2,1,0:T(8,128)(2,1)} %shard_map.65), calls=%async_computation.4 | async-start | bytes 786432 | tf_op jit(solution)/shard_map/all_to_all | solution.py:161
  90.0 11.2 %collective-permute-start.6 = (bf16[192,256]{1,0:T(8,128)(2,1)S(1)}, bf16[192,256]{1,0:T(8,128)(2,1)S(1)}, u32[]{:S(2)}, u32[]{:S(2)}) collective-permute-start(bf16[192,256]{1,0:T(8,128)(2,1)S(1)} %get-tuple-element.28), channel_id=1, source_target_pairs={{0,24},{1,25},{2,26},{3,27},{4,28},{5,29},{6,30},{7,31},{8,0},{9,1... | collective-permute-start | bytes 294920 | tf_op jit(solution)/shard_map/ppermute | solution.py:158

commit v7 on v6

--- a/solution.py
+++ b/solution.py
@@ -112,6 +112,11 @@
     refs[-1][...] = total.astype(refs[-1].dtype)
 
 
+def finish(sums_ref, own_ref, lower_ref, last_ref, enc_grad_ref, weight_grad_ref):
+    join_columns(sums_ref, enc_grad_ref)
+    weight_grad_ref[0] = own_ref[...] + lower_ref[...].astype(jnp.float32) + last_ref[...].astype(jnp.float32)
+
+
 def call(kernel, outs, args, flops=0, scalars=0, scratch=()):
     outs = [jax.ShapeDtypeStruct(shape, dtype) for shape, dtype in outs]
     vmem = pl.BlockSpec(memory_space=pltpu.VMEM)
@@ -147,13 +152,17 @@
         ]
         return lax.ppermute(array, "dp", pairs)
 
-    def returned(array, ups):
+    def passed(array, way, chosen):
         pairs = [
-            ((up * line + at) * Z_HI * NEAR + far * NEAR + near, (up * line + at) * Z_HI * NEAR + (far - 1) % Z_HI * NEAR + near)
-            for up in ups
+            (
+                ((up * line + at) * Z_HI + far) * NEAR + near,
+                ((up * line + at) * Z_HI + (far + way) % Z_HI) * NEAR + near,
+            )
+            for up in range(Z_LO)
             for at in range(line)
             for far in range(Z_HI)
             for near in range(NEAR)
+            if (up, near % 2) in chosen
         ]
         return lax.ppermute(array, ("section", "dp"), pairs)
 
@@ -192,18 +201,21 @@
         scratch=[pltpu.VMEM((Z_HI, depth, both), high)],
     )
     beyond = shifted(beyond, 1)
-    after = shifted(call(add_terms, [((depth, both), low)], [after, beyond]), 1)
-    lower, upper = returned(before, range(Z_LO // 2)), returned(before, range(Z_LO // 2, Z_LO))
+    after = call(add_terms, [((depth, both), low)], [after, beyond])
+    late = [(3, 0), (3, 1)]
+    after, last = passed(after, 1, [(up, core) for up in range(3) for core in range(2)]), passed(after, 1, late)
+    early = [(1, 1), (2, 0), (2, 1), (3, 0), (3, 1)]
+    lower, upper = passed(before, -1, [(0, 0), (0, 1), (1, 0)]), passed(before, -1, early)
     total = call(row_total, [((piece, width), low)], [part])
-    above = [lowered(total, step) for step in (2,3,1)]
+    above = [lowered(total, step) for step in (3,2,1)]
     above, beyond = lax.optimization_barrier((above, beyond))
     sums = call(suffix_sums, [((line * NEAR, 2 * piece // NEAR, width // 2), low)], [part, *above])
     sums = exchange(sums, ("section", "dp"), plane_groups)
     mine = call(add_terms, [((depth, both), high)], [mine, after, upper], flops=int(4e9))
     sums, mine = lax.optimization_barrier((sums, mine))
-    enc_grad = call(join_columns, [((1, rows, model), low)], [sums])
-    enc_grad, mine, lower = lax.optimization_barrier((enc_grad, mine, lower))
-    weight_grad = call(add_terms, [((depth, both), high)], [mine, lower])[None]
+    enc_grad, weight_grad = call(
+        finish, [((1, rows, model), low), ((1, depth, both), high)], [sums, mine, lower, last]
+    )
     return enc_grad, weight_grad
 
 

time: 103 us -> 104 us (level)
  the two profiles are of different devices: /device:TPU:1 before, /device:TPU:33 now
where the time goes in v7:
time: 104 us; the launch traced here: 103 us
  blocking collectives  49.5 us (48%)
  starting transfers between devices  36.5 us (35%)
  waiting for transfers between devices  10.5 us (10%)
  Pallas kernels  4.85 us (5%)
    all_gather x1, blocking collectives, shards(): lax.all_gather(own, 'dp', axis=0, tiled=True, axis_index_groups=far_groups)  26 us
    all_to_all x2, blocking collectives, exchange(): return lax.all_to_all(array, axis, 0, 0, axis_index_groups=groups)  23.5 us
    all_to_all x3, starting transfers between devices, exchange(): return lax.all_to_all(array, axis, 0, 0, axis_index_groups=groups)  17.4 us
    ppermute x4, starting transfers between devices, passed(): return lax.ppermute(array, ('section', 'dp'), pairs)  10.5 us
    all_to_all x3, waiting for transfers between devices, exchange(): return lax.all_to_all(array, axis, 0, 0, axis_index_groups=groups)  10.5 us
    pallas_call x10, Pallas kernels, call(): pl.pallas_call(kernel, out_shape=outs, in_specs=[smem] * scalars + [vmem]...  4.85 us
    ppermute x1, starting transfers between devices, shifted(): return lax.ppermute(array, 'dp', pairs)  4.63 us
    ppermute x3, starting transfers between devices, lowered(): return lax.ppermute(array, 'section', pairs)  3.88 us
  transfers between devices with their start and end apart: 11, of which 2 were waited for; matrix products, arithmetic and copies ran while one was open for 0% of the time, Pallas kernels for 1%

profile of v7, /device:TPU:33, one launch (start us, length us, event | category | flops | bytes accessed | tf_op | source)
XLA Modules:
  0.0 103.2 jit_solution(14425354294796088763)
XLA Ops:
  0.6 0.0 copy-start
  0.6 1.0 copy-done
  1.6 0.9 shard_map.59
  2.5 0.0 copy-start.3
  2.5 5.3 %all-to-all-start = ((bf16[8,32,768]{2,1,0:T(8,128)(2,1)}), bf16[8,32,768]{2,1,0:T(8,128)(2,1)S(1)}, u32[]{:S(2)}, u32[]{:S(2)}) async-start(bf16[8,32,768]{2,1,0:T(8,128)(2,1)} %shard_map.59), calls=%async_computation | async-start | bytes 786432 | tf_op jit(solution)/shard_map/all_to_all | solution.py:170
  7.8 0.0 copy-done.3
  7.8 26.0 %all_gather.3.weights_ref = bf16[768,256]{1,0:T(8,128)(2,1)S(1)} all-gather(bf16[192,256]{1,0:T(8,128)(2,1)S(1)} %bitcast.6), channel_id=1, replica_groups={{0,8,16,24},{1,9,17,25},{2,10,18,26},{3,11,19,27},{4,12,20,28},{5,13,21..., dimensions={0}, use_global_device_ids=true | all-gather | bytes 491520 | tf_op jit(solution)/shard_map/all_gather | solution.py:175
  33.8 0.0 all-to-all-done.enc_ref
  33.8 0.3 shard_map.60
  34.1 0.0 copy-start.1
  34.1 0.0 copy-start.2
  34.1 14.8 %all_to_all.25.kv_ref = f32[8,32,256]{2,1,0:T(8,128)S(1)} all-to-all(f32[8,32,256]{2,1,0:T(8,128)S(1)} %shard_map.60), channel_id=1, replica_groups={{0,1,2,3,4,5,6,7},{8,9,10,11,12,13,14,15},{16,17,18,19,20,21,22,23},{24..., dimensions={0} | all-to-all | bytes 524288 | tf_op jit(solution)/shard_map/all_to_all | solution.py:170
  48.9 0.0 copy-done.1
  48.9 0.0 copy-done.2
  48.9 0.4 shard_map.61
  49.3 8.7 %all_to_all.26.dkv_ref = bf16[8,32,256]{2,1,0:T(8,128)(2,1)S(1)} all-to-all(bf16[8,32,256]{2,1,0:T(8,128)(2,1)S(1)} %broadcast_in_dim.2), channel_id=1, replica_groups={{0,1,2,3,4,5,6,7},{8,9,10,11,12,13,14,15},{16,17,18,19,20,21,22,23},{24..., dimensions={0} | all-to-all | bytes 262144 | tf_op jit(solution)/shard_map/all_to_all | solution.py:170
  58.0 1.0 %shard_map.62 = bf16[4,64,768]{2,1,0:T(8,128)(2,1)} custom-call(bf16[8,32,256]{2,1,0:T(8,128)(2,1)S(1)} %all_to_all.26.dkv_ref, bf16[768,256]{1,0:T(8,128)(2,1)S(1)} %all_gather.3.weights_ref), custom_call_target="tpu_custom_call" | custom-call | flops 100663296 | bytes 917504 | tf_op jit(solution)/shard_map/pallas_call | solution.py:125
  59.0 4.0 %all-to-all-start.3 = ((bf16[4,64,768]{2,1,0:T(8,128)(2,1)}), bf16[4,64,768]{2,1,0:T(8,128)(2,1)S(1)}, u32[]{:S(2)}, u32[]{:S(2)}) async-start(bf16[4,64,768]{2,1,0:T(8,128)(2,1)} %shard_map.62), calls=%async_computation.3 | async-start | bytes 786432 | tf_op jit(solution)/shard_map/all_to_all | solution.py:170
  63.0 0.4 shard_map.64
  63.4 4.6 %collective-permute-start.3 = (bf16[192,256]{1,0:T(8,128)(2,1)S(1)}, bf16[192,256]{1,0:T(8,128)(2,1)S(1)}, u32[]{:S(2)}, u32[]{:S(2)}) collective-permute-start(bf16[192,256]{1,0:T(8,128)(2,1)S(1)} %get-tuple-element.19), channel_id=1, source_target_pairs={{0,8},{1,9},{2,10},{3,11},{4,12},{5,13},{6,14},{7,15},{8,16},{9,17... | collective-permute-start | bytes 294920 | tf_op jit(solution)/shard_map/ppermute | solution.py:153
  68.1 1.6 %all-to-all-done.3.in_ref = bf16[4,64,768]{2,1,0:T(8,128)(2,1)S(1)} async-done(((bf16[4,64,768]{2,1,0:T(8,128)(2,1)}), bf16[4,64,768]{2,1,0:T(8,128)(2,1)S(1)}, u32[]{:S(2)}, u32[]{:S(2)}) %all-to-all-start.3) | async-done | bytes 393248 | tf_op jit(solution)/shard_map/all_to_all | solution.py:170
  69.7 0.1 shard_map.63
  69.7 0.7 collective-permute-start
  70.4 1.3 %collective-permute-start.1 = (bf16[64,768]{1,0:T(8,128)(2,1)S(1)}, bf16[64,768]{1,0:T(8,128)(2,1)S(1)}, u32[]{:S(2)}, u32[]{:S(2)}) collective-permute-start(bf16[64,768]{1,0:T(8,128)(2,1)S(1)} %shard_map.63), channel_id=1, source_target_pairs={{256,0},{288,32},{320,64},{352,96},{384,128},{416,160},{448,192},{... | collective-permute-start | bytes 294920 | tf_op jit(solution)/shard_map/ppermute | solution.py:190
  71.7 1.9 %collective-permute-start.2 = (bf16[64,768]{1,0:T(8,128)(2,1)S(1)}, bf16[64,768]{1,0:T(8,128)(2,1)S(1)}, u32[]{:S(2)}, u32[]{:S(2)}) collective-permute-start(bf16[64,768]{1,0:T(8,128)(2,1)S(1)} %shard_map.63), channel_id=1, source_target_pairs={{128,0},{160,32},{192,64},{224,96},{256,128},{288,160},{320,192},{... | collective-permute-start | bytes 294920 | tf_op jit(solution)/shard_map/ppermute | solution.py:190
  73.6 5.5 %collective-permute-start.5 = (bf16[192,256]{1,0:T(8,128)(2,1)S(1)}, bf16[192,256]{1,0:T(8,128)(2,1)S(1)}, u32[]{:S(2)}, u32[]{:S(2)}) collective-permute-start(bf16[192,256]{1,0:T(8,128)(2,1)S(1)} %get-tuple-element.25), channel_id=1, source_target_pairs={{129,153},{131,155},{133,157},{135,159},{137,129},{139,131},{141,1... | collective-permute-start | bytes 294920 | tf_op jit(solution)/shard_map/ppermute | solution.py:167
  79.1 0.0 collective-permute-done.3.refs_0_
  79.1 3.7 %collective-permute-start.4 = (bf16[192,256]{1,0:T(8,128)(2,1)S(1)}, bf16[192,256]{1,0:T(8,128)(2,1)S(1)}, u32[]{:S(2)}, u32[]{:S(2)}) collective-permute-start(bf16[192,256]{1,0:T(8,128)(2,1)S(1)} %shard_map.66), channel_id=1, source_target_pairs={{0,8},{1,9},{2,10},{3,11},{4,12},{5,13},{6,14},{7,15},{8,16},{9,17... | collective-permute-start | bytes 294920 | tf_op jit(solution)/shard_map/ppermute | solution.py:167
  82.9 0.0 collective-permute-done.one_ref
  82.9 0.0 collective-permute-done.1.two_ref
  82.9 0.0 collective-permute-done.2.three_ref
  82.9 0.8 shard_map.65
  83.8 8.2 %all-to-all-start.4 = ((bf16[32,16,384]{2,1,0:T(8,128)(2,1)}), bf16[32,16,384]{2,1,0:T(8,128)(2,1)S(1)}, u32[]{:S(2)}, u32[]{:S(2)}) async-start(bf16[32,16,384]{2,1,0:T(8,128)(2,1)} %shard_map.65), calls=%async_computation.4 | async-start | bytes 786432 | tf_op jit(solution)/shard_map/all_to_all | solution.py:170
  91.9 0.7 collective-permute-start.6
  92.6 0.7 collective-permute-start.7
  93.3 0.0 collective-permute-done.5.refs_1_
  93.3 0.0 collective-permute-done.4.refs_0_
  93.3 8.9 %all-to-all-done.4.sums_ref = bf16[32,16,384]{2,1,0:T(8,128)(2,1)S(1)} async-done(((bf16[32,16,384]{2,1,0:T(8,128)(2,1)}), bf16[32,16,384]{2,1,0:T(8,128)(2,1)S(1)}, u32[]{:S(2)}, u32[]{:S(2)}) %all-to-all-start.4) | async-done | bytes 393248 | tf_op jit(solution)/shard_map/all_to_all | solution.py:170
  102.2 0.0 collective-permute-done.6.lower_ref
  102.2 0.0 collective-permute-done.7.last_ref
  102.2 0.9 shard_map.68
  (3 shorter events, 0.1 us)
Async XLA Ops:
  0.6 1.0 copy-start
  2.5 5.3 %copy-start.3 = (bf16[1,192,256]{2,1,0:T(8,128)(2,1)S(1)}, bf16[1,192,256]{2,1,0:T(8,128)(2,1)}, u32[]{:S(2)}) copy-start(bf16[1,192,256]{2,1,0:T(8,128)(2,1)} %param.5) | copy-start | bytes 294916
  2.5 31.3 %all-to-all-start = ((bf16[8,32,768]{2,1,0:T(8,128)(2,1)}), bf16[8,32,768]{2,1,0:T(8,128)(2,1)S(1)}, u32[]{:S(2)}, u32[]{:S(2)}) async-start(bf16[8,32,768]{2,1,0:T(8,128)(2,1)} %shard_map.59), calls=%async_computation | async-start | bytes 786432 | tf_op jit(solution)/shard_map/all_to_all | solution.py:170
  34.1 14.8 %copy-start.1 = (bf16[1,512,128]{2,1,0:T(8,128)(2,1)S(1)}, bf16[1,512,128]{2,1,0:T(8,128)(2,1)}, u32[]{:S(2)}) copy-start(bf16[1,512,128]{2,1,0:T(8,128)(2,1)} %param.6) | copy-start | bytes 393220
  34.1 14.8 %copy-start.2 = (bf16[1,512,128]{2,1,0:T(8,128)(2,1)S(1)}, bf16[1,512,128]{2,1,0:T(8,128)(2,1)}, u32[]{:S(2)}) copy-start(bf16[1,512,128]{2,1,0:T(8,128)(2,1)} %param.7) | copy-start | bytes 393220
  59.0 10.7 %all-to-all-start.3 = ((bf16[4,64,768]{2,1,0:T(8,128)(2,1)}), bf16[4,64,768]{2,1,0:T(8,128)(2,1)S(1)}, u32[]{:S(2)}, u32[]{:S(2)}) async-start(bf16[4,64,768]{2,1,0:T(8,128)(2,1)} %shard_map.62), calls=%async_computation.3 | async-start | bytes 786432 | tf_op jit(solution)/shard_map/all_to_all | solution.py:170
  63.4 15.7 %collective-permute-start.3 = (bf16[192,256]{1,0:T(8,128)(2,1)S(1)}, bf16[192,256]{1,0:T(8,128)(2,1)S(1)}, u32[]{:S(2)}, u32[]{:S(2)}) collective-permute-start(bf16[192,256]{1,0:T(8,128)(2,1)S(1)} %get-tuple-element.19), channel_id=1, source_target_pairs={{0,8},{1,9},{2,10},{3,11},{4,12},{5,13},{6,14},{7,15},{8,16},{9,17... | collective-permute-start | bytes 294920 | tf_op jit(solution)/shard_map/ppermute | solution.py:153
  69.7 13.2 %collective-permute-start = (bf16[64,768]{1,0:T(8,128)(2,1)S(1)}, bf16[64,768]{1,0:T(8,128)(2,1)S(1)}, u32[]{:S(2)}, u32[]{:S(2)}) collective-permute-start(bf16[64,768]{1,0:T(8,128)(2,1)S(1)} %shard_map.63), channel_id=1, source_target_pairs={{384,0},{416,32},{448,64},{480,96},{385,1},{417,33},{449,65},{481,... | collective-permute-start | bytes 294920 | tf_op jit(solution)/shard_map/ppermute | solution.py:190
  70.4 12.5 %collective-permute-start.1 = (bf16[64,768]{1,0:T(8,128)(2,1)S(1)}, bf16[64,768]{1,0:T(8,128)(2,1)S(1)}, u32[]{:S(2)}, u32[]{:S(2)}) collective-permute-start(bf16[64,768]{1,0:T(8,128)(2,1)S(1)} %shard_map.63), channel_id=1, source_target_pairs={{256,0},{288,32},{320,64},{352,96},{384,128},{416,160},{448,192},{... | collective-permute-start | bytes 294920 | tf_op jit(solution)/shard_map/ppermute | solution.py:190
  71.7 11.2 %collective-permute-start.2 = (bf16[64,768]{1,0:T(8,128)(2,1)S(1)}, bf16[64,768]{1,0:T(8,128)(2,1)S(1)}, u32[]{:S(2)}, u32[]{:S(2)}) collective-permute-start(bf16[64,768]{1,0:T(8,128)(2,1)S(1)} %shard_map.63), channel_id=1, source_target_pairs={{128,0},{160,32},{192,64},{224,96},{256,128},{288,160},{320,192},{... | collective-permute-start | bytes 294920 | tf_op jit(solution)/shard_map/ppermute | solution.py:190
  73.6 19.6 %collective-permute-start.5 = (bf16[192,256]{1,0:T(8,128)(2,1)S(1)}, bf16[192,256]{1,0:T(8,128)(2,1)S(1)}, u32[]{:S(2)}, u32[]{:S(2)}) collective-permute-start(bf16[192,256]{1,0:T(8,128)(2,1)S(1)} %get-tuple-element.25), channel_id=1, source_target_pairs={{129,153},{131,155},{133,157},{135,159},{137,129},{139,131},{141,1... | collective-permute-start | bytes 294920 | tf_op jit(solution)/shard_map/ppermute | solution.py:167
  79.1 14.2 %collective-permute-start.4 = (bf16[192,256]{1,0:T(8,128)(2,1)S(1)}, bf16[192,256]{1,0:T(8,128)(2,1)S(1)}, u32[]{:S(2)}, u32[]{:S(2)}) collective-permute-start(bf16[192,256]{1,0:T(8,128)(2,1)S(1)} %shard_map.66), channel_id=1, source_target_pairs={{0,8},{1,9},{2,10},{3,11},{4,12},{5,13},{6,14},{7,15},{8,16},{9,17... | collective-permute-start | bytes 294920 | tf_op jit(solution)/shard_map/ppermute | solution.py:167
  83.8 18.5 %all-to-all-start.4 = ((bf16[32,16,384]{2,1,0:T(8,128)(2,1)}), bf16[32,16,384]{2,1,0:T(8,128)(2,1)S(1)}, u32[]{:S(2)}, u32[]{:S(2)}) async-start(bf16[32,16,384]{2,1,0:T(8,128)(2,1)} %shard_map.65), calls=%async_computation.4 | async-start | bytes 786432 | tf_op jit(solution)/shard_map/all_to_all | solution.py:170
  91.9 10.3 %collective-permute-start.6 = (bf16[192,256]{1,0:T(8,128)(2,1)S(1)}, bf16[192,256]{1,0:T(8,128)(2,1)S(1)}, u32[]{:S(2)}, u32[]{:S(2)}) collective-permute-start(bf16[192,256]{1,0:T(8,128)(2,1)S(1)} %get-tuple-element.25), channel_id=1, source_target_pairs={{0,24},{1,25},{2,26},{3,27},{4,28},{5,29},{6,30},{7,31},{8,0},{9,1... | collective-permute-start | bytes 294920 | tf_op jit(solution)/shard_map/ppermute | solution.py:167
  92.6 9.6 %collective-permute-start.7 = (bf16[192,256]{1,0:T(8,128)(2,1)S(1)}, bf16[192,256]{1,0:T(8,128)(2,1)S(1)}, u32[]{:S(2)}, u32[]{:S(2)}) collective-permute-start(bf16[192,256]{1,0:T(8,128)(2,1)S(1)} %shard_map.66), channel_id=1, source_target_pairs={{384,392},{385,393},{386,394},{387,395},{388,396},{389,397},{390,3... | collective-permute-start | bytes 294920 | tf_op jit(solution)/shard_map/ppermute | solution.py:167

commit v8 on v6

--- a/solution.py
+++ b/solution.py
@@ -147,9 +147,12 @@
         ]
         return lax.ppermute(array, "dp", pairs)
 
-    def returned(array, ups):
+    def passed(array, step, ups):
         pairs = [
-            ((up * line + at) * Z_HI * NEAR + far * NEAR + near, (up * line + at) * Z_HI * NEAR + (far - 1) % Z_HI * NEAR + near)
+            (
+                ((up * line + at) * Z_HI + far) * NEAR + near,
+                ((up * line + at) * Z_HI + (far + step) % Z_HI) * NEAR + near,
+            )
             for up in ups
             for at in range(line)
             for far in range(Z_HI)
@@ -192,18 +195,19 @@
         scratch=[pltpu.VMEM((Z_HI, depth, both), high)],
     )
     beyond = shifted(beyond, 1)
-    after = shifted(call(add_terms, [((depth, both), low)], [after, beyond]), 1)
-    lower, upper = returned(before, range(Z_LO // 2)), returned(before, range(Z_LO // 2, Z_LO))
+    after = call(add_terms, [((depth, both), low)], [after, beyond])
+    low_after, high_after = passed(after, 1, range(3)), passed(after, 1, range(3, Z_LO))
+    low_before, high_before = passed(before, -1, range(2)), passed(before, -1, range(2, Z_LO))
     total = call(row_total, [((piece, width), low)], [part])
-    above = [lowered(total, step) for step in (2,3,1)]
+    above = [lowered(total, step) for step in (2, 3, 1)]
     above, beyond = lax.optimization_barrier((above, beyond))
     sums = call(suffix_sums, [((line * NEAR, 2 * piece // NEAR, width // 2), low)], [part, *above])
     sums = exchange(sums, ("section", "dp"), plane_groups)
-    mine = call(add_terms, [((depth, both), high)], [mine, after, upper], flops=int(4e9))
+    mine = call(add_terms, [((depth, both), high)], [mine, low_after, high_before], flops=int(4e9))
     sums, mine = lax.optimization_barrier((sums, mine))
     enc_grad = call(join_columns, [((1, rows, model), low)], [sums])
-    enc_grad, mine, lower = lax.optimization_barrier((enc_grad, mine, lower))
-    weight_grad = call(add_terms, [((depth, both), high)], [mine, lower])[None]
+    enc_grad, mine, high_after, low_before = lax.optimization_barrier((enc_grad, mine, high_after, low_before))
+    weight_grad = call(add_terms, [((depth, both), high)], [mine, high_after, low_before])[None]
     return enc_grad, weight_grad
 
 

time: 103 us -> 103 us (level)
    ppermute x2 -> x4, starting transfers between devices: 4.03 us -> 10.4 us  [passed(): return lax.ppermute(array, ('section', 'dp'), pairs)]
    ppermute x2 -> x1, starting transfers between devices: 11.5 us -> 5.74 us  [shifted(): return lax.ppermute(array, 'dp', pairs)]
  transfers between devices with their start and end apart: 10 -> 11, of which waited for: 2 -> 2; matrix products, arithmetic and copies ran while one was open for 0% -> 0% of each run, Pallas kernels for 2% -> 2%
where the time goes in v8:
time: 103 us; the launch traced here: 102 us
  blocking collectives  44.5 us (43%)
  starting transfers between devices  43.4 us (42%)
  waiting for transfers between devices  6.74 us (7%)
  Pallas kernels  5.51 us (5%)
    all_to_all x3, starting transfers between devices, exchange(): return lax.all_to_all(array, axis, 0, 0, axis_index_groups=groups)  23.3 us
    all_gather x1, blocking collectives, shards(): lax.all_gather(own, 'dp', axis=0, tiled=True, axis_index_groups=far_groups)  22.7 us
    all_to_all x2, blocking collectives, exchange(): return lax.all_to_all(array, axis, 0, 0, axis_index_groups=groups)  21.8 us
    ppermute x4, starting transfers between devices, passed(): return lax.ppermute(array, ('section', 'dp'), pairs)  10.4 us
    all_to_all x3, waiting for transfers between devices, exchange(): return lax.all_to_all(array, axis, 0, 0, axis_index_groups=groups)  6.72 us
    ppermute x1, starting transfers between devices, shifted(): return lax.ppermute(array, 'dp', pairs)  5.74 us
    pallas_call x11, Pallas kernels, call(): pl.pallas_call(kernel, out_shape=outs, in_specs=[smem] * scalars + [vmem]...  5.51 us
    ppermute x3, starting transfers between devices, lowered(): return lax.ppermute(array, 'section', pairs)  3.88 us
  transfers between devices with their start and end apart: 11, of which 2 were waited for; matrix products, arithmetic and copies ran while one was open for 0% of the time, Pallas kernels for 2%

profile of v8, /device:TPU:1, one launch (start us, length us, event | category | flops | bytes accessed | tf_op | source)
XLA Modules:
  0.0 102.0 jit_solution(16631628610682074118)
XLA Ops:
  0.6 0.0 copy-start
  0.6 1.0 copy-done
  1.6 0.9 shard_map.59
  2.5 0.0 copy-start.3
  2.5 10.4 %all-to-all-start = ((bf16[8,32,768]{2,1,0:T(8,128)(2,1)}), bf16[8,32,768]{2,1,0:T(8,128)(2,1)S(1)}, u32[]{:S(2)}, u32[]{:S(2)}) async-start(bf16[8,32,768]{2,1,0:T(8,128)(2,1)} %shard_map.59), calls=%async_computation | async-start | bytes 786432 | tf_op jit(solution)/shard_map/all_to_all | solution.py:164
  12.9 0.0 copy-done.3
  12.9 22.7 %all_gather.3.weights_ref = bf16[768,256]{1,0:T(8,128)(2,1)S(1)} all-gather(bf16[192,256]{1,0:T(8,128)(2,1)S(1)} %bitcast.8), channel_id=1, replica_groups={{0,8,16,24},{1,9,17,25},{2,10,18,26},{3,11,19,27},{4,12,20,28},{5,13,21..., dimensions={0}, use_global_device_ids=true | all-gather | bytes 491520 | tf_op jit(solution)/shard_map/all_gather | solution.py:169
  35.6 0.0 all-to-all-done.enc_ref
  35.6 0.3 shard_map.60
  35.8 0.0 copy-start.1
  35.9 0.0 copy-start.2
  35.9 13.1 %all_to_all.25.kv_ref = f32[8,32,256]{2,1,0:T(8,128)S(1)} all-to-all(f32[8,32,256]{2,1,0:T(8,128)S(1)} %shard_map.60), channel_id=1, replica_groups={{0,1,2,3,4,5,6,7},{8,9,10,11,12,13,14,15},{16,17,18,19,20,21,22,23},{24..., dimensions={0} | all-to-all | bytes 524288 | tf_op jit(solution)/shard_map/all_to_all | solution.py:164
  49.0 0.0 copy-done.1
  49.0 0.0 copy-done.2
  49.0 0.4 shard_map.61
  49.4 8.7 %all_to_all.26.dkv_ref = bf16[8,32,256]{2,1,0:T(8,128)(2,1)S(1)} all-to-all(bf16[8,32,256]{2,1,0:T(8,128)(2,1)S(1)} %broadcast_in_dim.4), channel_id=1, replica_groups={{0,1,2,3,4,5,6,7},{8,9,10,11,12,13,14,15},{16,17,18,19,20,21,22,23},{24..., dimensions={0} | all-to-all | bytes 262144 | tf_op jit(solution)/shard_map/all_to_all | solution.py:164
  58.1 1.0 %shard_map.62 = bf16[4,64,768]{2,1,0:T(8,128)(2,1)} custom-call(bf16[8,32,256]{2,1,0:T(8,128)(2,1)S(1)} %all_to_all.26.dkv_ref, bf16[768,256]{1,0:T(8,128)(2,1)S(1)} %all_gather.3.weights_ref), custom_call_target="tpu_custom_call" | custom-call | flops 100663296 | bytes 917504 | tf_op jit(solution)/shard_map/pallas_call | solution.py:120
  59.1 4.0 %all-to-all-start.3 = ((bf16[4,64,768]{2,1,0:T(8,128)(2,1)}), bf16[4,64,768]{2,1,0:T(8,128)(2,1)S(1)}, u32[]{:S(2)}, u32[]{:S(2)}) async-start(bf16[4,64,768]{2,1,0:T(8,128)(2,1)} %shard_map.62), calls=%async_computation.3 | async-start | bytes 786432 | tf_op jit(solution)/shard_map/all_to_all | solution.py:164
  63.1 0.4 shard_map.64
  63.5 5.7 %collective-permute-start.3 = (bf16[192,256]{1,0:T(8,128)(2,1)S(1)}, bf16[192,256]{1,0:T(8,128)(2,1)S(1)}, u32[]{:S(2)}, u32[]{:S(2)}) collective-permute-start(bf16[192,256]{1,0:T(8,128)(2,1)S(1)} %get-tuple-element.23), channel_id=1, source_target_pairs={{0,8},{1,9},{2,10},{3,11},{4,12},{5,13},{6,14},{7,15},{8,16},{9,17... | collective-permute-start | bytes 294920 | tf_op jit(solution)/shard_map/ppermute | solution.py:148
  69.3 0.5 all-to-all-done.3.in_ref
  69.8 0.1 shard_map.63
  69.9 1.3 %collective-permute-start = (bf16[64,768]{1,0:T(8,128)(2,1)S(1)}, bf16[64,768]{1,0:T(8,128)(2,1)S(1)}, u32[]{:S(2)}, u32[]{:S(2)}) collective-permute-start(bf16[64,768]{1,0:T(8,128)(2,1)S(1)} %shard_map.63), channel_id=1, source_target_pairs={{256,0},{288,32},{320,64},{352,96},{384,128},{416,160},{448,192},{... | collective-permute-start | bytes 294920 | tf_op jit(solution)/shard_map/ppermute | solution.py:184
  71.2 1.3 %collective-permute-start.1 = (bf16[64,768]{1,0:T(8,128)(2,1)S(1)}, bf16[64,768]{1,0:T(8,128)(2,1)S(1)}, u32[]{:S(2)}, u32[]{:S(2)}) collective-permute-start(bf16[64,768]{1,0:T(8,128)(2,1)S(1)} %shard_map.63), channel_id=1, source_target_pairs={{384,0},{416,32},{448,64},{480,96},{385,1},{417,33},{449,65},{481,... | collective-permute-start | bytes 294920 | tf_op jit(solution)/shard_map/ppermute | solution.py:184
  72.5 1.3 %collective-permute-start.2 = (bf16[64,768]{1,0:T(8,128)(2,1)S(1)}, bf16[64,768]{1,0:T(8,128)(2,1)S(1)}, u32[]{:S(2)}, u32[]{:S(2)}) collective-permute-start(bf16[64,768]{1,0:T(8,128)(2,1)S(1)} %shard_map.63), channel_id=1, source_target_pairs={{128,0},{160,32},{192,64},{224,96},{256,128},{288,160},{320,192},{... | collective-permute-start | bytes 294920 | tf_op jit(solution)/shard_map/ppermute | solution.py:184
  73.8 0.7 collective-permute-start.5
  74.4 0.0 collective-permute-done.3.refs_0_
  74.5 5.7 %collective-permute-start.4 = (bf16[192,256]{1,0:T(8,128)(2,1)S(1)}, bf16[192,256]{1,0:T(8,128)(2,1)S(1)}, u32[]{:S(2)}, u32[]{:S(2)}) collective-permute-start(bf16[192,256]{1,0:T(8,128)(2,1)S(1)} %shard_map.66), channel_id=1, source_target_pairs={{0,8},{1,9},{2,10},{3,11},{4,12},{5,13},{6,14},{7,15},{8,16},{9,17... | collective-permute-start | bytes 294920 | tf_op jit(solution)/shard_map/ppermute | solution.py:161
  80.2 0.0 collective-permute-done.one_ref
  80.2 0.0 collective-permute-done.1.two_ref
  80.2 0.0 collective-permute-done.2.three_ref
  80.2 0.8 shard_map.65
  81.1 8.9 %all-to-all-start.4 = ((bf16[32,16,384]{2,1,0:T(8,128)(2,1)}), bf16[32,16,384]{2,1,0:T(8,128)(2,1)S(1)}, u32[]{:S(2)}, u32[]{:S(2)}) async-start(bf16[32,16,384]{2,1,0:T(8,128)(2,1)} %shard_map.65), calls=%async_computation.4 | async-start | bytes 786432 | tf_op jit(solution)/shard_map/all_to_all | solution.py:164
  90.0 3.4 %collective-permute-start.7 = (bf16[192,256]{1,0:T(8,128)(2,1)S(1)}, bf16[192,256]{1,0:T(8,128)(2,1)S(1)}, u32[]{:S(2)}, u32[]{:S(2)}) collective-permute-start(bf16[192,256]{1,0:T(8,128)(2,1)S(1)} %get-tuple-element.29), channel_id=1, source_target_pairs={{0,24},{1,25},{2,26},{3,27},{4,28},{5,29},{6,30},{7,31},{8,0},{9,1... | collective-permute-start | bytes 294920 | tf_op jit(solution)/shard_map/ppermute | solution.py:161
  93.4 0.7 collective-permute-start.6
  94.1 0.0 collective-permute-done.5.refs_1_
  94.1 0.0 collective-permute-done.4.refs_0_
  94.1 6.2 %all-to-all-done.4.in_ref = bf16[32,16,384]{2,1,0:T(8,128)(2,1)S(1)} async-done(((bf16[32,16,384]{2,1,0:T(8,128)(2,1)}), bf16[32,16,384]{2,1,0:T(8,128)(2,1)S(1)}, u32[]{:S(2)}, u32[]{:S(2)}) %all-to-all-start.4) | async-done | bytes 393248 | tf_op jit(solution)/shard_map/all_to_all | solution.py:164
  100.4 0.9 shard_map.68
  101.2 0.0 collective-permute-done.7.refs_1_
  101.2 0.0 collective-permute-done.6.refs_0_
  101.2 0.7 shard_map.69
  (3 shorter events, 0.1 us)
Async XLA Ops:
  0.6 1.0 copy-start
  2.5 10.4 %copy-start.3 = (bf16[1,192,256]{2,1,0:T(8,128)(2,1)S(1)}, bf16[1,192,256]{2,1,0:T(8,128)(2,1)}, u32[]{:S(2)}) copy-start(bf16[1,192,256]{2,1,0:T(8,128)(2,1)} %param.5) | copy-start | bytes 294916
  2.5 33.1 %all-to-all-start = ((bf16[8,32,768]{2,1,0:T(8,128)(2,1)}), bf16[8,32,768]{2,1,0:T(8,128)(2,1)S(1)}, u32[]{:S(2)}, u32[]{:S(2)}) async-start(bf16[8,32,768]{2,1,0:T(8,128)(2,1)} %shard_map.59), calls=%async_computation | async-start | bytes 786432 | tf_op jit(solution)/shard_map/all_to_all | solution.py:164
  35.8 13.1 %copy-start.1 = (bf16[1,512,128]{2,1,0:T(8,128)(2,1)S(1)}, bf16[1,512,128]{2,1,0:T(8,128)(2,1)}, u32[]{:S(2)}) copy-start(bf16[1,512,128]{2,1,0:T(8,128)(2,1)} %param.6) | copy-start | bytes 393220
  35.9 13.1 %copy-start.2 = (bf16[1,512,128]{2,1,0:T(8,128)(2,1)S(1)}, bf16[1,512,128]{2,1,0:T(8,128)(2,1)}, u32[]{:S(2)}) copy-start(bf16[1,512,128]{2,1,0:T(8,128)(2,1)} %param.7) | copy-start | bytes 393220
  59.1 10.7 %all-to-all-start.3 = ((bf16[4,64,768]{2,1,0:T(8,128)(2,1)}), bf16[4,64,768]{2,1,0:T(8,128)(2,1)S(1)}, u32[]{:S(2)}, u32[]{:S(2)}) async-start(bf16[4,64,768]{2,1,0:T(8,128)(2,1)} %shard_map.62), calls=%async_computation.3 | async-start | bytes 786432 | tf_op jit(solution)/shard_map/all_to_all | solution.py:164
  63.5 10.9 %collective-permute-start.3 = (bf16[192,256]{1,0:T(8,128)(2,1)S(1)}, bf16[192,256]{1,0:T(8,128)(2,1)S(1)}, u32[]{:S(2)}, u32[]{:S(2)}) collective-permute-start(bf16[192,256]{1,0:T(8,128)(2,1)S(1)} %get-tuple-element.23), channel_id=1, source_target_pairs={{0,8},{1,9},{2,10},{3,11},{4,12},{5,13},{6,14},{7,15},{8,16},{9,17... | collective-permute-start | bytes 294920 | tf_op jit(solution)/shard_map/ppermute | solution.py:148
  69.9 10.4 %collective-permute-start = (bf16[64,768]{1,0:T(8,128)(2,1)S(1)}, bf16[64,768]{1,0:T(8,128)(2,1)S(1)}, u32[]{:S(2)}, u32[]{:S(2)}) collective-permute-start(bf16[64,768]{1,0:T(8,128)(2,1)S(1)} %shard_map.63), channel_id=1, source_target_pairs={{256,0},{288,32},{320,64},{352,96},{384,128},{416,160},{448,192},{... | collective-permute-start | bytes 294920 | tf_op jit(solution)/shard_map/ppermute | solution.py:184
  71.2 9.1 %collective-permute-start.1 = (bf16[64,768]{1,0:T(8,128)(2,1)S(1)}, bf16[64,768]{1,0:T(8,128)(2,1)S(1)}, u32[]{:S(2)}, u32[]{:S(2)}) collective-permute-start(bf16[64,768]{1,0:T(8,128)(2,1)S(1)} %shard_map.63), channel_id=1, source_target_pairs={{384,0},{416,32},{448,64},{480,96},{385,1},{417,33},{449,65},{481,... | collective-permute-start | bytes 294920 | tf_op jit(solution)/shard_map/ppermute | solution.py:184
  72.5 7.8 %collective-permute-start.2 = (bf16[64,768]{1,0:T(8,128)(2,1)S(1)}, bf16[64,768]{1,0:T(8,128)(2,1)S(1)}, u32[]{:S(2)}, u32[]{:S(2)}) collective-permute-start(bf16[64,768]{1,0:T(8,128)(2,1)S(1)} %shard_map.63), channel_id=1, source_target_pairs={{128,0},{160,32},{192,64},{224,96},{256,128},{288,160},{320,192},{... | collective-permute-start | bytes 294920 | tf_op jit(solution)/shard_map/ppermute | solution.py:184
  73.8 20.3 %collective-permute-start.5 = (bf16[192,256]{1,0:T(8,128)(2,1)S(1)}, bf16[192,256]{1,0:T(8,128)(2,1)S(1)}, u32[]{:S(2)}, u32[]{:S(2)}) collective-permute-start(bf16[192,256]{1,0:T(8,128)(2,1)S(1)} %get-tuple-element.29), channel_id=1, source_target_pairs={{256,280},{257,281},{258,282},{259,283},{260,284},{261,285},{262,2... | collective-permute-start | bytes 294920 | tf_op jit(solution)/shard_map/ppermute | solution.py:161
  74.5 19.6 %collective-permute-start.4 = (bf16[192,256]{1,0:T(8,128)(2,1)S(1)}, bf16[192,256]{1,0:T(8,128)(2,1)S(1)}, u32[]{:S(2)}, u32[]{:S(2)}) collective-permute-start(bf16[192,256]{1,0:T(8,128)(2,1)S(1)} %shard_map.66), channel_id=1, source_target_pairs={{0,8},{1,9},{2,10},{3,11},{4,12},{5,13},{6,14},{7,15},{8,16},{9,17... | collective-permute-start | bytes 294920 | tf_op jit(solution)/shard_map/ppermute | solution.py:161
  81.1 19.3 %all-to-all-start.4 = ((bf16[32,16,384]{2,1,0:T(8,128)(2,1)}), bf16[32,16,384]{2,1,0:T(8,128)(2,1)S(1)}, u32[]{:S(2)}, u32[]{:S(2)}) async-start(bf16[32,16,384]{2,1,0:T(8,128)(2,1)} %shard_map.65), calls=%async_computation.4 | async-start | bytes 786432 | tf_op jit(solution)/shard_map/all_to_all | solution.py:164
  90.0 11.2 %collective-permute-start.7 = (bf16[192,256]{1,0:T(8,128)(2,1)S(1)}, bf16[192,256]{1,0:T(8,128)(2,1)S(1)}, u32[]{:S(2)}, u32[]{:S(2)}) collective-permute-start(bf16[192,256]{1,0:T(8,128)(2,1)S(1)} %get-tuple-element.29), channel_id=1, source_target_pairs={{0,24},{1,25},{2,26},{3,27},{4,28},{5,29},{6,30},{7,31},{8,0},{9,1... | collective-permute-start | bytes 294920 | tf_op jit(solution)/shard_map/ppermute | solution.py:161
  93.4 7.8 %collective-permute-start.6 = (bf16[192,256]{1,0:T(8,128)(2,1)S(1)}, bf16[192,256]{1,0:T(8,128)(2,1)S(1)}, u32[]{:S(2)}, u32[]{:S(2)}) collective-permute-start(bf16[192,256]{1,0:T(8,128)(2,1)S(1)} %shard_map.66), channel_id=1, source_target_pairs={{384,392},{385,393},{386,394},{387,395},{388,396},{389,397},{390,3... | collective-permute-start | bytes 294920 | tf_op jit(solution)/shard_map/ppermute | solution.py:161

commit v9 on v6

--- a/solution.py
+++ b/solution.py
@@ -112,6 +112,11 @@
     refs[-1][...] = total.astype(refs[-1].dtype)
 
 
+def finish(sums_ref, own_ref, last_ref, enc_grad_ref, weight_grad_ref):
+    join_columns(sums_ref, enc_grad_ref)
+    weight_grad_ref[0] = own_ref[...] + last_ref[...].astype(jnp.float32)
+
+
 def call(kernel, outs, args, flops=0, scalars=0, scratch=()):
     outs = [jax.ShapeDtypeStruct(shape, dtype) for shape, dtype in outs]
     vmem = pl.BlockSpec(memory_space=pltpu.VMEM)
@@ -201,9 +206,9 @@
     sums = exchange(sums, ("section", "dp"), plane_groups)
     mine = call(add_terms, [((depth, both), high)], [mine, after, upper], flops=int(4e9))
     sums, mine = lax.optimization_barrier((sums, mine))
-    enc_grad = call(join_columns, [((1, rows, model), low)], [sums])
-    enc_grad, mine, lower = lax.optimization_barrier((enc_grad, mine, lower))
-    weight_grad = call(add_terms, [((depth, both), high)], [mine, lower])[None]
+    enc_grad, weight_grad = call(
+        finish, [((1, rows, model), low), ((1, depth, both), high)], [sums, mine, lower]
+    )
     return enc_grad, weight_grad
 
 

time: 103 us -> 104 us (level)
  the two profiles are of different devices: /device:TPU:1 before, /device:TPU:39 now
where the time goes in v9:
time: 104 us; the launch traced here: 103 us
  blocking collectives  49.5 us (48%)
  starting transfers between devices  38.2 us (37%)
  waiting for transfers between devices  8.62 us (8%)
  Pallas kernels  4.82 us (5%)
    all_gather x1, blocking collectives, shards(): lax.all_gather(own, 'dp', axis=0, tiled=True, axis_index_groups=far_groups)  26 us
    all_to_all x2, blocking collectives, exchange(): return lax.all_to_all(array, axis, 0, 0, axis_index_groups=groups)  23.5 us
    all_to_all x3, starting transfers between devices, exchange(): return lax.all_to_all(array, axis, 0, 0, axis_index_groups=groups)  18.1 us
    ppermute x2, starting transfers between devices, shifted(): return lax.ppermute(array, 'dp', pairs)  10 us
    ppermute x2, starting transfers between devices, returned(): return lax.ppermute(array, ('section', 'dp'), pairs)  5.36 us
    pallas_call x10, Pallas kernels, call(): pl.pallas_call(kernel, out_shape=outs, in_specs=[smem] * scalars + [vmem]...  4.82 us
    ppermute x3, starting transfers between devices, lowered(): return lax.ppermute(array, 'section', pairs)  4.71 us
    ppermute x2, waiting for transfers between devices, returned(): return lax.ppermute(array, ('section', 'dp'), pairs)  3.71 us
  transfers between devices with their start and end apart: 10, of which 4 were waited for; matrix products, arithmetic and copies ran while one was open for 0% of the time, Pallas kernels for 1%

profile of v9, /device:TPU:39, one launch (start us, length us, event | category | flops | bytes accessed | tf_op | source)
XLA Modules:
  0.0 102.9 jit_solution(1659630151142235340)
XLA Ops:
  0.6 0.0 copy-start
  0.6 1.0 copy-done
  1.6 0.9 shard_map.59
  2.5 0.0 copy-start.3
  2.5 5.3 %all-to-all-start = ((bf16[8,32,768]{2,1,0:T(8,128)(2,1)}), bf16[8,32,768]{2,1,0:T(8,128)(2,1)S(1)}, u32[]{:S(2)}, u32[]{:S(2)}) async-start(bf16[8,32,768]{2,1,0:T(8,128)(2,1)} %shard_map.59), calls=%async_computation | async-start | bytes 786432 | tf_op jit(solution)/shard_map/all_to_all | solution.py:166
  7.8 0.0 copy-done.3
  7.8 26.0 %all_gather.3.weights_ref = bf16[768,256]{1,0:T(8,128)(2,1)S(1)} all-gather(bf16[192,256]{1,0:T(8,128)(2,1)S(1)} %bitcast.6), channel_id=1, replica_groups={{0,8,16,24},{1,9,17,25},{2,10,18,26},{3,11,19,27},{4,12,20,28},{5,13,21..., dimensions={0}, use_global_device_ids=true | all-gather | bytes 491520 | tf_op jit(solution)/shard_map/all_gather | solution.py:171
  33.8 0.0 all-to-all-done.enc_ref
  33.8 0.3 shard_map.60
  34.1 0.0 copy-start.1
  34.1 0.0 copy-start.2
  34.1 14.8 %all_to_all.25.kv_ref = f32[8,32,256]{2,1,0:T(8,128)S(1)} all-to-all(f32[8,32,256]{2,1,0:T(8,128)S(1)} %shard_map.60), channel_id=1, replica_groups={{0,1,2,3,4,5,6,7},{8,9,10,11,12,13,14,15},{16,17,18,19,20,21,22,23},{24..., dimensions={0} | all-to-all | bytes 524288 | tf_op jit(solution)/shard_map/all_to_all | solution.py:166
  48.9 0.0 copy-done.1
  48.9 0.0 copy-done.2
  48.9 0.4 shard_map.61
  49.3 8.7 %all_to_all.26.dkv_ref = bf16[8,32,256]{2,1,0:T(8,128)(2,1)S(1)} all-to-all(bf16[8,32,256]{2,1,0:T(8,128)(2,1)S(1)} %broadcast_in_dim.2), channel_id=1, replica_groups={{0,1,2,3,4,5,6,7},{8,9,10,11,12,13,14,15},{16,17,18,19,20,21,22,23},{24..., dimensions={0} | all-to-all | bytes 262144 | tf_op jit(solution)/shard_map/all_to_all | solution.py:166
  58.0 1.0 %shard_map.62 = bf16[4,64,768]{2,1,0:T(8,128)(2,1)} custom-call(bf16[8,32,256]{2,1,0:T(8,128)(2,1)S(1)} %all_to_all.26.dkv_ref, bf16[768,256]{1,0:T(8,128)(2,1)S(1)} %all_gather.3.weights_ref), custom_call_target="tpu_custom_call" | custom-call | flops 100663296 | bytes 917504 | tf_op jit(solution)/shard_map/pallas_call | solution.py:125
  59.0 4.2 %all-to-all-start.3 = ((bf16[4,64,768]{2,1,0:T(8,128)(2,1)}), bf16[4,64,768]{2,1,0:T(8,128)(2,1)S(1)}, u32[]{:S(2)}, u32[]{:S(2)}) async-start(bf16[4,64,768]{2,1,0:T(8,128)(2,1)} %shard_map.62), calls=%async_computation.3 | async-start | bytes 786432 | tf_op jit(solution)/shard_map/all_to_all | solution.py:166
  63.2 0.4 shard_map.64
  63.6 4.6 %collective-permute-start.3 = (bf16[192,256]{1,0:T(8,128)(2,1)S(1)}, bf16[192,256]{1,0:T(8,128)(2,1)S(1)}, u32[]{:S(2)}, u32[]{:S(2)}) collective-permute-start(bf16[192,256]{1,0:T(8,128)(2,1)S(1)} %get-tuple-element.19), channel_id=1, source_target_pairs={{0,8},{1,9},{2,10},{3,11},{4,12},{5,13},{6,14},{7,15},{8,16},{9,17... | collective-permute-start | bytes 294920 | tf_op jit(solution)/shard_map/ppermute | solution.py:153
  68.3 0.0 all-to-all-done.3.in_ref
  68.3 0.1 shard_map.63
  68.3 1.3 %collective-permute-start = (bf16[64,768]{1,0:T(8,128)(2,1)S(1)}, bf16[64,768]{1,0:T(8,128)(2,1)S(1)}, u32[]{:S(2)}, u32[]{:S(2)}) collective-permute-start(bf16[64,768]{1,0:T(8,128)(2,1)S(1)} %shard_map.63), channel_id=1, source_target_pairs={{256,0},{288,32},{320,64},{352,96},{384,128},{416,160},{448,192},{... | collective-permute-start | bytes 294920 | tf_op jit(solution)/shard_map/ppermute | solution.py:186
  69.6 0.7 collective-permute-start.1
  70.3 2.7 %collective-permute-start.2 = (bf16[64,768]{1,0:T(8,128)(2,1)S(1)}, bf16[64,768]{1,0:T(8,128)(2,1)S(1)}, u32[]{:S(2)}, u32[]{:S(2)}) collective-permute-start(bf16[64,768]{1,0:T(8,128)(2,1)S(1)} %shard_map.63), channel_id=1, source_target_pairs={{128,0},{160,32},{192,64},{224,96},{256,128},{288,160},{320,192},{... | collective-permute-start | bytes 294920 | tf_op jit(solution)/shard_map/ppermute | solution.py:186
  73.1 0.7 collective-permute-start.5
  73.7 0.8 collective-permute-done.3.refs_0_
  74.5 5.4 %collective-permute-start.4 = (bf16[192,256]{1,0:T(8,128)(2,1)S(1)}, bf16[192,256]{1,0:T(8,128)(2,1)S(1)}, u32[]{:S(2)}, u32[]{:S(2)}) collective-permute-start(bf16[192,256]{1,0:T(8,128)(2,1)S(1)} %shard_map.66), channel_id=1, source_target_pairs={{0,8},{1,9},{2,10},{3,11},{4,12},{5,13},{6,14},{7,15},{8,16},{9,17... | collective-permute-start | bytes 294920 | tf_op jit(solution)/shard_map/ppermute | solution.py:153
  79.9 0.0 collective-permute-done.one_ref
  79.9 0.0 collective-permute-done.1.two_ref
  79.9 0.5 collective-permute-done.2.three_ref
  80.4 0.8 shard_map.65
  81.3 8.6 %all-to-all-start.4 = ((bf16[32,16,384]{2,1,0:T(8,128)(2,1)}), bf16[32,16,384]{2,1,0:T(8,128)(2,1)S(1)}, u32[]{:S(2)}, u32[]{:S(2)}) async-start(bf16[32,16,384]{2,1,0:T(8,128)(2,1)} %shard_map.65), calls=%async_computation.4 | async-start | bytes 786432 | tf_op jit(solution)/shard_map/all_to_all | solution.py:166
  89.9 4.7 %collective-permute-start.6 = (bf16[192,256]{1,0:T(8,128)(2,1)S(1)}, bf16[192,256]{1,0:T(8,128)(2,1)S(1)}, u32[]{:S(2)}, u32[]{:S(2)}) collective-permute-start(bf16[192,256]{1,0:T(8,128)(2,1)S(1)} %get-tuple-element.25), channel_id=1, source_target_pairs={{0,24},{1,25},{2,26},{3,27},{4,28},{5,29},{6,30},{7,31},{8,0},{9,1... | collective-permute-start | bytes 294920 | tf_op jit(solution)/shard_map/ppermute | solution.py:163
  94.6 0.0 collective-permute-done.5.refs_1_
  94.6 0.0 collective-permute-done.4.refs_0_
  94.7 3.6 %all-to-all-done.4.sums_ref = bf16[32,16,384]{2,1,0:T(8,128)(2,1)S(1)} async-done(((bf16[32,16,384]{2,1,0:T(8,128)(2,1)}), bf16[32,16,384]{2,1,0:T(8,128)(2,1)S(1)}, u32[]{:S(2)}, u32[]{:S(2)}) %all-to-all-start.4) | async-done | bytes 393248 | tf_op jit(solution)/shard_map/all_to_all | solution.py:166
  98.3 3.7 %collective-permute-done.6.last_ref = bf16[192,256]{1,0:T(8,128)(2,1)S(1)} collective-permute-done((bf16[192,256]{1,0:T(8,128)(2,1)S(1)}, bf16[192,256]{1,0:T(8,128)(2,1)S(1)}, u32[]{:S(2)}, u32[]{:S(2)}) %collective-permute-start.6) | collective-permute-done | bytes 98336 | tf_op jit(solution)/shard_map/ppermute | solution.py:163
  102.0 0.9 shard_map.68
  (3 shorter events, 0.1 us)
Async XLA Ops:
  0.6 1.0 copy-start
  2.5 5.3 %copy-start.3 = (bf16[1,192,256]{2,1,0:T(8,128)(2,1)S(1)}, bf16[1,192,256]{2,1,0:T(8,128)(2,1)}, u32[]{:S(2)}) copy-start(bf16[1,192,256]{2,1,0:T(8,128)(2,1)} %param.5) | copy-start | bytes 294916
  2.5 31.3 %all-to-all-start = ((bf16[8,32,768]{2,1,0:T(8,128)(2,1)}), bf16[8,32,768]{2,1,0:T(8,128)(2,1)S(1)}, u32[]{:S(2)}, u32[]{:S(2)}) async-start(bf16[8,32,768]{2,1,0:T(8,128)(2,1)} %shard_map.59), calls=%async_computation | async-start | bytes 786432 | tf_op jit(solution)/shard_map/all_to_all | solution.py:166
  34.1 14.8 %copy-start.1 = (bf16[1,512,128]{2,1,0:T(8,128)(2,1)S(1)}, bf16[1,512,128]{2,1,0:T(8,128)(2,1)}, u32[]{:S(2)}) copy-start(bf16[1,512,128]{2,1,0:T(8,128)(2,1)} %param.6) | copy-start | bytes 393220
  34.1 14.8 %copy-start.2 = (bf16[1,512,128]{2,1,0:T(8,128)(2,1)S(1)}, bf16[1,512,128]{2,1,0:T(8,128)(2,1)}, u32[]{:S(2)}) copy-start(bf16[1,512,128]{2,1,0:T(8,128)(2,1)} %param.7) | copy-start | bytes 393220
  59.0 9.3 %all-to-all-start.3 = ((bf16[4,64,768]{2,1,0:T(8,128)(2,1)}), bf16[4,64,768]{2,1,0:T(8,128)(2,1)S(1)}, u32[]{:S(2)}, u32[]{:S(2)}) async-start(bf16[4,64,768]{2,1,0:T(8,128)(2,1)} %shard_map.62), calls=%async_computation.3 | async-start | bytes 786432 | tf_op jit(solution)/shard_map/all_to_all | solution.py:166
  63.6 10.9 %collective-permute-start.3 = (bf16[192,256]{1,0:T(8,128)(2,1)S(1)}, bf16[192,256]{1,0:T(8,128)(2,1)S(1)}, u32[]{:S(2)}, u32[]{:S(2)}) collective-permute-start(bf16[192,256]{1,0:T(8,128)(2,1)S(1)} %get-tuple-element.19), channel_id=1, source_target_pairs={{0,8},{1,9},{2,10},{3,11},{4,12},{5,13},{6,14},{7,15},{8,16},{9,17... | collective-permute-start | bytes 294920 | tf_op jit(solution)/shard_map/ppermute | solution.py:153
  68.3 11.6 %collective-permute-start = (bf16[64,768]{1,0:T(8,128)(2,1)S(1)}, bf16[64,768]{1,0:T(8,128)(2,1)S(1)}, u32[]{:S(2)}, u32[]{:S(2)}) collective-permute-start(bf16[64,768]{1,0:T(8,128)(2,1)S(1)} %shard_map.63), channel_id=1, source_target_pairs={{256,0},{288,32},{320,64},{352,96},{384,128},{416,160},{448,192},{... | collective-permute-start | bytes 294920 | tf_op jit(solution)/shard_map/ppermute | solution.py:186
  69.6 10.3 %collective-permute-start.1 = (bf16[64,768]{1,0:T(8,128)(2,1)S(1)}, bf16[64,768]{1,0:T(8,128)(2,1)S(1)}, u32[]{:S(2)}, u32[]{:S(2)}) collective-permute-start(bf16[64,768]{1,0:T(8,128)(2,1)S(1)} %shard_map.63), channel_id=1, source_target_pairs={{384,0},{416,32},{448,64},{480,96},{385,1},{417,33},{449,65},{481,... | collective-permute-start | bytes 294920 | tf_op jit(solution)/shard_map/ppermute | solution.py:186
  70.3 10.1 %collective-permute-start.2 = (bf16[64,768]{1,0:T(8,128)(2,1)S(1)}, bf16[64,768]{1,0:T(8,128)(2,1)S(1)}, u32[]{:S(2)}, u32[]{:S(2)}) collective-permute-start(bf16[64,768]{1,0:T(8,128)(2,1)S(1)} %shard_map.63), channel_id=1, source_target_pairs={{128,0},{160,32},{192,64},{224,96},{256,128},{288,160},{320,192},{... | collective-permute-start | bytes 294920 | tf_op jit(solution)/shard_map/ppermute | solution.py:186
  73.1 21.5 %collective-permute-start.5 = (bf16[192,256]{1,0:T(8,128)(2,1)S(1)}, bf16[192,256]{1,0:T(8,128)(2,1)S(1)}, u32[]{:S(2)}, u32[]{:S(2)}) collective-permute-start(bf16[192,256]{1,0:T(8,128)(2,1)S(1)} %get-tuple-element.25), channel_id=1, source_target_pairs={{256,280},{257,281},{258,282},{259,283},{260,284},{261,285},{262,2... | collective-permute-start | bytes 294920 | tf_op jit(solution)/shard_map/ppermute | solution.py:163
  74.5 20.1 %collective-permute-start.4 = (bf16[192,256]{1,0:T(8,128)(2,1)S(1)}, bf16[192,256]{1,0:T(8,128)(2,1)S(1)}, u32[]{:S(2)}, u32[]{:S(2)}) collective-permute-start(bf16[192,256]{1,0:T(8,128)(2,1)S(1)} %shard_map.66), channel_id=1, source_target_pairs={{0,8},{1,9},{2,10},{3,11},{4,12},{5,13},{6,14},{7,15},{8,16},{9,17... | collective-permute-start | bytes 294920 | tf_op jit(solution)/shard_map/ppermute | solution.py:153
  81.3 17.0 %all-to-all-start.4 = ((bf16[32,16,384]{2,1,0:T(8,128)(2,1)}), bf16[32,16,384]{2,1,0:T(8,128)(2,1)S(1)}, u32[]{:S(2)}, u32[]{:S(2)}) async-start(bf16[32,16,384]{2,1,0:T(8,128)(2,1)} %shard_map.65), calls=%async_computation.4 | async-start | bytes 786432 | tf_op jit(solution)/shard_map/all_to_all | solution.py:166
  89.9 12.1 %collective-permute-start.6 = (bf16[192,256]{1,0:T(8,128)(2,1)S(1)}, bf16[192,256]{1,0:T(8,128)(2,1)S(1)}, u32[]{:S(2)}, u32[]{:S(2)}) collective-permute-start(bf16[192,256]{1,0:T(8,128)(2,1)S(1)} %get-tuple-element.25), channel_id=1, source_target_pairs={{0,24},{1,25},{2,26},{3,27},{4,28},{5,29},{6,30},{7,31},{8,0},{9,1... | collective-permute-start | bytes 294920 | tf_op jit(solution)/shard_map/ppermute | solution.py:163
